TPU v7x, 256 devices: a whole 4x4x8 slice. The times are simulated.
256 devices in a mesh: dp: 32 (over z, y), tensor: 8 (over x, core).
Axes of the slice: x: 4, y: 4, z: 8, core: 2. Of those that a mesh axis runs over, the one named last changes fastest.
Arguments:
- hidden: bfloat16 [24576, 14336], P('dp', 'tensor'), may hold values from -6 to 6
- layer_output_gradient: bfloat16 [24576, 4096], P('dp', 'tensor'), may hold values from -6 to 6
- frozen_down_weight: bfloat16 [14336, 4096], P('tensor', 'dp'), may hold values from -0.046875 to 0.046875
- adapter_down_weight: bfloat16 [14336, 128], P('tensor'), may hold values from -0.046875 to 0.046875
- adapter_up_weight: bfloat16 [128, 4096], replicated, may hold values from -0.09375 to 0.09375
- chosen_expert_index: int32 [24576, 2], P('dp'), may hold values from 0 to 7, all different within a row
- gates: float32 [24576, 2], P('dp'), may hold values from 0.1 to 0.9
Outputs:
- hidden_input_gradient: bfloat16 [24576, 14336], P('dp', 'tensor')
- down_factor_gradient: float32 [14336, 128], P('tensor')
- up_factor_gradient: float32 [128, 4096], P(None, ('dp', 'tensor'))
- gate_gradient: float32 [24576, 2], P('dp')
All inputs are finite; a program needn't handle non-finite values.
Results may differ from a plain program's by a relative error of at most 0.0031.
Values may be sent and summed in bfloat16 or wider, within the bound.
No kernel may reach another device: no remote copies, remote signals or barrier semaphores. Data moves between devices by JAX's collectives and lax.ppermute only.
A program may use at most 128 MiB of HBM per device.

v0:
```python
import jax
import jax.numpy as jnp
from jax import lax
from jax.sharding import PartitionSpec as P

ADAPTER_EXPERTS = 8
LOW_RANK = 16


SCALE = 2.0


def per_device(
    hidden,
    layer_output_gradient,
    frozen_down_weight,
    adapter_down_weight,
    adapter_up_weight,
    chosen_expert_index,
    gates,
):
    full_output_gradient = lax.all_gather(layer_output_gradient, "tensor", axis=1, tiled=True)
    rank_projection = lax.psum(
        jnp.dot(hidden, adapter_down_weight, preferred_element_type=jnp.float32), "tensor"
    )
    rank_output_gradient = lax.dot_general(
        full_output_gradient,
        adapter_up_weight,
        (((1,), (1,)), ((), ())),
        preferred_element_type=jnp.float32,
    )
    onehot = (
        chosen_expert_index[:, :, None]
        == jnp.arange(ADAPTER_EXPERTS, dtype=jnp.int32)[None, None, :]
    ).astype(jnp.float32)
    weight = jnp.repeat(jnp.sum(onehot * gates[:, :, None], axis=1), LOW_RANK, axis=1)
    gated_rank_gradient = (SCALE * weight * rank_output_gradient).astype(jnp.bfloat16)
    gated_rank_projection = (SCALE * weight * rank_projection).astype(jnp.bfloat16)
    frozen_gradient_term = lax.dot_general(
        full_output_gradient,
        lax.all_gather(frozen_down_weight, "dp", axis=1, tiled=True),
        (((1,), (1,)), ((), ())),
        preferred_element_type=jnp.float32,
    )
    adapter_gradient_term = lax.dot_general(
        gated_rank_gradient,
        adapter_down_weight,
        (((1,), (1,)), ((), ())),
        preferred_element_type=jnp.float32,
    )
    hidden_input_gradient = (frozen_gradient_term + adapter_gradient_term).astype(jnp.bfloat16)
    data_count = lax.axis_size("dp")
    tensor_count = lax.axis_size("tensor")
    tokens_here = full_output_gradient.shape[0]
    token_scale = float(tokens_here * data_count) ** (-0.5)
    piece_width = full_output_gradient.shape[1] // (data_count * tensor_count)
    strided = full_output_gradient.reshape(tokens_here, data_count, tensor_count, piece_width)
    picked = lax.dynamic_index_in_dim(strided, lax.axis_index("tensor"), 2, keepdims=False)
    picked = picked.reshape(tokens_here, data_count * piece_width)
    per_expert_down_gradient = lax.dot_general(
        hidden, gated_rank_gradient, (((0,), (0,)), ((), ())), preferred_element_type=jnp.float32
    )
    per_expert_up_gradient = lax.dot_general(
        gated_rank_projection, picked, (((0,), (0,)), ((), ())), preferred_element_type=jnp.float32
    )
    down_factor_gradient = lax.psum(per_expert_down_gradient, "dp") * token_scale
    up_factor_gradient = (
        lax.psum_scatter(per_expert_up_gradient, "dp", scatter_dimension=1, tiled=True)
        * token_scale
    )
    product = jnp.sum(
        (rank_projection * rank_output_gradient).reshape(tokens_here, ADAPTER_EXPERTS, LOW_RANK),
        axis=2,
    )
    gate_gradient = SCALE * jnp.sum(onehot * product[:, None, :], axis=2)
    return (hidden_input_gradient, down_factor_gradient, up_factor_gradient, gate_gradient)


def solution(mesh):
    return jax.shard_map(
        per_device,
        mesh=mesh,
        in_specs=(
            P("dp", "tensor"),
            P("dp", "tensor"),
            P("tensor", "dp"),
            P("tensor", None),
            P(),
            P("dp", None),
            P("dp", None),
        ),
        out_specs=(P("dp", "tensor"), P("tensor", None), P(None, ("dp", "tensor")), P("dp", None)),
        check_vma=False,
    )
```

profile of v0, /device:TPU:4, one launch (start us, length us, event | category | flops | bytes accessed | tf_op | source)
XLA Modules:
  0.0 660.7 jit_solution(1613949864431341855)
XLA Ops:
  7.2 0.0 copy-start
  7.2 0.0 all-reduce.5.cloned.1.call-start
  7.2 1.7 copy-done
  8.9 2.8 fusion.4
  11.8 0.0 all-reduce.5.cloned.1.call-update
  11.8 0.0 copy-start.4
  11.8 0.0 all-gather.3.cloned.1.call-start
  11.9 2.3 copy.26
  14.2 0.0 all-gather.3.cloned.1.call-update
  14.2 0.0 reduce-scatter.2.cloned.1.call-start
  14.2 62.2 %all-reduce.5.cloned.1.call-done = f32[768,128]{0,1:T(8,128)} async-done(((f32[768,128]{0,1:T(8,128)}), f32[768,128]{0,1:T(8,128)}) %all-reduce.5.cloned.1.call-update) | async-done | bytes 393232 | tf_op jit(solution)/shard_map/psum | solution.py:23
  76.5 47.9 %all-gather.3.cloned.1.call-done = bf16[768,4096]{0,1:T(8,128)(2,1)} async-done(((bf16[768,512]{0,1:T(8,128)(2,1)}), bf16[768,4096]{0,1:T(8,128)(2,1)}) %all-gather.3.cloned.1.call-update) | async-done | bytes 6291472 | tf_op jit(solution)/shard_map/all_gather | solution.py:22
  124.4 4.1 fusion.2
  128.5 0.1 bitcast_reduce_fusion
  128.7 1.2 constant_dynamic-slice_fusion
  129.9 0.1 fusion.1
  130.0 1.1 fusion.5
  131.0 0.0 reduce-scatter.2.cloned.1.call-update
  131.1 0.0 all-reduce.3.cloned.1.call-start
  131.1 1.5 convolution_bitcast_fusion
  132.6 0.0 all-reduce.3.cloned.1.call-update
  132.6 0.0 all-gather.5.cloned.1.call-start
  132.6 0.5 all-gather.5.cloned.1.call-update
  133.2 0.6 broadcast_multiply_fusion.3
  133.8 3.3 fusion.3
  137.1 208.1 %reduce-scatter.2.cloned.1.call-done = f32[128,16]{0,1:T(8,128)} async-done(((f32[128,512]{0,1:T(8,128)}), f32[128,16]{0,1:T(8,128)}) %reduce-scatter.2.cloned.1.call-update) | async-done | bytes 8208 | tf_op jit(solution)/shard_map/reduce_scatter | solution.py:68
  345.2 1.3 broadcast_multiply_fusion.2
  346.5 150.3 %all-reduce.3.cloned.1.call-done = f32[1792,128]{0,1:T(8,128)} async-done(((f32[1792,128]{0,1:T(8,128)}), f32[1792,128]{0,1:T(8,128)}) %all-reduce.3.cloned.1.call-update) | async-done | bytes 917520 | tf_op jit(solution)/shard_map/psum | solution.py:66
  496.8 2.2 broadcast_multiply_fusion
  499.0 2.4 copy.28
  501.4 133.3 %all-gather.5.cloned.1.call-done = bf16[1792,4096]{1,0:T(8,128)(2,1)} async-done(((bf16[1792,128]{1,0:T(8,128)(2,1)}), bf16[1792,4096]{1,0:T(8,128)(2,1)}) %all-gather.5.cloned.1.call-update) | async-done | bytes 14680080 | tf_op jit(solution)/shard_map/all_gather | solution.py:41
  634.7 19.4 %add_convert_fusion = bf16[768,1792]{1,0:T(8,128)(2,1)} fusion(f32[768,1792]{1,0:T(8,128)} %fusion.3, bf16[768,4096]{0,1:T(8,128)(2,1)} %all-gather.3.cloned.1.call-done, bf16[1792,4096]{1,0:T(8,128)(2,1)} %all-gather.5.cloned.1.call-done), kind=kOutput, calls=%fused_computation | convolution fusion | flops 11277041664 | bytes 29229056 | tf_op jit(solution)/shard_map/dot_general | solution.py:39
  (9 shorter events, 0.1 us)
Async XLA Ops:
  7.2 1.8 copy-start
  7.2 69.3 %all-reduce.5.cloned.1.call-start = ((), (), s32[]{:S(2)}) async-start(), calls=%async_computation.4 | async-start | bytes 786432 | tf_op jit(solution)/shard_map/psum | solution.py:23
  11.8 116.8 %copy-start.3 = (s32[768,2]{0,1:T(2,128)S(1)}, s32[768,2]{0,1:T(2,128)}, u32[]{:S(2)}) copy-start(s32[768,2]{0,1:T(2,128)} %param.12) | copy-start | bytes 18436
  11.8 116.8 %copy-start.4 = (f32[768,2]{0,1:T(2,128)S(1)}, f32[768,2]{0,1:T(2,128)}, u32[]{:S(2)}) copy-start(f32[768,2]{0,1:T(2,128)} %param.13) | copy-start | bytes 18436
  11.8 112.6 %all-gather.3.cloned.1.call-start = ((), (), s32[]{:S(2)}) async-start(), calls=%async_computation.1 | async-start | bytes 7077888 | tf_op jit(solution)/shard_map/all_gather | solution.py:22
  14.2 331.1 %reduce-scatter.2.cloned.1.call-start = ((), (), s32[]{:S(2)}) async-start(), calls=%async_computation.5 | async-start | bytes 270336 | tf_op jit(solution)/shard_map/reduce_scatter | solution.py:68
  124.4 5.5 copy-start.2
  128.5 5.3 copy-start.1
  131.1 365.8 %all-reduce.3.cloned.1.call-start = ((), (), s32[]{:S(2)}) async-start(), calls=%async_computation.3 | async-start | bytes 1835008 | tf_op jit(solution)/shard_map/psum | solution.py:66
  132.6 502.1 %all-gather.5.cloned.1.call-start = ((), (), s32[]{:S(2)}) async-start(), calls=%async_computation.2 | async-start | bytes 15138816 | tf_op jit(solution)/shard_map/all_gather | solution.py:41
Sparse Core Ops, SparseCore 0:
  11.9 64.5 all-reduce.4
  79.0 45.3 all-gather.2
  131.2 214.0 reduce-scatter.1
  349.1 147.6 all-reduce.2
  499.1 135.5 all-gather.4
where the time goes:
time: 661 us
  waiting for transfers between devices  602 us (91%)
  matrix products  32.3 us (5%)
  between operations  13.9 us (2%)
  local copies, waits for them, and re-layouts  7.64 us (1%)
    reduce_scatter x1, waiting for transfers between devices, per_device(): lax.psum_scatter(per_expert_up_gradient, 'dp', scatter_dimension=1, tiled...  208 us
    psum x1, waiting for transfers between devices, per_device(): lax.psum(per_expert_down_gradient, 'dp') * token_scale  150 us
    all_gather x1, waiting for transfers between devices, per_device(): lax.all_gather(frozen_down_weight, 'dp', axis=1, tiled=True)  133 us
    psum x1, waiting for transfers between devices, per_device(): lax.psum(jnp.dot(hidden, adapter_down_weight, preferred_element_type=jnp....  62.2 us
    all_gather x1, waiting for transfers between devices, per_device(): lax.all_gather(layer_output_gradient, 'tensor', axis=1, tiled=True)  47.9 us
    dot_general x1, matrix products, per_device(): lax.dot_general(full_output_gradient, lax.all_gather(frozen_down_weight,...  19.4 us
  transfers between devices with their start and end apart: 5, of which 5 were waited for; matrix products, arithmetic and copies ran while one was open for 2% of the time, Pallas kernels for 0%

commit v1 on v0

v1 whole, which is shorter than its diff:
```python
import functools

import jax
import jax.numpy as jnp
from jax import lax
from jax.experimental import pallas as pl
from jax.experimental.pallas import tpu as pltpu
from jax.sharding import PartitionSpec as P

EXPERTS = 8
RANK = 16
SCALE = 2.0
NZ, NY, NX = 8, 4, 4
ROWS_A = 1024
TILE = 256
Z_ORDER = (0, 1, -1, 2, -2, 3, -3, 4)
Z_GROUPS = [[z * NY + y for z in range(NZ)] for y in range(NY)]
VMEM_BYTES = 48 * 1024 * 1024


def move_z(value, step):
    pairs = [(z * NY + y, (z + step) % NZ * NY + y) for z in range(NZ) for y in range(NY)]
    return lax.ppermute(value, "dp", pairs)


def move_y(value, step):
    pairs = [(z * NY + y, z * NY + (y + step) % NY) for z in range(NZ) for y in range(NY)]
    return lax.ppermute(value, "dp", pairs)


def move_x(value, step):
    pairs = [(x * 2 + c, (x + step) % NX * 2 + c) for x in range(NX) for c in range(2)]
    return lax.ppermute(value, "tensor", pairs)


def swap_x(value, partner):
    return lax.ppermute(value, "tensor", [(x * 2 + c, partner(x) * 2 + c) for x in range(NX) for c in range(2)])


def swap_core(value):
    return lax.ppermute(value, "tensor", [(i, i ^ 1) for i in range(2 * NX)])


def arrange_kernel(place, near, far, out):
    z, y, x, c = place[0], place[1], place[2], place[3]
    for k, dz in enumerate(Z_ORDER):
        owner = lax.rem(z - dz + NZ, NZ)
        dx = lax.rem(x - lax.div(owner, 2) + NX, NX)
        same = lax.rem(owner, 2) == c
        for j in range(NY):
            lanes = pl.ds(pl.multiple_of(lax.rem(y - j + NY, NY) * 128, 128), 128)
            at = pl.ds((k * NY + j) * 128, 128)

            @pl.when(same)
            def _():
                out[:, at] = near[dx, :, lanes]

            @pl.when(jnp.logical_not(same))
            def _():
                out[:, at] = far[dx, :, lanes]


def arrange(place, near, far):
    tokens = near.shape[1]
    return pl.pallas_call(
        arrange_kernel,
        out_shape=jax.ShapeDtypeStruct((tokens, 4096), jnp.bfloat16),
        in_specs=[
            pl.BlockSpec(memory_space=pltpu.SMEM),
            pl.BlockSpec(memory_space=pltpu.VMEM),
            pl.BlockSpec(memory_space=pltpu.VMEM),
        ],
        out_specs=pl.BlockSpec(memory_space=pltpu.VMEM),
        compiler_params=pltpu.CompilerParams(vmem_limit_bytes=VMEM_BYTES),
        cost_estimate=pl.CostEstimate(flops=0, bytes_accessed=4 * tokens * 4096, transcendentals=0),
    )(place, near, far)


def finish(left, routed, right, factor):
    dims = (((1,), (1,)), ((), ()))
    total = lax.dot_general(left[...], right, dims, preferred_element_type=jnp.float32)
    total += lax.dot_general(routed[...], factor[...], dims, preferred_element_type=jnp.float32)
    return total.astype(jnp.bfloat16)


def kernel_a(left, routed, factor, n1, n2, p1, p2, m1, m2, fp1, fp2, fm1, fm2, out):
    low = pl.program_id(0) < 2
    parts = []
    for k in range(NZ):
        i = k if k < 3 else k - 3
        n, p, m, fp, fm = (n1, p1, m1, fp1, fm1) if k < 3 else (n2, p2, m2, fp2, fm2)
        parts += [n[i], p[i], jnp.where(low, fp[i], fm[i]), m[i]]
    out[...] = finish(left, routed, jnp.concatenate(parts, axis=1), factor)


def kernel_b(place, left, routed, factor, blocks, base, out):
    del base
    z = place[0]
    parts = []
    for dz in Z_ORDER:
        owner = lax.rem(z - dz + NZ, NZ)
        parts += [blocks[owner, j] for j in range(NY)]
    out[...] = finish(left, routed, jnp.concatenate(parts, axis=1), factor)


def cost(tokens, columns):
    return pl.CostEstimate(
        flops=2 * tokens * columns * 4224,
        bytes_accessed=2 * (tokens * 4224 + columns * 4224 + tokens * columns),
        transcendentals=0,
    )


def whole(shape):
    return pl.BlockSpec(shape, lambda n: (0,) * len(shape), pipeline_mode=pl.Buffered(1))


def project(place, left, routed, factor, a_blocks, b_blocks):
    tokens, depth = left.shape
    units = factor.shape[0]
    a_tiles = ROWS_A // TILE
    b_tiles = (units - ROWS_A) // TILE
    common = [whole((tokens, depth)), whole((tokens, 128))]
    a_specs = []
    for i, block in enumerate(a_blocks):
        if i < 6:
            index = lambda n: (0, n, 0)
        elif i < 8:
            index = lambda n: (0, jnp.minimum(n, 1), 0)
        else:
            index = lambda n: (0, jnp.maximum(n - 2, 0), 0)
        a_specs.append(pl.BlockSpec((block.shape[0], TILE, 128), index))
    params = pltpu.CompilerParams(vmem_limit_bytes=VMEM_BYTES)
    out_shape = jax.ShapeDtypeStruct((tokens, units), jnp.bfloat16)
    first = pl.pallas_call(
        kernel_a,
        grid=(a_tiles,),
        out_shape=out_shape,
        in_specs=common + [pl.BlockSpec((TILE, 128), lambda n: (n, 0))] + a_specs,
        out_specs=pl.BlockSpec((tokens, TILE), lambda n: (0, n)),
        compiler_params=params,
        cost_estimate=cost(tokens, ROWS_A),
    )(left, routed, factor, *a_blocks)
    return pl.pallas_call(
        kernel_b,
        grid=(b_tiles,),
        out_shape=out_shape,
        in_specs=[pl.BlockSpec(memory_space=pltpu.SMEM)]
        + common
        + [
            pl.BlockSpec((TILE, 128), lambda n: (n + a_tiles, 0)),
            pl.BlockSpec((NZ, NY, TILE, 128), lambda n: (0, 0, n, 0)),
            pl.BlockSpec(memory_space=pl.ANY),
        ],
        out_specs=pl.BlockSpec((tokens, TILE), lambda n: (0, n + a_tiles)),
        input_output_aliases={5: 0},
        compiler_params=params,
        cost_estimate=cost(tokens, units - ROWS_A),
    )(place, left, routed, factor, b_blocks, first)


def gather_a(own):
    half = own.shape[0] // 2
    up, down = [own], [own]
    for _ in range(3):
        up.append(move_z(up[-1], 1))
        down.append(move_z(down[-1], -1))
    across = jnp.concatenate([move_z(up[3][:half], 1), move_z(down[3][half:], -1)], axis=0)
    first = jnp.stack([own, up[1], down[1]])
    second = jnp.stack([up[2], down[2], up[3], down[3], across])
    blocks = [[first, second], [], [], [], []]
    for group in (first, second):
        plus = move_y(group, 1)
        minus = move_y(group, -1)
        blocks[1].append(plus)
        blocks[2].append(minus)
        blocks[3].append(move_y(plus[:, :half], 1))
        blocks[4].append(move_y(minus[:, half:], -1))
    return [piece for pair in blocks for piece in pair]


def gather_b(own):
    half = own.shape[0] // 2
    plus = move_y(own, 1)
    minus = move_y(own, -1)
    across = jnp.concatenate([move_y(plus[:half], 1), move_y(minus[half:], -1)], axis=0)
    column = jnp.stack([own, plus, across, minus])
    return lax.all_gather(column, "dp", axis=0, axis_index_groups=Z_GROUPS)


def gather_tokens(own):
    half = own.shape[0] // 2
    plus = move_x(own, 1)
    minus = move_x(own, -1)
    across = jnp.concatenate([move_x(plus[:half], 1), move_x(minus[half:], -1)], axis=0)
    near = jnp.stack([own, plus, across, minus])
    return near, swap_core(near)


def sum_tensor(value, core):
    half = value.shape[0] // 2
    halves = value.reshape(2, half, value.shape[1])
    kept = lax.dynamic_index_in_dim(halves, core, 0, keepdims=False)
    sent = lax.dynamic_index_in_dim(halves, 1 - core, 0, keepdims=False)
    kept = kept + swap_core(sent)
    kept = kept + swap_x(kept, lambda x: x ^ 1)
    kept = kept + swap_x(kept, lambda x: 3 - x)
    other = swap_core(kept)
    return jnp.where(core == 0, jnp.concatenate([kept, other]), jnp.concatenate([other, kept]))


def per_device(
    hidden,
    layer_output_gradient,
    frozen_down_weight,
    adapter_down_weight,
    adapter_up_weight,
    chosen_expert_index,
    gates,
):
    dp_index = lax.axis_index("dp").astype(jnp.int32)
    tensor_index = lax.axis_index("tensor").astype(jnp.int32)
    core = lax.rem(tensor_index, 2)
    place = jnp.stack([lax.div(dp_index, NY), lax.rem(dp_index, NY), lax.div(tensor_index, 2), core])
    tokens_here, width = layer_output_gradient.shape
    token_scale = float(tokens_here * NZ * NY) ** (-0.5)

    a_blocks = gather_a(frozen_down_weight[:ROWS_A])
    b_blocks = gather_b(frozen_down_weight[ROWS_A:])
    near, far = gather_tokens(layer_output_gradient)
    left = arrange(place, near, far)

    inner_part = jnp.dot(hidden, adapter_down_weight, preferred_element_type=jnp.float32)
    up_here = lax.dynamic_slice_in_dim(adapter_up_weight, tensor_index * width, width, axis=1)
    outer_part = lax.dot_general(
        layer_output_gradient, up_here, (((1,), (1,)), ((), ())), preferred_element_type=jnp.float32
    )
    both = sum_tensor(jnp.concatenate([inner_part, outer_part], axis=1), core)
    inner, outer = both[:, :128], both[:, 128:]
    onehot = (
        chosen_expert_index[:, :, None] == jnp.arange(EXPERTS, dtype=jnp.int32)[None, None, :]
    ).astype(jnp.float32)
    weight = jnp.repeat(jnp.sum(onehot * gates[:, :, None], axis=1), RANK, axis=1)
    routed_outer = (SCALE * weight * outer).astype(jnp.bfloat16)
    routed_inner = (SCALE * weight * inner).astype(jnp.bfloat16)
    product = jnp.sum((inner * outer).reshape(tokens_here, EXPERTS, RANK), axis=2)
    gate_gradient = SCALE * jnp.sum(onehot * product[:, None, :], axis=2)

    over_tokens = (((0,), (0,)), ((), ()))
    down_part = lax.dot_general(hidden, routed_outer, over_tokens, preferred_element_type=jnp.float32)
    up_part = lax.dot_general(
        layer_output_gradient, routed_inner, over_tokens, preferred_element_type=jnp.float32
    )
    n = NZ * NY
    parts = jnp.concatenate([down_part.reshape(n, -1, 128), up_part.reshape(n, -1, 128)], axis=1)
    parts = lax.all_to_all(parts.astype(jnp.bfloat16), "dp", 0, 0, tiled=True)
    total = jnp.sum(parts.astype(jnp.float32), axis=0) * token_scale
    down_rows = down_part.shape[0] // n
    down_factor_gradient = lax.all_gather(total[:down_rows], "dp", axis=0, tiled=True)
    pairs = [(d * 8 + t, (4 * t + d // 8) * 8 + d % 8) for d in range(n) for t in range(8)]
    up_factor_gradient = lax.ppermute(total[down_rows:], ("dp", "tensor"), pairs).T

    hidden_input_gradient = project(place, left, routed_outer, adapter_down_weight, a_blocks, b_blocks)
    return (hidden_input_gradient, down_factor_gradient, up_factor_gradient, gate_gradient)


def solution(mesh):
    return jax.shard_map(
        per_device,
        mesh=mesh,
        in_specs=(
            P("dp", "tensor"),
            P("dp", "tensor"),
            P("tensor", "dp"),
            P("tensor", None),
            P(),
            P("dp", None),
            P("dp", None),
        ),
        out_specs=(P("dp", "tensor"), P("tensor", None), P(None, ("dp", "tensor")), P("dp", None)),
        check_vma=False,
    )
```

time: 661 us -> 272 us (0.41)
  waiting for transfers between devices: 602 us -> 57.9 us
  starting transfers between devices: 0.21 us -> 61 us
  blocking collectives: 0 us -> 56.2 us
  Pallas kernels: 0 us -> 29.7 us
  matrix products: 32.3 us -> 6.07 us
  local copies, waits for them, and re-layouts: 7.64 us -> 28.9 us
  other arithmetic: 4.24 us -> 16 us
    psum x2 -> x0, waiting for transfers between devices: 213 us -> none  [the longest x1 150 us: per_device(): lax.psum(per_expert_down_gradient, 'dp') * token_scale]
    reduce_scatter x1 -> x0, waiting for transfers between devices: 208 us -> none  [per_device(): lax.psum_scatter(per_expert_up_gradient, 'dp', scatter_dimension=1, tiled...]
    all_gather x2 -> x1, waiting for transfers between devices: 181 us -> 0.01 us  [gather_b(): return lax.all_gather(column, 'dp', axis=0, axis_index_groups=Z_GROUPS)]
    all_gather x0 -> x1, blocking collectives: none -> 56.2 us  [per_device(): lax.all_gather(total[:down_rows], 'dp', axis=0, tiled=True)]
    ppermute x0 -> x30, starting transfers between devices: none -> 51.5 us  [the longest x12 20.2 us: move_y(): return lax.ppermute(value, 'dp', pairs)]
    ppermute x0 -> x30, waiting for transfers between devices: none -> 50.8 us  [the longest x8 28.5 us: move_z(): return lax.ppermute(value, 'dp', pairs)]
    pallas_call x0 -> x3, Pallas kernels: none -> 29.7 us  [the longest x1 12.2 us: project(): pl.pallas_call(kernel_a, grid=(a_tiles,), out_shape=out_shape, in_specs=c...]
    dot_general x5 -> x3, matrix products: 29.4 us -> 5.02 us  [the longest x1 2.09 us: per_device(): lax.dot_general(layer_output_gradient, routed_inner, over_tokens, preferr...]
  transfers between devices with their start and end apart: 5 -> 32, of which waited for: 5 -> 12; matrix products, arithmetic and copies ran while one was open for 2% -> 17% of each run, Pallas kernels for 0% -> 7%
where the time goes in v1:
time: 272 us; the launch traced here: 270 us
  starting transfers between devices  61 us (22%)
  waiting for transfers between devices  57.9 us (21%)
  blocking collectives  56.2 us (21%)
  Pallas kernels  29.7 us (11%)
  local copies, waits for them, and re-layouts  28.9 us (11%)
  other arithmetic  16 us (6%)
  between operations  14.3 us (5%)
  matrix products  6.07 us (2%)
    all_gather x1, blocking collectives, per_device(): lax.all_gather(total[:down_rows], 'dp', axis=0, tiled=True)  56.2 us
    ppermute x8, waiting for transfers between devices, move_z(): return lax.ppermute(value, 'dp', pairs)  28.5 us
    ppermute x12, starting transfers between devices, move_y(): return lax.ppermute(value, 'dp', pairs)  20.2 us
    ppermute x8, starting transfers between devices, move_z(): return lax.ppermute(value, 'dp', pairs)  17.3 us
    ppermute x12, waiting for transfers between devices, move_y(): return lax.ppermute(value, 'dp', pairs)  15.6 us
    pallas_call x1, Pallas kernels, project(): pl.pallas_call(kernel_a, grid=(a_tiles,), out_shape=out_shape, in_specs=c...  12.2 us
    pallas_call x1, Pallas kernels, project(): pl.pallas_call(kernel_b, grid=(b_tiles,), out_shape=out_shape, in_specs=[...  10 us
    all_to_all x1, starting transfers between devices, per_device(): parts = lax.all_to_all(parts.astype(jnp.bfloat16), 'dp', 0, 0, tiled=True)  9.46 us
  transfers between devices with their start and end apart: 32, of which 12 were waited for; matrix products, arithmetic and copies ran while one was open for 17% of the time, Pallas kernels for 7%

profile of v1, /device:TPU:4, one launch (start us, length us, event | category | flops | bytes accessed | tf_op | source)
XLA Modules:
  0.0 270.1 jit_solution(12727434645586456299)
XLA Ops:
  11.7 4.7 %collective-permute-done.9 = bf16[768,128]{1,0:T(8,128)(2,1)S(1)} collective-permute-done((bf16[768,128]{1,0:T(8,128)(2,1)S(1)}, bf16[768,128]{1,0:T(8,128)(2,1)S(1)}, u32[]{:S(2)}, u32[]{:S(2)}) %collective-permute-start.9) | collective-permute-done | bytes 196640 | tf_op jit(solution)/shard_map/ppermute | solution.py:28
  16.8 3.0 %collective-permute-start.12 = (bf16[384,128]{1,0:T(8,128)(2,1)S(1)}, bf16[384,128]{1,0:T(8,128)(2,1)S(1)}, u32[]{:S(2)}, u32[]{:S(2)}) collective-permute-start(bf16[384,128]{1,0:T(8,128)(2,1)S(1)} %slice.68), channel_id=1, source_target_pairs={{0,24},{8,0},{16,8},{24,16},{32,56},{40,32},{48,40},{56,48},{64,88... | collective-permute-start | bytes 294920 | tf_op jit(solution)/shard_map/ppermute | solution.py:28
  19.8 2.5 collective-permute-done.10
  26.9 2.3 copy.42
  32.7 1.9 collective-permute-start.13
  34.6 3.9 %collective-permute-start.14 = (bf16[1024,128]{1,0:T(8,128)(2,1)S(1)}, bf16[1024,128]{1,0:T(8,128)(2,1)}, u32[]{:S(2)}, u32[]{:S(2)}) collective-permute-start(bf16[1024,128]{1,0:T(8,128)(2,1)S(1)} %get-tuple-element.7), channel_id=1, source_target_pairs={{0,224},{8,232},{16,240},{24,248},{32,0},{40,8},{48,16},{56,24},{6... | collective-permute-start | bytes 786440 | tf_op jit(solution)/shard_map/ppermute | solution.py:23
  40.6 9.3 %collective-permute-done.13 = bf16[1024,128]{1,0:T(8,128)(2,1)} collective-permute-done((bf16[1024,128]{1,0:T(8,128)(2,1)S(1)}, bf16[1024,128]{1,0:T(8,128)(2,1)}, u32[]{:S(2)}, u32[]{:S(2)}) %collective-permute-start.13) | collective-permute-done | bytes 262176 | tf_op jit(solution)/shard_map/ppermute | solution.py:23
  50.6 3.8 %collective-permute-start.16 = (bf16[1024,128]{1,0:T(8,128)(2,1)}, bf16[1024,128]{1,0:T(8,128)(2,1)S(1)}, u32[]{:S(2)}, u32[]{:S(2)}) collective-permute-start(bf16[1024,128]{1,0:T(8,128)(2,1)} %collective-permute-done.14), channel_id=1, source_target_pairs={{0,224},{8,232},{16,240},{24,248},{32,0},{40,8},{48,16},{56,24},{6... | collective-permute-start | bytes 786440 | tf_op jit(solution)/shard_map/ppermute | solution.py:23
  56.9 8.8 %collective-permute-done.15 = bf16[1024,128]{1,0:T(8,128)(2,1)} collective-permute-done((bf16[1024,128]{1,0:T(8,128)(2,1)}, bf16[1024,128]{1,0:T(8,128)(2,1)}, u32[]{:S(2)}, u32[]{:S(2)}) %collective-permute-start.15) | collective-permute-done | bytes 262176 | tf_op jit(solution)/shard_map/ppermute | solution.py:23
  66.5 3.6 %collective-permute-start.18 = (bf16[1024,128]{1,0:T(8,128)(2,1)S(1)}, bf16[1024,128]{1,0:T(8,128)(2,1)S(1)}, u32[]{:S(2)}, u32[]{:S(2)}) collective-permute-start(bf16[1024,128]{1,0:T(8,128)(2,1)S(1)} %collective-permute-done.16), channel_id=1, source_target_pairs={{0,224},{8,232},{16,240},{24,248},{32,0},{40,8},{48,16},{56,24},{6... | collective-permute-start | bytes 786440 | tf_op jit(solution)/shard_map/ppermute | solution.py:23
  72.6 8.5 %collective-permute-done.17 = bf16[1024,128]{1,0:T(8,128)(2,1)S(1)} collective-permute-done((bf16[1024,128]{1,0:T(8,128)(2,1)}, bf16[1024,128]{1,0:T(8,128)(2,1)S(1)}, u32[]{:S(2)}, u32[]{:S(2)}) %collective-permute-start.17) | collective-permute-done | bytes 262176 | tf_op jit(solution)/shard_map/ppermute | solution.py:23
  81.7 3.8 %collective-permute-start.20 = (bf16[512,128]{1,0:T(8,128)(2,1)S(1)}, bf16[512,128]{1,0:T(8,128)(2,1)S(1)}, u32[]{:S(2)}, u32[]{:S(2)}) collective-permute-start(bf16[512,128]{1,0:T(8,128)(2,1)S(1)} %slice.70), channel_id=1, source_target_pairs={{0,224},{8,232},{16,240},{24,248},{32,0},{40,8},{48,16},{56,24},{6... | collective-permute-start | bytes 393224 | tf_op jit(solution)/shard_map/ppermute | solution.py:23
  93.1 2.9 %collective-permute-start.24 = (bf16[5,1024,128]{2,1,0:T(8,128)(2,1)}, bf16[5,1024,128]{2,1,0:T(8,128)(2,1)}, u32[]{:S(2)}, u32[]{:S(2)}) collective-permute-start(bf16[5,1024,128]{2,1,0:T(8,128)(2,1)} %fusion.2.n2), channel_id=1, source_target_pairs={{0,24},{8,0},{16,8},{24,16},{32,56},{40,32},{48,40},{56,48},{64,88... | collective-permute-start | bytes 3932168 | tf_op jit(solution)/shard_map/ppermute | solution.py:28
  97.8 5.0 %collective-permute-done.1 = bf16[384,512]{1,0:T(8,128)(2,1)S(1)} collective-permute-done((bf16[384,512]{1,0:T(8,128)(2,1)S(1)}, bf16[384,512]{1,0:T(8,128)(2,1)S(1)}, u32[]{:S(2)}, u32[]{:S(2)}) %collective-permute-start.1) | collective-permute-done | bytes 393248 | tf_op jit(solution)/shard_map/ppermute | solution.py:33
  102.9 3.1 %pad_maximum_fusion.near = bf16[4,768,512]{2,1,0:T(8,128)(2,1)} fusion(bf16[1,768,512]{2,1,0:T(8,128)(2,1)} %bitcast.7, bf16[1,768,512]{2,1,0:T(8,128)(2,1)S(1)} %maximum_bitcast_fusion, bf16[1,768,512]{2,1,0:T(8,128)(2,1)} %bitcast.5, bf16[1,768,512]{2,1,0:T(8,128)(2,1)} %bitcast.4), kind=kLoop, calls=%fused_computation | loop fusion | flops 4718592 | bytes 6291456 | tf_op jit(solution)/shard_map/stack | solution.py:196
  107.7 1.9 copy.41
  111.6 1.9 copy.37
  116.0 2.1 fusion.1
  119.1 2.0 copy.38
  123.0 9.5 %all-to-all-start = ((bf16[32,72,128]{2,1,0:T(8,128)(2,1)}), bf16[32,72,128]{2,1,0:T(8,128)(2,1)}, u32[]{:S(2)}, u32[]{:S(2)}) async-start(bf16[32,72,128]{2,1,0:T(8,128)(2,1)} %pad_maximum_fusion.4), calls=%async_computation | async-start | bytes 1179648 | tf_op jit(solution)/shard_map/all_to_all | solution.py:256
  132.5 2.1 pad_maximum_fusion.3.n1
  137.8 2.0 slice.72
  140.3 2.0 slice.74
  142.3 2.7 %collective-permute-start.28 = (bf16[5,512,128]{2,1,0:T(8,128)(2,1)}, bf16[5,512,128]{2,1,0:T(8,128)(2,1)}, u32[]{:S(2)}, u32[]{:S(2)}) collective-permute-start(bf16[5,512,128]{2,1,0:T(8,128)(2,1)} %slice.74), channel_id=1, source_target_pairs={{0,24},{8,0},{16,8},{24,16},{32,56},{40,32},{48,40},{56,48},{64,88... | collective-permute-start | bytes 1966088 | tf_op jit(solution)/shard_map/ppermute | solution.py:28
  145.0 7.1 %all-to-all-done = bf16[32,72,128]{2,1,0:T(8,128)(2,1)} async-done(((bf16[32,72,128]{2,1,0:T(8,128)(2,1)}), bf16[32,72,128]{2,1,0:T(8,128)(2,1)}, u32[]{:S(2)}, u32[]{:S(2)}) %all-to-all-start) | async-done | bytes 589856 | tf_op jit(solution)/shard_map/all_to_all | solution.py:256
  153.3 8.4 %collective-permute-done.21.p1 = bf16[3,1024,128]{2,1,0:T(8,128)(2,1)} collective-permute-done((bf16[3,1024,128]{2,1,0:T(8,128)(2,1)}, bf16[3,1024,128]{2,1,0:T(8,128)(2,1)}, u32[]{:S(2)}, u32[]{:S(2)}) %collective-permute-start.21) | collective-permute-done | bytes 786464 | tf_op jit(solution)/shard_map/ppermute | solution.py:28
  161.7 7.8 %collective-permute-start.29 = (f32[16,128]{1,0:T(8,128)S(1)}, f32[16,128]{1,0:T(8,128)S(1)}, u32[]{:S(2)}, u32[]{:S(2)}) collective-permute-start(f32[16,128]{1,0:T(8,128)S(1)} %slice.77), channel_id=1, source_target_pairs={{0,0},{1,32},{2,64},{3,96},{4,128},{5,160},{6,192},{7,224},{8,1},{... | collective-permute-start | bytes 24584 | tf_op jit(solution)/shard_map/ppermute | solution.py:261
  171.9 3.3 %collective-permute-start.27 = (bf16[3,512,128]{2,1,0:T(8,128)(2,1)S(1)}, bf16[3,512,128]{2,1,0:T(8,128)(2,1)S(1)}, u32[]{:S(2)}, u32[]{:S(2)}) collective-permute-start(bf16[3,512,128]{2,1,0:T(8,128)(2,1)S(1)} %slice.73), channel_id=1, source_target_pairs={{0,24},{8,0},{16,8},{24,16},{32,56},{40,32},{48,40},{56,48},{64,88... | collective-permute-start | bytes 1179656 | tf_op jit(solution)/shard_map/ppermute | solution.py:28
  175.8 56.2 %all_gather.11 = f32[1792,128]{1,0:T(8,128)} all-gather(f32[56,128]{1,0:T(8,128)S(1)} %slice.76), channel_id=1, replica_groups=mesh['dp'=32,'tensor'=8] {'dp'}, dimensions={0}, use_global_device_ids=true | all-gather | bytes 946176 | tf_op jit(solution)/shard_map/all_gather | solution.py:259
  232.0 7.4 %shard_map.102.left = bf16[768,4096]{1,0:T(8,128)(2,1)} custom-call(s32[4]{0:T(128)S(1)} %pad_add_fusion.place, bf16[4,768,512]{2,1,0:T(8,128)(2,1)} %pad_maximum_fusion.near, bf16[4,768,512]{2,1,0:T(8,128)(2,1)} %collective-permute-done.4.far), custom_call_target="tpu_custom_call" | custom-call | bytes 12582912 | tf_op jit(solution)/shard_map/pallas_call | solution.py:65
  239.5 12.2 %shard_map.103.base = bf16[768,1792]{1,0:T(8,128)(2,1)} custom-call(bf16[768,4096]{1,0:T(8,128)(2,1)} %shard_map.102.left, bf16[768,128]{1,0:T(8,128)(2,1)S(1)} %multiply_convert_fusion.1.routed, bf16[1792,128]{1,0:T(8,128)(2,1)S(1)} %copy-done.1, bf16[3,1024,128]{2,1,0:T(8,128)(2,1)} %pad_maximum_fusion.3.n1, bf16[5,1024,128]{2,1,0:T(8,128)(2,1)} %fusion.2.n2, ...), custom_call_target="tpu_custom_call" | custom-call | flops 6643777536 | bytes 16711680 | tf_op jit(solution)/shard_map/pallas_call | solution.py:135
  251.7 10.0 %shard_map.104 = bf16[768,1792]{1,0:T(8,128)(2,1)} custom-call(s32[4]{0:T(128)S(1)} %pad_add_fusion.place, bf16[768,4096]{1,0:T(8,128)(2,1)} %shard_map.102.left, bf16[768,128]{1,0:T(8,128)(2,1)S(1)} %multiply_convert_fusion.1.routed, bf16[1792,128]{1,0:T(8,128)(2,1)S(1)} %copy-done.1, ...), custom_call_target="tpu_custom_call", output_to_operand_aliasing={{}: (5, {})} | custom-call | flops 4982833152 | bytes 14155776 | tf_op jit(solution)/shard_map/pallas_call | solution.py:144
  (105 shorter events, 50.0 us)
Async XLA Ops:
  7.2 244.6 %all-gather.3.cloned.1.call-start = ((), (), s32[]{:S(2)}) async-start(), calls=%async_computation.1 | async-start | bytes 7077888 | tf_op jit(solution)/shard_map/all_gather | solution.py:188
  8.4 8.0 %collective-permute-start.9 = (bf16[768,128]{1,0:T(8,128)(2,1)S(1)}, bf16[768,128]{1,0:T(8,128)(2,1)S(1)}, u32[]{:S(2)}, u32[]{:S(2)}) collective-permute-start(bf16[768,128]{1,0:T(8,128)(2,1)S(1)} %get-tuple-element.9), channel_id=1, source_target_pairs={{0,8},{8,16},{16,24},{24,0},{32,40},{40,48},{48,56},{56,32},{64,72... | collective-permute-start | bytes 589832 | tf_op jit(solution)/shard_map/ppermute | solution.py:28
  10.0 6.7 %collective-permute-start.11 = (bf16[768,128]{1,0:T(8,128)(2,1)S(1)}, bf16[768,128]{1,0:T(8,128)(2,1)S(1)}, u32[]{:S(2)}, u32[]{:S(2)}) collective-permute-start(bf16[768,128]{1,0:T(8,128)(2,1)S(1)} %get-tuple-element.9), channel_id=1, source_target_pairs={{0,24},{8,0},{16,8},{24,16},{32,56},{40,32},{48,40},{56,48},{64,88... | collective-permute-start | bytes 589832 | tf_op jit(solution)/shard_map/ppermute | solution.py:28
  16.4 5.9 %collective-permute-start.10 = (bf16[384,128]{1,0:T(8,128)(2,1)S(1)}, bf16[384,128]{1,0:T(8,128)(2,1)S(1)}, u32[]{:S(2)}, u32[]{:S(2)}) collective-permute-start(bf16[384,128]{1,0:T(8,128)(2,1)S(1)} %slice.67), channel_id=1, source_target_pairs={{0,8},{8,16},{16,24},{24,0},{32,40},{40,48},{48,56},{56,32},{64,72... | collective-permute-start | bytes 294920 | tf_op jit(solution)/shard_map/ppermute | solution.py:28
  16.8 5.5 %collective-permute-start.12 = (bf16[384,128]{1,0:T(8,128)(2,1)S(1)}, bf16[384,128]{1,0:T(8,128)(2,1)S(1)}, u32[]{:S(2)}, u32[]{:S(2)}) collective-permute-start(bf16[384,128]{1,0:T(8,128)(2,1)S(1)} %slice.68), channel_id=1, source_target_pairs={{0,24},{8,0},{16,8},{24,16},{32,56},{40,32},{48,40},{56,48},{64,88... | collective-permute-start | bytes 294920 | tf_op jit(solution)/shard_map/ppermute | solution.py:28
  31.0 23.5 %collective-permute-start.5 = (f32[384,256]{1,0:T(8,128)}, f32[384,256]{1,0:T(8,128)}, u32[]{:S(2)}, u32[]{:S(2)}) collective-permute-start(f32[384,256]{1,0:T(8,128)} %dynamic-slice_bitcast_fusion), channel_id=1, source_target_pairs={{0,1},{1,0},{2,3},{3,2},{4,5},{5,4},{6,7},{7,6},{8,9},{9,8},{10,11... | collective-permute-start | bytes 1179656 | tf_op jit(solution)/shard_map/ppermute | solution.py:41
  32.7 17.2 %collective-permute-start.13 = (bf16[1024,128]{1,0:T(8,128)(2,1)S(1)}, bf16[1024,128]{1,0:T(8,128)(2,1)}, u32[]{:S(2)}, u32[]{:S(2)}) collective-permute-start(bf16[1024,128]{1,0:T(8,128)(2,1)S(1)} %get-tuple-element.7), channel_id=1, source_target_pairs={{0,32},{8,40},{16,48},{24,56},{32,64},{40,72},{48,80},{56,88},{64,... | collective-permute-start | bytes 786440 | tf_op jit(solution)/shard_map/ppermute | solution.py:23
  34.6 16.0 %collective-permute-start.14 = (bf16[1024,128]{1,0:T(8,128)(2,1)S(1)}, bf16[1024,128]{1,0:T(8,128)(2,1)}, u32[]{:S(2)}, u32[]{:S(2)}) collective-permute-start(bf16[1024,128]{1,0:T(8,128)(2,1)S(1)} %get-tuple-element.7), channel_id=1, source_target_pairs={{0,224},{8,232},{16,240},{24,248},{32,0},{40,8},{48,16},{56,24},{6... | collective-permute-start | bytes 786440 | tf_op jit(solution)/shard_map/ppermute | solution.py:23
  38.6 47.6 %collective-permute-start = (bf16[768,512]{1,0:T(8,128)(2,1)}, bf16[768,512]{1,0:T(8,128)(2,1)}, u32[]{:S(2)}, u32[]{:S(2)}) collective-permute-start(bf16[768,512]{1,0:T(8,128)(2,1)} %param.8), channel_id=1, source_target_pairs={{0,2},{1,3},{2,4},{3,5},{4,6},{5,7},{6,0},{7,1},{8,10},{9,11},{10,... | collective-permute-start | bytes 2359304 | tf_op jit(solution)/shard_map/ppermute | solution.py:33
  39.8 48.6 %collective-permute-start.2 = (bf16[768,512]{1,0:T(8,128)(2,1)}, bf16[768,512]{1,0:T(8,128)(2,1)}, u32[]{:S(2)}, u32[]{:S(2)}) collective-permute-start(bf16[768,512]{1,0:T(8,128)(2,1)} %param.8), channel_id=1, source_target_pairs={{0,6},{1,7},{2,0},{3,1},{4,2},{5,3},{6,4},{7,5},{8,14},{9,15},{10,... | collective-permute-start | bytes 2359304 | tf_op jit(solution)/shard_map/ppermute | solution.py:33
  49.9 15.8 %collective-permute-start.15 = (bf16[1024,128]{1,0:T(8,128)(2,1)}, bf16[1024,128]{1,0:T(8,128)(2,1)}, u32[]{:S(2)}, u32[]{:S(2)}) collective-permute-start(bf16[1024,128]{1,0:T(8,128)(2,1)} %collective-permute-done.13), channel_id=1, source_target_pairs={{0,32},{8,40},{16,48},{24,56},{32,64},{40,72},{48,80},{56,88},{64,... | collective-permute-start | bytes 786440 | tf_op jit(solution)/shard_map/ppermute | solution.py:23
  50.6 15.9 %collective-permute-start.16 = (bf16[1024,128]{1,0:T(8,128)(2,1)}, bf16[1024,128]{1,0:T(8,128)(2,1)S(1)}, u32[]{:S(2)}, u32[]{:S(2)}) collective-permute-start(bf16[1024,128]{1,0:T(8,128)(2,1)} %collective-permute-done.14), channel_id=1, source_target_pairs={{0,224},{8,232},{16,240},{24,248},{32,0},{40,8},{48,16},{56,24},{6... | collective-permute-start | bytes 786440 | tf_op jit(solution)/shard_map/ppermute | solution.py:23
  55.6 29.9 %collective-permute-start.6 = (f32[384,256]{1,0:T(8,128)S(1)}, f32[384,256]{1,0:T(8,128)S(1)}, u32[]{:S(2)}, u32[]{:S(2)}) collective-permute-start(f32[384,256]{1,0:T(8,128)S(1)} %bitcast_add_fusion), channel_id=1, source_target_pairs={{0,2},{1,3},{2,0},{3,1},{4,6},{5,7},{6,4},{7,5},{8,10},{9,11},{10,... | collective-permute-start | bytes 1179656 | tf_op jit(solution)/shard_map/ppermute | solution.py:37
  65.7 15.4 %collective-permute-start.17 = (bf16[1024,128]{1,0:T(8,128)(2,1)}, bf16[1024,128]{1,0:T(8,128)(2,1)S(1)}, u32[]{:S(2)}, u32[]{:S(2)}) collective-permute-start(bf16[1024,128]{1,0:T(8,128)(2,1)} %collective-permute-done.15), channel_id=1, source_target_pairs={{0,32},{8,40},{16,48},{24,56},{32,64},{40,72},{48,80},{56,88},{64,... | collective-permute-start | bytes 786440 | tf_op jit(solution)/shard_map/ppermute | solution.py:23
  66.5 15.1 %collective-permute-start.18 = (bf16[1024,128]{1,0:T(8,128)(2,1)S(1)}, bf16[1024,128]{1,0:T(8,128)(2,1)S(1)}, u32[]{:S(2)}, u32[]{:S(2)}) collective-permute-start(bf16[1024,128]{1,0:T(8,128)(2,1)S(1)} %collective-permute-done.16), channel_id=1, source_target_pairs={{0,224},{8,232},{16,240},{24,248},{32,0},{40,8},{48,16},{56,24},{6... | collective-permute-start | bytes 786440 | tf_op jit(solution)/shard_map/ppermute | solution.py:23
  81.1 10.7 %collective-permute-start.19 = (bf16[512,128]{1,0:T(8,128)(2,1)S(1)}, bf16[512,128]{1,0:T(8,128)(2,1)S(1)}, u32[]{:S(2)}, u32[]{:S(2)}) collective-permute-start(bf16[512,128]{1,0:T(8,128)(2,1)S(1)} %slice.69), channel_id=1, source_target_pairs={{0,32},{8,40},{16,48},{24,56},{32,64},{40,72},{48,80},{56,88},{64,... | collective-permute-start | bytes 393224 | tf_op jit(solution)/shard_map/ppermute | solution.py:23
  81.7 10.2 %collective-permute-start.20 = (bf16[512,128]{1,0:T(8,128)(2,1)S(1)}, bf16[512,128]{1,0:T(8,128)(2,1)S(1)}, u32[]{:S(2)}, u32[]{:S(2)}) collective-permute-start(bf16[512,128]{1,0:T(8,128)(2,1)S(1)} %slice.70), channel_id=1, source_target_pairs={{0,224},{8,232},{16,240},{24,248},{32,0},{40,8},{48,16},{56,24},{6... | collective-permute-start | bytes 393224 | tf_op jit(solution)/shard_map/ppermute | solution.py:23
  85.5 12.1 %collective-permute-start.7 = (f32[384,256]{1,0:T(8,128)S(1)}, f32[384,256]{1,0:T(8,128)S(1)}, u32[]{:S(2)}, u32[]{:S(2)}) collective-permute-start(f32[384,256]{1,0:T(8,128)S(1)} %add.24), channel_id=1, source_target_pairs={{0,6},{1,7},{2,4},{3,5},{4,2},{5,3},{6,0},{7,1},{8,14},{9,15},{10,... | collective-permute-start | bytes 1179656 | tf_op jit(solution)/shard_map/ppermute | solution.py:37
  87.2 15.6 %collective-permute-start.1 = (bf16[384,512]{1,0:T(8,128)(2,1)S(1)}, bf16[384,512]{1,0:T(8,128)(2,1)S(1)}, u32[]{:S(2)}, u32[]{:S(2)}) collective-permute-start(bf16[384,512]{1,0:T(8,128)(2,1)S(1)} %slice.64), channel_id=1, source_target_pairs={{0,2},{1,3},{2,4},{3,5},{4,6},{5,7},{6,0},{7,1},{8,10},{9,11},{10,... | collective-permute-start | bytes 1179656 | tf_op jit(solution)/shard_map/ppermute | solution.py:33
  89.3 13.5 %collective-permute-start.3 = (bf16[384,512]{1,0:T(8,128)(2,1)S(1)}, bf16[384,512]{1,0:T(8,128)(2,1)S(1)}, u32[]{:S(2)}, u32[]{:S(2)}) collective-permute-start(bf16[384,512]{1,0:T(8,128)(2,1)S(1)} %slice.65), channel_id=1, source_target_pairs={{0,6},{1,7},{2,0},{3,1},{4,2},{5,3},{6,4},{7,5},{8,14},{9,15},{10,... | collective-permute-start | bytes 1179656 | tf_op jit(solution)/shard_map/ppermute | solution.py:33
  92.6 45.2 %collective-permute-start.22 = (bf16[5,1024,128]{2,1,0:T(8,128)(2,1)}, bf16[5,1024,128]{2,1,0:T(8,128)(2,1)}, u32[]{:S(2)}, u32[]{:S(2)}) collective-permute-start(bf16[5,1024,128]{2,1,0:T(8,128)(2,1)} %fusion.2.n2), channel_id=1, source_target_pairs={{0,8},{8,16},{16,24},{24,0},{32,40},{40,48},{48,56},{56,32},{64,72... | collective-permute-start | bytes 3932168 | tf_op jit(solution)/shard_map/ppermute | solution.py:28
  93.1 47.2 %collective-permute-start.24 = (bf16[5,1024,128]{2,1,0:T(8,128)(2,1)}, bf16[5,1024,128]{2,1,0:T(8,128)(2,1)}, u32[]{:S(2)}, u32[]{:S(2)}) collective-permute-start(bf16[5,1024,128]{2,1,0:T(8,128)(2,1)} %fusion.2.n2), channel_id=1, source_target_pairs={{0,24},{8,0},{16,8},{24,16},{32,56},{40,32},{48,40},{56,48},{64,88... | collective-permute-start | bytes 3932168 | tf_op jit(solution)/shard_map/ppermute | solution.py:28
  97.7 8.3 %collective-permute-start.8 = (f32[384,256]{1,0:T(8,128)S(1)}, f32[384,256]{1,0:T(8,128)S(1)}, u32[]{:S(2)}, u32[]{:S(2)}) collective-permute-start(f32[384,256]{1,0:T(8,128)S(1)} %add.25), channel_id=1, source_target_pairs={{0,1},{1,0},{2,3},{3,2},{4,5},{5,4},{6,7},{7,6},{8,9},{9,8},{10,11... | collective-permute-start | bytes 1179656 | tf_op jit(solution)/shard_map/ppermute | solution.py:41
  106.0 126.0 %collective-permute-start.4 = (bf16[4,768,512]{2,1,0:T(8,128)(2,1)}, bf16[4,768,512]{2,1,0:T(8,128)(2,1)}, u32[]{:S(2)}, u32[]{:S(2)}) collective-permute-start(bf16[4,768,512]{2,1,0:T(8,128)(2,1)} %pad_maximum_fusion.near), channel_id=1, source_target_pairs={{0,1},{1,0},{2,3},{3,2},{4,5},{5,4},{6,7},{7,6},{8,9},{9,8},{10,11... | collective-permute-start | bytes 9437192 | tf_op jit(solution)/shard_map/ppermute | solution.py:41
  123.0 29.1 %all-to-all-start = ((bf16[32,72,128]{2,1,0:T(8,128)(2,1)}), bf16[32,72,128]{2,1,0:T(8,128)(2,1)}, u32[]{:S(2)}, u32[]{:S(2)}) async-start(bf16[32,72,128]{2,1,0:T(8,128)(2,1)} %pad_maximum_fusion.4), calls=%async_computation | async-start | bytes 1179648 | tf_op jit(solution)/shard_map/all_to_all | solution.py:256
  134.6 27.1 %collective-permute-start.21 = (bf16[3,1024,128]{2,1,0:T(8,128)(2,1)}, bf16[3,1024,128]{2,1,0:T(8,128)(2,1)}, u32[]{:S(2)}, u32[]{:S(2)}) collective-permute-start(bf16[3,1024,128]{2,1,0:T(8,128)(2,1)} %pad_maximum_fusion.3.n1), channel_id=1, source_target_pairs={{0,8},{8,16},{16,24},{24,0},{32,40},{40,48},{48,56},{56,32},{64,72... | collective-permute-start | bytes 2359304 | tf_op jit(solution)/shard_map/ppermute | solution.py:28
  136.3 34.3 %collective-permute-start.23 = (bf16[3,1024,128]{2,1,0:T(8,128)(2,1)}, bf16[3,1024,128]{2,1,0:T(8,128)(2,1)}, u32[]{:S(2)}, u32[]{:S(2)}) collective-permute-start(bf16[3,1024,128]{2,1,0:T(8,128)(2,1)} %pad_maximum_fusion.3.n1), channel_id=1, source_target_pairs={{0,24},{8,0},{16,8},{24,16},{32,56},{40,32},{48,40},{56,48},{64,88... | collective-permute-start | bytes 2359304 | tf_op jit(solution)/shard_map/ppermute | solution.py:28
  139.8 99.7 %collective-permute-start.26 = (bf16[5,512,128]{2,1,0:T(8,128)(2,1)}, bf16[5,512,128]{2,1,0:T(8,128)(2,1)}, u32[]{:S(2)}, u32[]{:S(2)}) collective-permute-start(bf16[5,512,128]{2,1,0:T(8,128)(2,1)} %slice.72), channel_id=1, source_target_pairs={{0,8},{8,16},{16,24},{24,0},{32,40},{40,48},{48,56},{56,32},{64,72... | collective-permute-start | bytes 1966088 | tf_op jit(solution)/shard_map/ppermute | solution.py:28
  142.3 97.2 %collective-permute-start.28 = (bf16[5,512,128]{2,1,0:T(8,128)(2,1)}, bf16[5,512,128]{2,1,0:T(8,128)(2,1)}, u32[]{:S(2)}, u32[]{:S(2)}) collective-permute-start(bf16[5,512,128]{2,1,0:T(8,128)(2,1)} %slice.74), channel_id=1, source_target_pairs={{0,24},{8,0},{16,8},{24,16},{32,56},{40,32},{48,40},{56,48},{64,88... | collective-permute-start | bytes 1966088 | tf_op jit(solution)/shard_map/ppermute | solution.py:28
  161.7 10.3 %collective-permute-start.29 = (f32[16,128]{1,0:T(8,128)S(1)}, f32[16,128]{1,0:T(8,128)S(1)}, u32[]{:S(2)}, u32[]{:S(2)}) collective-permute-start(f32[16,128]{1,0:T(8,128)S(1)} %slice.77), channel_id=1, source_target_pairs={{0,0},{1,32},{2,64},{3,96},{4,128},{5,160},{6,192},{7,224},{8,1},{... | collective-permute-start | bytes 24584 | tf_op jit(solution)/shard_map/ppermute | solution.py:261
  170.6 68.9 %collective-permute-start.25 = (bf16[3,512,128]{2,1,0:T(8,128)(2,1)S(1)}, bf16[3,512,128]{2,1,0:T(8,128)(2,1)S(1)}, u32[]{:S(2)}, u32[]{:S(2)}) collective-permute-start(bf16[3,512,128]{2,1,0:T(8,128)(2,1)S(1)} %slice.71), channel_id=1, source_target_pairs={{0,8},{8,16},{16,24},{24,0},{32,40},{40,48},{48,56},{56,32},{64,72... | collective-permute-start | bytes 1179656 | tf_op jit(solution)/shard_map/ppermute | solution.py:28
  171.9 67.5 %collective-permute-start.27 = (bf16[3,512,128]{2,1,0:T(8,128)(2,1)S(1)}, bf16[3,512,128]{2,1,0:T(8,128)(2,1)S(1)}, u32[]{:S(2)}, u32[]{:S(2)}) collective-permute-start(bf16[3,512,128]{2,1,0:T(8,128)(2,1)S(1)} %slice.73), channel_id=1, source_target_pairs={{0,24},{8,0},{16,8},{24,16},{32,56},{40,32},{48,40},{56,48},{64,88... | collective-permute-start | bytes 1179656 | tf_op jit(solution)/shard_map/ppermute | solution.py:28
  (8 other events, 41.6 us)
Sparse Core Ops, SparseCore 0:
  23.4 95.7 all-gather.2

commit v2 on v0

v2 whole, which is shorter than its diff:
```python
import jax
import jax.numpy as jnp
from jax import lax
from jax.experimental import pallas as pl
from jax.experimental.pallas import tpu as pltpu
from jax.sharding import PartitionSpec as P

EXPERTS = 8
RANK = 16
SCALE = 2.0
NZ, NY, NX = 8, 4, 4
ROWS_A = 1024
TILE = 256
Z_GROUPS = [[z * NY + y for z in range(NZ)] for y in range(NY)]
VMEM_BYTES = 60 * 1024 * 1024
LAST = (((1,), (1,)), ((), ()))
FIRST = (((0,), (0,)), ((), ()))


def move_y(value, step):
    pairs = [(z * NY + y, z * NY + (y + step) % NY) for z in range(NZ) for y in range(NY)]
    return lax.ppermute(value, "dp", pairs)


def turn_x(value):
    pairs = [(x * 2 + c, (x + 1 - 2 * c) % NX * 2 + c) for x in range(NX) for c in range(2)]
    return lax.ppermute(value, "tensor", pairs)


def swap_x(value, partner):
    return lax.ppermute(value, "tensor", [(x * 2 + c, partner(x) * 2 + c) for x in range(NX) for c in range(2)])


def swap_core(value):
    return lax.ppermute(value, "tensor", [(i, i ^ 1) for i in range(2 * NX)])


def full(*shape):
    return pl.BlockSpec(shape, lambda n: (0,) * len(shape))


def smem():
    return pl.BlockSpec(memory_space=pltpu.SMEM)


PARAMS = pltpu.CompilerParams(vmem_limit_bytes=VMEM_BYTES)
LIGHT = pl.CostEstimate(flops=0, bytes_accessed=0, transcendentals=0)


def project_low_rank_kernel(place, hidden, factor, gradient, up, kept, sent):
    half = kept.shape[0]
    width = gradient.shape[1]
    tensor = place[2] * 2 + place[3]
    lanes = pl.ds(pl.multiple_of(tensor * width, width), width)
    mine = pl.ds(pl.multiple_of(place[3] * half, half), half)
    other = pl.ds(pl.multiple_of((1 - place[3]) * half, half), half)
    for rows, out in ((mine, kept), (other, sent)):
        out[:, :128] = jnp.dot(hidden[rows, :], factor[...], preferred_element_type=jnp.float32)
        out[:, 128:] = lax.dot_general(
            gradient[rows, :], up[:, lanes], LAST, preferred_element_type=jnp.float32
        )


def project_low_rank(place, hidden, factor, gradient, up):
    half = jax.ShapeDtypeStruct((hidden.shape[0] // 2, 256), jnp.float32)
    return pl.pallas_call(
        project_low_rank_kernel,
        grid=(1,),
        out_shape=(half, half),
        in_specs=[smem()] + [full(*value.shape) for value in (hidden, factor, gradient, up)],
        out_specs=(full(*half.shape), full(*half.shape)),
        compiler_params=PARAMS,
        cost_estimate=LIGHT,
    )(place, hidden, factor, gradient, up)


def route_kernel(place, kept, other, chosen, gates, hidden, gradient, *refs):
    chunks, (routed, gate_gradient, parts) = refs[:NY], refs[NY:]
    zero = place[3] == 0
    both = jnp.concatenate(
        [jnp.where(zero, kept[...], other[...]), jnp.where(zero, other[...], kept[...])], axis=0
    )
    inner, outer = both[:, :128], both[:, 128:]
    expert = lax.broadcasted_iota(jnp.int32, inner.shape, 1) // RANK
    hits = [chosen[:, k : k + 1] == expert for k in range(2)]
    weight = jnp.where(hits[0], gates[:, 0:1], 0.0) + jnp.where(hits[1], gates[:, 1:2], 0.0)
    routed_outer = (SCALE * weight * outer).astype(jnp.bfloat16)
    routed_inner = (SCALE * weight * inner).astype(jnp.bfloat16)
    routed[...] = routed_outer
    product = inner * outer
    for k in range(2):
        picked = jnp.where(hits[k], product, 0.0)
        gate_gradient[:, k : k + 1] = SCALE * jnp.sum(picked, axis=1, keepdims=True)
    down = lax.dot_general(hidden[...], routed_outer, FIRST, preferred_element_type=jnp.float32)
    up = lax.dot_general(gradient[...], routed_inner, FIRST, preferred_element_type=jnp.float32)
    n = NZ * NY
    for whole_sum, first in ((down, 0), (up, down.shape[0] // n)):
        rows = whole_sum.shape[0] // n
        pieces = whole_sum.astype(jnp.bfloat16).reshape(NZ, NY, rows, 128)
        for y in range(NY):
            parts[y, :, pl.ds(first, rows), :] = pieces[:, y]
    for j, chunk in enumerate(chunks):
        chunk[...] = parts[lax.rem(place[1] + j, NY)]


def route(place, kept, other, chosen, gates, hidden, gradient):
    n = NZ * NY
    tokens = hidden.shape[0]
    rows = (hidden.shape[1] + gradient.shape[1]) // n
    outs = (
        *[jax.ShapeDtypeStruct((NZ, rows, 128), jnp.bfloat16)] * NY,
        jax.ShapeDtypeStruct((tokens, 128), jnp.bfloat16),
        jax.ShapeDtypeStruct((tokens, 2), jnp.float32),
    )
    return pl.pallas_call(
        route_kernel,
        grid=(1,),
        out_shape=outs,
        in_specs=[smem()]
        + [full(*value.shape) for value in (kept, other, chosen, gates, hidden, gradient)],
        out_specs=tuple(full(*out.shape) for out in outs),
        scratch_shapes=[pltpu.VMEM((NY, NZ, rows, 128), jnp.bfloat16)],
        compiler_params=PARAMS,
        cost_estimate=LIGHT,
    )(place, kept, other, chosen, gates, hidden, gradient)


def copied(*values):
    def kernel(*refs):
        for i in range(len(values)):
            refs[len(values) + i][...] = refs[i][...]

    specs = [full(*value.shape) for value in values]
    return pl.pallas_call(
        kernel,
        grid=(1,),
        out_shape=tuple(jax.ShapeDtypeStruct(value.shape, value.dtype) for value in values),
        in_specs=specs,
        out_specs=tuple(specs),
        compiler_params=PARAMS,
        cost_estimate=LIGHT,
    )(*values)


def arrange_kernel(place, *refs):
    out = refs[-1]
    x, c = place[2], place[3]
    sign = 1 - 2 * c
    width = out.shape[1] // 8
    for step in range(NX):
        for block, turn, core in ((refs[step], sign, c), (refs[NX + step], -sign, 1 - c)):
            owner = lax.rem(x - turn * step + 2 * NX, NX) * 2 + core
            out[:, pl.ds(pl.multiple_of(owner * width, width), width)] = block[...]


def arrange(place, blocks):
    tokens, width = blocks[0].shape
    return pl.pallas_call(
        arrange_kernel,
        grid=(1,),
        out_shape=jax.ShapeDtypeStruct((tokens, width * 8), jnp.bfloat16),
        in_specs=[smem()] + [full(*block.shape) for block in blocks],
        out_specs=full(tokens, width * 8),
        compiler_params=PARAMS,
        cost_estimate=LIGHT,
    )(place, *blocks)


A_TILES = ROWS_A // TILE


A_TILES = ROWS_A // TILE


def lanes_of(place, z, dy):
    owner = z * NY + lax.rem(place[1] - dy + NY, NY)
    return pl.ds(pl.multiple_of(owner * 128, 128), 128)


def own_kernel(place, left, routed, factor, own, out, sides, later, picked):
    @pl.when(pl.program_id(0) == 0)
    def _():
        for z in range(NZ):
            lanes = pl.ds(z * 128, 128)
            picked[:, lanes] = left[:, lanes_of(place, z, 0)]
            sides[:, lanes] = left[:, lanes_of(place, z, 1)]
            sides[:, pl.ds((NZ + z) * 128, 128)] = left[:, lanes_of(place, z, -1)]
            later[:, lanes] = left[:, lanes_of(place, z, 2)]

    right = jnp.concatenate([own[z] for z in range(NZ)], axis=1)
    total = lax.dot_general(picked[...], right, LAST, preferred_element_type=jnp.float32)
    total += lax.dot_general(routed[...], factor[...], LAST, preferred_element_type=jnp.float32)
    out[...] = total


def sides_kernel(picked, partial, plus, minus, out):
    right = jnp.concatenate([side[z] for side in (plus, minus) for z in range(NZ)], axis=1)
    total = lax.dot_general(picked[...], right, LAST, preferred_element_type=jnp.float32)
    out[...] = total + partial[...]


def last_rows_kernel(place, left, routed, factor, blocks, out, right):
    for z in range(NZ):
        for dy in range(NY):
            right[:, lanes_of(place, z, dy)] = blocks[z, dy]
    total = lax.dot_general(left[...], right[...], LAST, preferred_element_type=jnp.float32)
    total += lax.dot_general(routed[...], factor[...], LAST, preferred_element_type=jnp.float32)
    out[...] = total.astype(out.dtype)


def late_kernel(picked, partial, low, high, base, out):
    del base
    blocks = [low[z] for z in range(NZ // 2)] + [high[z] for z in range(NZ // 2)]
    right = jnp.concatenate(blocks, axis=1)
    total = lax.dot_general(picked[...], right, LAST, preferred_element_type=jnp.float32)
    out[...] = (total + partial[...]).astype(out.dtype)


def whole(shape):
    return pl.BlockSpec(shape, lambda n: (0,) * len(shape), pipeline_mode=pl.Buffered(1))


def project_own(place, left, routed, factor, own):
    tokens, depth = left.shape
    used = depth // NY
    return pl.pallas_call(
        own_kernel,
        grid=(A_TILES,),
        out_shape=(
            jax.ShapeDtypeStruct((tokens, ROWS_A), jnp.float32),
            jax.ShapeDtypeStruct((tokens, 2 * used), jnp.bfloat16),
            jax.ShapeDtypeStruct((tokens, used), jnp.bfloat16),
        ),
        in_specs=[smem(), whole((tokens, depth)), whole((tokens, 128))]
        + [pl.BlockSpec((TILE, 128), lambda n: (n, 0))]
        + [pl.BlockSpec((NZ, TILE, 128), lambda n: (0, n, 0))],
        out_specs=(
            pl.BlockSpec((tokens, TILE), lambda n: (0, n)),
            pl.BlockSpec((tokens, 2 * used), lambda n: (0, 0)),
            pl.BlockSpec((tokens, used), lambda n: (0, 0)),
        ),
        scratch_shapes=[pltpu.VMEM((tokens, used), jnp.bfloat16)],
        compiler_params=PARAMS,
        cost_estimate=LIGHT,
    )(place, left, routed, factor, own)


def project_sides(picked, partial, plus, minus):
    tokens, depth = picked.shape
    return pl.pallas_call(
        sides_kernel,
        grid=(A_TILES,),
        out_shape=jax.ShapeDtypeStruct(partial.shape, jnp.float32),
        in_specs=[whole((tokens, depth)), pl.BlockSpec((tokens, TILE), lambda n: (0, n))]
        + [pl.BlockSpec((NZ, TILE, 128), lambda n: (0, n, 0))] * 2,
        out_specs=pl.BlockSpec((tokens, TILE), lambda n: (0, n)),
        compiler_params=PARAMS,
        cost_estimate=LIGHT,
    )(picked, partial, plus, minus)


def project_last_rows(place, left, routed, factor, blocks):
    tokens, depth = left.shape
    units = factor.shape[0]
    return pl.pallas_call(
        last_rows_kernel,
        grid=(units // TILE - A_TILES,),
        out_shape=jax.ShapeDtypeStruct((tokens, units), jnp.bfloat16),
        in_specs=[smem(), whole((tokens, depth)), whole((tokens, 128))]
        + [
            pl.BlockSpec((TILE, 128), lambda n: (n + A_TILES, 0)),
            pl.BlockSpec((NZ, NY, TILE, 128), lambda n: (0, 0, n, 0)),
        ],
        out_specs=pl.BlockSpec((tokens, TILE), lambda n: (0, n + A_TILES)),
        scratch_shapes=[pltpu.VMEM((TILE, depth), jnp.bfloat16)],
        compiler_params=PARAMS,
        cost_estimate=LIGHT,
    )(place, left, routed, factor, blocks)


def project_late(picked, partial, low, high, base):
    tokens, depth = picked.shape
    return pl.pallas_call(
        late_kernel,
        grid=(A_TILES,),
        out_shape=jax.ShapeDtypeStruct(base.shape, jnp.bfloat16),
        in_specs=[whole((tokens, depth)), pl.BlockSpec((tokens, TILE), lambda n: (0, n))]
        + [pl.BlockSpec((NZ // 2, TILE, 128), lambda n: (0, n, 0))] * 2
        + [pl.BlockSpec(memory_space=pl.ANY)],
        out_specs=pl.BlockSpec((tokens, TILE), lambda n: (0, n)),
        input_output_aliases={4: 0},
        compiler_params=PARAMS,
        cost_estimate=LIGHT,
    )(picked, partial, low, high, base)


def per_device(
    hidden,
    layer_output_gradient,
    frozen_down_weight,
    adapter_down_weight,
    adapter_up_weight,
    chosen_expert_index,
    gates,
):
    together = lambda *values: lax.optimization_barrier(values)
    dp_index = lax.axis_index("dp").astype(jnp.int32)
    tensor_index = lax.axis_index("tensor").astype(jnp.int32)
    place = jnp.stack(
        [lax.div(dp_index, NY), lax.rem(dp_index, NY), lax.div(tensor_index, 2), lax.rem(tensor_index, 2)]
    )
    tokens_here = hidden.shape[0]
    token_scale = float(tokens_here * NZ * NY) ** (-0.5)
    n = NZ * NY

    own, last = frozen_down_weight[:ROWS_A], frozen_down_weight[ROWS_A:]
    row = lax.all_gather(own, "dp", axis=0, axis_index_groups=Z_GROUPS)
    kept, sent = project_low_rank(
        place, hidden, adapter_down_weight, layer_output_gradient, adapter_up_weight
    )
    last, kept, sent = together(last, kept, sent)
    b1, b2, b3 = move_y(last, 1), move_y(last, 2), move_y(last, -1)
    near = [layer_output_gradient, turn_x(layer_output_gradient)]
    kept = kept + swap_core(sent)
    kept = kept + swap_x(kept, lambda x: x ^ 1)
    chosen, weights = copied(chosen_expert_index, gates)
    kept, chosen, weights = together(kept, chosen, weights)
    kept = kept + swap_x(kept, lambda x: 3 - x)
    b1, b2, b3, kept, near[1] = together(b1, b2, b3, kept, near[1])
    column = jnp.stack([last, b1, b2, b3])
    b_blocks = lax.all_gather(column, "dp", axis=0, axis_index_groups=Z_GROUPS)

    other = swap_core(kept)
    *chunks, routed, gate_gradient = route(
        place, kept, other, chosen, weights, hidden, layer_output_gradient
    )
    near.append(turn_x(near[-1]))

    came = [move_y(chunks[j], j) for j in range(1, NY)]
    parts = sum(chunk.astype(jnp.float32) for chunk in [chunks[0]] + came).astype(jnp.bfloat16)
    row, parts, near[2] = together(row, parts, near[2])
    plus, minus = move_y(row, 1), move_y(row, -1)
    parts = lax.all_to_all(parts, "dp", 0, 0, tiled=True, axis_index_groups=Z_GROUPS)
    total = jnp.sum(parts.astype(jnp.float32), axis=0) * token_scale
    down_rows = hidden.shape[1] // n
    down = jnp.broadcast_to(total[:down_rows].astype(jnp.bfloat16)[None], (NZ, down_rows, 128))
    down = lax.all_to_all(down, "dp", 0, 0, tiled=True, axis_index_groups=Z_GROUPS)
    near.append(turn_x(near[-1]))
    left = arrange(place, near + [swap_core(block) for block in near])
    partial, side_left, late_left = project_own(place, left, routed, adapter_down_weight, row)
    came = [down] + [move_y(down, j) for j in range(1, NY)]
    plus, minus, partial, side_left, late_left, *came = together(
        plus, minus, partial, side_left, late_left, *came
    )

    half = NZ // 2
    low, high = move_y(plus[:half], 1), move_y(minus[half:], -1)
    partial = project_sides(side_left, partial, plus, minus)
    pairs = [(d * 8 + t, (4 * t + d // 8) * 8 + d % 8) for d in range(n) for t in range(8)]
    up_factor_gradient = lax.ppermute(total[down_rows:], ("dp", "tensor"), pairs).T
    came = jnp.stack([came[(3 - i) % NY] for i in range(2 * NY - 1)])
    came = lax.dynamic_slice_in_dim(came, 3 - place[1], NY, axis=0)
    down_factor_gradient = came.transpose(1, 0, 2, 3).reshape(-1, 128).astype(jnp.float32)

    hidden_input_gradient = project_last_rows(place, left, routed, adapter_down_weight, b_blocks)
    hidden_input_gradient, low, high, partial, down_factor_gradient, up_factor_gradient = together(
        hidden_input_gradient, low, high, partial, down_factor_gradient, up_factor_gradient
    )
    hidden_input_gradient = project_late(late_left, partial, low, high, hidden_input_gradient)
    return (hidden_input_gradient, down_factor_gradient, up_factor_gradient, gate_gradient)


def solution(mesh):
    return jax.shard_map(
        per_device,
        mesh=mesh,
        in_specs=(
            P("dp", "tensor"),
            P("dp", "tensor"),
            P("tensor", "dp"),
            P("tensor", None),
            P(),
            P("dp", None),
            P("dp", None),
        ),
        out_specs=(P("dp", "tensor"), P("tensor", None), P(None, ("dp", "tensor")), P("dp", None)),
        check_vma=False,
    )
```

time: 661 us -> 178 us (0.27)
  waiting for transfers between devices: 602 us -> 50 us
  Pallas kernels: 0 us -> 53 us
  starting transfers between devices: 0.21 us -> 38.9 us
  matrix products: 32.3 us -> 0 us
  local copies, waits for them, and re-layouts: 7.64 us -> 14.3 us
    psum x2 -> x0, waiting for transfers between devices: 213 us -> none  [the longest x1 150 us: per_device(): lax.psum(per_expert_down_gradient, 'dp') * token_scale]
    reduce_scatter x1 -> x0, waiting for transfers between devices: 208 us -> none  [per_device(): lax.psum_scatter(per_expert_up_gradient, 'dp', scatter_dimension=1, tiled...]
    all_gather x2, waiting for transfers between devices: 181 us -> 0.01 us  [the longest x1 0.01 us: per_device(): row = lax.all_gather(own, 'dp', axis=0, axis_index_groups=Z_GROUPS)]
    pallas_call x0 -> x8, Pallas kernels: none -> 53 us  [the longest x1 10.7 us: project_last_rows(): pl.pallas_call(last_rows_kernel, grid=(units // TILE - A_TILES,), out_sha...]
    dot_general x6 -> x0, matrix products: 32.3 us -> none  [the longest x1 19.4 us: per_device(): lax.dot_general(full_output_gradient, lax.all_gather(frozen_down_weight,...]
    ppermute x0 -> x25, waiting for transfers between devices: none -> 30.4 us  [the longest x13 15 us: move_y(): return lax.ppermute(value, 'dp', pairs)]
    ppermute x0 -> x25, starting transfers between devices: none -> 27.1 us  [the longest x13 16.1 us: move_y(): return lax.ppermute(value, 'dp', pairs)]
    all_to_all x0 -> x2, waiting for transfers between devices: none -> 19.6 us  [the longest x1 10 us: per_device(): lax.all_to_all(down, 'dp', 0, 0, tiled=True, axis_index_groups=Z_GROUPS)]
  transfers between devices with their start and end apart: 5 -> 29, of which waited for: 5 -> 14; matrix products, arithmetic and copies ran while one was open for 2% -> 10% of each run, Pallas kernels for 0% -> 27%
where the time goes in v2:
time: 178 us; the launch traced here: 176 us
  Pallas kernels  53 us (30%)
  waiting for transfers between devices  50 us (28%)
  starting transfers between devices  38.9 us (22%)
  local copies, waits for them, and re-layouts  14.3 us (8%)
  between operations  14.3 us (8%)
  other arithmetic  5.68 us (3%)
    ppermute x13, starting transfers between devices, move_y(): return lax.ppermute(value, 'dp', pairs)  16.1 us
    ppermute x13, waiting for transfers between devices, move_y(): return lax.ppermute(value, 'dp', pairs)  15 us
    ppermute x2, waiting for transfers between devices, swap_x(): lax.ppermute(value, 'tensor', [(x * 2 + c, partner(x) * 2 + c) for x in r...  10.9 us
    pallas_call x1, Pallas kernels, project_last_rows(): pl.pallas_call(last_rows_kernel, grid=(units // TILE - A_TILES,), out_sha...  10.7 us
    pallas_call x1, Pallas kernels, project_own(): pl.pallas_call(own_kernel, grid=(A_TILES,), out_shape=(jax.ShapeDtypeStru...  10.4 us
    all_to_all x1, waiting for transfers between devices, per_device(): lax.all_to_all(down, 'dp', 0, 0, tiled=True, axis_index_groups=Z_GROUPS)  10 us
    all_to_all x1, waiting for transfers between devices, per_device(): lax.all_to_all(parts, 'dp', 0, 0, tiled=True, axis_index_groups=Z_GROUPS)  9.54 us
    all_to_all x1, starting transfers between devices, per_device(): lax.all_to_all(parts, 'dp', 0, 0, tiled=True, axis_index_groups=Z_GROUPS)  8.42 us
  transfers between devices with their start and end apart: 29, of which 14 were waited for; matrix products, arithmetic and copies ran while one was open for 10% of the time, Pallas kernels for 27%

profile of v2, /device:TPU:4, one launch (start us, length us, event | category | flops | bytes accessed | tf_op | source)
XLA Modules:
  0.0 176.3 jit_solution(7399914567207366907)
XLA Ops:
  7.2 1.7 slice.19
  10.6 4.3 %shard_map.102 = (f32[384,256]{1,0:T(8,128)}, f32[384,256]{1,0:T(8,128)}) custom-call(s32[4]{0:T(128)} %pad_add_fusion.place, bf16[768,1792]{1,0:T(8,128)(2,1)} %hidden.3, bf16[1792,128]{1,0:T(8,128)(2,1)} %factor.5, bf16[768,512]{1,0:T(8,128)(2,1)} %refs_0_.2, bf16[128,4096]{1,0:T(8,128)(2,1)} %up.1), custom_call_target="tpu_custom_call" | custom-call | tf_op jit(solution)/shard_map/pallas_call | solution.py:66
  14.9 1.9 %collective-permute-done.3 = f32[384,256]{1,0:T(8,128)S(1)} collective-permute-done((f32[384,256]{1,0:T(8,128)}, f32[384,256]{1,0:T(8,128)S(1)}, u32[]{:S(2)}, u32[]{:S(2)}) %collective-permute-start.3) | collective-permute-done | bytes 393248 | tf_op jit(solution)/shard_map/ppermute | solution.py:35
  21.9 2.1 %shard_map.103 = (s32[768,2]{1,0:T(8,128)}, f32[768,2]{1,0:T(8,128)}) custom-call(s32[768,2]{1,0:T(8,128)} %copy.20.refs_0_, f32[768,2]{1,0:T(8,128)} %copy.21.refs_1_), custom_call_target="tpu_custom_call" | custom-call | tf_op jit(solution)/shard_map/pallas_call | solution.py:134
  24.0 6.0 %collective-permute-done.4 = f32[384,256]{1,0:T(8,128)S(1)} collective-permute-done((f32[384,256]{1,0:T(8,128)S(1)}, f32[384,256]{1,0:T(8,128)S(1)}, u32[]{:S(2)}, u32[]{:S(2)}) %collective-permute-start.4) | collective-permute-done | bytes 393248 | tf_op jit(solution)/shard_map/ppermute | solution.py:31
  30.4 2.8 %collective-permute-start.2 = (bf16[768,128]{1,0:T(8,128)(2,1)S(1)}, bf16[768,128]{1,0:T(8,128)(2,1)S(1)}, u32[]{:S(2)}, u32[]{:S(2)}) collective-permute-start(bf16[768,128]{1,0:T(8,128)(2,1)S(1)} %slice.20), channel_id=1, source_target_pairs={{0,24},{8,0},{16,8},{24,16},{32,56},{40,32},{48,40},{56,48},{64,88... | collective-permute-start | bytes 589832 | tf_op jit(solution)/shard_map/ppermute | solution.py:22
  34.8 4.9 %collective-permute-done.5 = f32[384,256]{1,0:T(8,128)S(1)} collective-permute-done((f32[384,256]{1,0:T(8,128)S(1)}, f32[384,256]{1,0:T(8,128)S(1)}, u32[]{:S(2)}, u32[]{:S(2)}) %collective-permute-start.5) | collective-permute-done | bytes 393248 | tf_op jit(solution)/shard_map/ppermute | solution.py:31
  40.6 1.6 collective-permute-done.1
  42.2 2.0 %collective-permute-done = bf16[768,128]{1,0:T(8,128)(2,1)S(1)} collective-permute-done((bf16[768,128]{1,0:T(8,128)(2,1)S(1)}, bf16[768,128]{1,0:T(8,128)(2,1)S(1)}, u32[]{:S(2)}, u32[]{:S(2)}) %collective-permute-start) | collective-permute-done | bytes 196640 | tf_op jit(solution)/shard_map/ppermute | solution.py:22
  46.7 1.7 collective-permute-done.7.other
  49.1 5.2 %shard_map.104 = (bf16[8,72,128]{2,1,0:T(8,128)(2,1)}, bf16[8,72,128]{2,1,0:T(8,128)(2,1)}, bf16[8,72,128]{2,1,0:T(8,128)(2,1)}, bf16[8,72,128]{2,1,0:T(8,128)(2...) custom-call(s32[4]{0:T(128)} %pad_add_fusion.place, f32[384,256]{1,0:T(8,128)} %copy-done.3, f32[384,256]{1,0:T(8,128)} %copy-done.8, ...), custom_call_target="tpu_custom_call" | custom-call | tf_op jit(solution)/shard_map/pallas_call | solution.py:115
  54.3 2.1 %collective-permute-start.9 = (bf16[8,72,128]{2,1,0:T(8,128)(2,1)}, bf16[8,72,128]{2,1,0:T(8,128)(2,1)S(1)}, u32[]{:S(2)}, u32[]{:S(2)}) collective-permute-start(bf16[8,72,128]{2,1,0:T(8,128)(2,1)} %get-tuple-element.59), channel_id=1, source_target_pairs={{0,16},{8,24},{16,0},{24,8},{32,48},{40,56},{48,32},{56,40},{64,80... | collective-permute-start | bytes 442376 | tf_op jit(solution)/shard_map/ppermute | solution.py:22
  57.6 7.2 %collective-permute-done.8 = bf16[8,72,128]{2,1,0:T(8,128)(2,1)S(1)} collective-permute-done((bf16[8,72,128]{2,1,0:T(8,128)(2,1)}, bf16[8,72,128]{2,1,0:T(8,128)(2,1)S(1)}, u32[]{:S(2)}, u32[]{:S(2)}) %collective-permute-start.8) | collective-permute-done | bytes 147488 | tf_op jit(solution)/shard_map/ppermute | solution.py:22
  65.4 1.7 add_convert_fusion
  67.0 2.3 %collective-permute-start.13 = (bf16[8,1024,128]{2,1,0:T(8,128)(2,1)}, bf16[8,1024,128]{2,1,0:T(8,128)(2,1)S(1)}, u32[]{:S(2)}, u32[]{:S(2)}) collective-permute-start(bf16[8,1024,128]{2,1,0:T(8,128)(2,1)} %bitcast.32), channel_id=1, source_target_pairs={{0,24},{8,0},{16,8},{24,16},{32,56},{40,32},{48,40},{56,48},{64,88... | collective-permute-start | bytes 6291464 | tf_op jit(solution)/shard_map/ppermute | solution.py:22
  69.4 2.8 %collective-permute-start.14 = (bf16[768,512]{1,0:T(8,128)(2,1)}, bf16[768,512]{1,0:T(8,128)(2,1)}, u32[]{:S(2)}, u32[]{:S(2)}) collective-permute-start(bf16[768,512]{1,0:T(8,128)(2,1)} %collective-permute-done.11.refs_2_), channel_id=1, source_target_pairs={{0,2},{1,7},{2,4},{3,1},{4,6},{5,3},{6,0},{7,5},{8,10},{9,15},{10,... | collective-permute-start | bytes 2359304 | tf_op jit(solution)/shard_map/ppermute | solution.py:27
  72.2 8.4 %all-to-all-start = ((bf16[8,72,128]{2,1,0:T(8,128)(2,1)}), bf16[8,72,128]{2,1,0:T(8,128)(2,1)S(1)}, u32[]{:S(2)}, u32[]{:S(2)}) async-start(bf16[8,72,128]{2,1,0:T(8,128)(2,1)} %add_convert_fusion), calls=%async_computation | async-start | bytes 294912 | tf_op jit(solution)/shard_map/all_to_all | solution.py:343
  82.3 9.5 %all-to-all-done = bf16[8,72,128]{2,1,0:T(8,128)(2,1)S(1)} async-done(((bf16[8,72,128]{2,1,0:T(8,128)(2,1)}), bf16[8,72,128]{2,1,0:T(8,128)(2,1)S(1)}, u32[]{:S(2)}, u32[]{:S(2)}) %all-to-all-start) | async-done | bytes 147488 | tf_op jit(solution)/shard_map/all_to_all | solution.py:343
  92.6 3.4 %all-to-all-start.1 = ((bf16[8,56,128]{2,1,0:T(8,128)(2,1)}), bf16[8,56,128]{2,1,0:T(8,128)(2,1)S(1)}, u32[]{:S(2)}, u32[]{:S(2)}) async-start(bf16[8,56,128]{2,1,0:T(8,128)(2,1)} %broadcast_in_dim.2), calls=%async_computation.1 | async-start | bytes 229376 | tf_op jit(solution)/shard_map/all_to_all | solution.py:347
  96.0 10.0 %all-to-all-done.1 = bf16[8,56,128]{2,1,0:T(8,128)(2,1)S(1)} async-done(((bf16[8,56,128]{2,1,0:T(8,128)(2,1)}), bf16[8,56,128]{2,1,0:T(8,128)(2,1)S(1)}, u32[]{:S(2)}, u32[]{:S(2)}) %all-to-all-start.1) | async-done | bytes 114720 | tf_op jit(solution)/shard_map/all_to_all | solution.py:347
  106.0 3.2 %collective-permute-start.21 = (bf16[8,56,128]{2,1,0:T(8,128)(2,1)S(1)}, bf16[8,56,128]{2,1,0:T(8,128)(2,1)S(1)}, u32[]{:S(2)}, u32[]{:S(2)}) collective-permute-start(bf16[8,56,128]{2,1,0:T(8,128)(2,1)S(1)} %all-to-all-done.1), channel_id=1, source_target_pairs={{0,24},{8,0},{16,8},{24,16},{32,56},{40,32},{48,40},{56,48},{64,88... | collective-permute-start | bytes 344072 | tf_op jit(solution)/shard_map/ppermute | solution.py:22
  110.1 1.7 copy.27
  111.9 6.0 %shard_map.105.left = bf16[768,4096]{1,0:T(8,128)(2,1)} custom-call(s32[4]{0:T(128)} %pad_add_fusion.place, bf16[768,512]{1,0:T(8,128)(2,1)} %refs_0_.2, bf16[768,512]{1,0:T(8,128)(2,1)} %copy-done.5, bf16[768,512]{1,0:T(8,128)(2,1)} %collective-permute-done.11.refs_2_, bf16[768,512]{1,0:T(8,128)(2,1)} %collective-permute-done.14.refs_3_, ...), custom_call_target="tpu_custom_call" | custom-call | tf_op jit(solution)/shard_map/pallas_call | solution.py:158
  117.9 10.4 %shard_map.106 = (f32[768,1024]{1,0:T(8,128)}, bf16[768,2048]{1,0:T(8,128)(2,1)}, bf16[768,1024]{1,0:T(8,128)(2,1)}) custom-call(s32[4]{0:T(128)} %pad_add_fusion.place, bf16[768,4096]{1,0:T(8,128)(2,1)} %shard_map.105.left, bf16[768,128]{1,0:T(8,128)(2,1)} %get-tuple-element.64.routed, bf16[1792,128]{1,0:T(8,128)(2,1)} %factor.5, bf16[8,1024,128]{2,1,0:T(8,128)(2,1)} %bitcast.34), custom_call_target="tpu_custom_call" | custom-call | tf_op jit(solution)/shard_map/pallas_call | solution.py:226
  128.3 3.6 %collective-permute-start.24 = (f32[16,128]{1,0:T(8,128)S(1)}, f32[16,128]{1,0:T(8,128)S(1)}, u32[]{:S(2)}, u32[]{:S(2)}) collective-permute-start(f32[16,128]{1,0:T(8,128)S(1)} %slice.26), channel_id=1, source_target_pairs={{0,0},{1,32},{2,64},{3,96},{4,128},{5,160},{6,192},{7,224},{8,1},{... | collective-permute-start | bytes 24584 | tf_op jit(solution)/shard_map/ppermute | solution.py:360
  132.0 3.0 %slice.22 = bf16[4,1024,128]{2,1,0:T(8,128)(2,1)} slice(bf16[8,1024,128]{2,1,0:T(8,128)(2,1)} %collective-permute-done.12.plus), slice={[0:4], [0:1024], [0:128]} | slice | bytes 2097152 | tf_op jit(solution)/shard_map/slice | solution.py:357
  136.8 1.3 collective-permute-start.22
  141.1 8.3 %shard_map.108.partial = f32[768,1024]{1,0:T(8,128)} custom-call(bf16[768,2048]{1,0:T(8,128)(2,1)} %get-tuple-element.75.picked, f32[768,1024]{1,0:T(8,128)} %get-tuple-element.76.partial, bf16[8,1024,128]{2,1,0:T(8,128)(2,1)} %collective-permute-done.12.plus, bf16[8,1024,128]{2,1,0:T(8,128)(2,1)} %copy-done.2), custom_call_target="tpu_custom_call" | custom-call | tf_op jit(solution)/shard_map/pallas_call | solution.py:250
  149.4 10.7 %shard_map.107.base = bf16[768,1792]{1,0:T(8,128)(2,1)} custom-call(s32[4]{0:T(128)} %pad_add_fusion.place, bf16[768,4096]{1,0:T(8,128)(2,1)} %shard_map.105.left, bf16[768,128]{1,0:T(8,128)(2,1)} %get-tuple-element.64.routed, bf16[1792,128]{1,0:T(8,128)(2,1)} %factor.5, bf16[8,4,768,128]{3,2,1,0:T(8,128)(2,1)} %bitcast.31), custom_call_target="tpu_custom_call" | custom-call | tf_op jit(solution)/shard_map/pallas_call | solution.py:265
  160.2 1.4 collective-permute-done.23.high
  161.6 1.3 collective-permute-done.22.low
  162.9 6.0 %shard_map.109 = bf16[768,1792]{1,0:T(8,128)(2,1)} custom-call(bf16[768,1024]{1,0:T(8,128)(2,1)} %get-tuple-element.69.picked, f32[768,1024]{1,0:T(8,128)} %shard_map.108.partial, bf16[4,1024,128]{2,1,0:T(8,128)(2,1)} %collective-permute-done.22.low, bf16[4,1024,128]{2,1,0:T(8,128)(2,1)} %copy-done.4, ...), custom_call_target="tpu_custom_call", output_to_operand_aliasing={{}: (4, {})} | custom-call | tf_op jit(solution)/shard_map/pallas_call | solution.py:283
  (85 shorter events, 23.3 us)
Async XLA Ops:
  7.2 59.9 %all-gather.5.cloned.1.call-start = ((), (), s32[]{:S(2)}) async-start(), calls=%async_computation.2 | async-start | bytes 2359296 | tf_op jit(solution)/shard_map/all_gather | solution.py:317
  8.9 140.5 %all-gather.7.cloned.1.call-start = ((), (), s32[]{:S(2)}) async-start(), calls=%async_computation.3 | async-start | bytes 7077888 | tf_op jit(solution)/shard_map/all_gather | solution.py:331
  10.6 10.4 %copy-start.10 = (f32[768,2]{0,1:T(2,128)S(1)}, f32[768,2]{0,1:T(2,128)}, u32[]{:S(2)}) copy-start(f32[768,2]{0,1:T(2,128)} %param.13) | copy-start | bytes 18436
  14.9 1.9 %collective-permute-start.3 = (f32[384,256]{1,0:T(8,128)}, f32[384,256]{1,0:T(8,128)S(1)}, u32[]{:S(2)}, u32[]{:S(2)}) collective-permute-start(f32[384,256]{1,0:T(8,128)} %get-tuple-element.50), channel_id=1, source_target_pairs={{0,1},{1,0},{2,3},{3,2},{4,5},{5,4},{6,7},{7,6},{8,9},{9,8},{10,11... | collective-permute-start | bytes 1179656 | tf_op jit(solution)/shard_map/ppermute | solution.py:35
  17.9 12.0 %collective-permute-start.4 = (f32[384,256]{1,0:T(8,128)S(1)}, f32[384,256]{1,0:T(8,128)S(1)}, u32[]{:S(2)}, u32[]{:S(2)}) collective-permute-start(f32[384,256]{1,0:T(8,128)S(1)} %add.22), channel_id=1, source_target_pairs={{0,2},{1,3},{2,0},{3,1},{4,6},{5,7},{6,4},{7,5},{8,10},{9,11},{10,... | collective-permute-start | bytes 1179656 | tf_op jit(solution)/shard_map/ppermute | solution.py:31
  19.2 25.0 %collective-permute-start.6 = (bf16[768,512]{1,0:T(8,128)(2,1)S(1)}, bf16[768,512]{1,0:T(8,128)(2,1)S(1)}, u32[]{:S(2)}, u32[]{:S(2)}) collective-permute-start(bf16[768,512]{1,0:T(8,128)(2,1)S(1)} %copy-done), channel_id=1, source_target_pairs={{0,2},{1,7},{2,4},{3,1},{4,6},{5,3},{6,0},{7,5},{8,10},{9,15},{10,... | collective-permute-start | bytes 2359304 | tf_op jit(solution)/shard_map/ppermute | solution.py:27
  30.0 9.7 %collective-permute-start.5 = (f32[384,256]{1,0:T(8,128)S(1)}, f32[384,256]{1,0:T(8,128)S(1)}, u32[]{:S(2)}, u32[]{:S(2)}) collective-permute-start(f32[384,256]{1,0:T(8,128)S(1)} %add.23), channel_id=1, source_target_pairs={{0,6},{1,7},{2,4},{3,5},{4,2},{5,3},{6,0},{7,1},{8,14},{9,15},{10,... | collective-permute-start | bytes 1179656 | tf_op jit(solution)/shard_map/ppermute | solution.py:31
  30.4 10.1 %collective-permute-start.2 = (bf16[768,128]{1,0:T(8,128)(2,1)S(1)}, bf16[768,128]{1,0:T(8,128)(2,1)S(1)}, u32[]{:S(2)}, u32[]{:S(2)}) collective-permute-start(bf16[768,128]{1,0:T(8,128)(2,1)S(1)} %slice.20), channel_id=1, source_target_pairs={{0,24},{8,0},{16,8},{24,16},{32,56},{40,32},{48,40},{56,48},{64,88... | collective-permute-start | bytes 589832 | tf_op jit(solution)/shard_map/ppermute | solution.py:22
  33.2 9.0 %collective-permute-start.1 = (bf16[768,128]{1,0:T(8,128)(2,1)S(1)}, bf16[768,128]{1,0:T(8,128)(2,1)S(1)}, u32[]{:S(2)}, u32[]{:S(2)}) collective-permute-start(bf16[768,128]{1,0:T(8,128)(2,1)S(1)} %slice.20), channel_id=1, source_target_pairs={{0,16},{8,24},{16,0},{24,8},{32,48},{40,56},{48,32},{56,40},{64,80... | collective-permute-start | bytes 589832 | tf_op jit(solution)/shard_map/ppermute | solution.py:22
  33.8 10.4 %collective-permute-start = (bf16[768,128]{1,0:T(8,128)(2,1)S(1)}, bf16[768,128]{1,0:T(8,128)(2,1)S(1)}, u32[]{:S(2)}, u32[]{:S(2)}) collective-permute-start(bf16[768,128]{1,0:T(8,128)(2,1)S(1)} %slice.20), channel_id=1, source_target_pairs={{0,8},{8,16},{16,24},{24,0},{32,40},{40,48},{48,56},{56,32},{64,72... | collective-permute-start | bytes 589832 | tf_op jit(solution)/shard_map/ppermute | solution.py:22
  44.2 10.1 %copy-start.5 = (bf16[768,512]{1,0:T(8,128)(2,1)}, bf16[768,512]{1,0:T(8,128)(2,1)S(1)}, u32[]{:S(2)}) copy-start(bf16[768,512]{1,0:T(8,128)(2,1)S(1)} %collective-permute-done.6.refs_1_) | copy-start | bytes 2359300
  45.4 24.0 %copy-start.1 = (bf16[768,512]{1,0:T(8,128)(2,1)S(1)}, bf16[768,512]{1,0:T(8,128)(2,1)}, u32[]{:S(2)}) copy-start(bf16[768,512]{1,0:T(8,128)(2,1)} %refs_0_.2) | copy-start | bytes 2359300
  45.4 21.6 %collective-permute-start.11 = (bf16[768,512]{1,0:T(8,128)(2,1)S(1)}, bf16[768,512]{1,0:T(8,128)(2,1)}, u32[]{:S(2)}, u32[]{:S(2)}) collective-permute-start(bf16[768,512]{1,0:T(8,128)(2,1)S(1)} %collective-permute-done.6.refs_1_), channel_id=1, source_target_pairs={{0,2},{1,7},{2,4},{3,1},{4,6},{5,3},{6,0},{7,5},{8,10},{9,15},{10,... | collective-permute-start | bytes 2359304 | tf_op jit(solution)/shard_map/ppermute | solution.py:27
  46.7 1.7 collective-permute-start.7
  54.3 10.4 %collective-permute-start.8 = (bf16[8,72,128]{2,1,0:T(8,128)(2,1)}, bf16[8,72,128]{2,1,0:T(8,128)(2,1)S(1)}, u32[]{:S(2)}, u32[]{:S(2)}) collective-permute-start(bf16[8,72,128]{2,1,0:T(8,128)(2,1)} %get-tuple-element.58), channel_id=1, source_target_pairs={{0,8},{8,16},{16,24},{24,0},{32,40},{40,48},{48,56},{56,32},{64,72... | collective-permute-start | bytes 442376 | tf_op jit(solution)/shard_map/ppermute | solution.py:22
  54.3 10.4 %collective-permute-start.9 = (bf16[8,72,128]{2,1,0:T(8,128)(2,1)}, bf16[8,72,128]{2,1,0:T(8,128)(2,1)S(1)}, u32[]{:S(2)}, u32[]{:S(2)}) collective-permute-start(bf16[8,72,128]{2,1,0:T(8,128)(2,1)} %get-tuple-element.59), channel_id=1, source_target_pairs={{0,16},{8,24},{16,0},{24,8},{32,48},{40,56},{48,32},{56,40},{64,80... | collective-permute-start | bytes 442376 | tf_op jit(solution)/shard_map/ppermute | solution.py:22
  56.4 9.0 %collective-permute-start.10 = (bf16[8,72,128]{2,1,0:T(8,128)(2,1)}, bf16[8,72,128]{2,1,0:T(8,128)(2,1)S(1)}, u32[]{:S(2)}, u32[]{:S(2)}) collective-permute-start(bf16[8,72,128]{2,1,0:T(8,128)(2,1)} %get-tuple-element.60), channel_id=1, source_target_pairs={{0,24},{8,0},{16,8},{24,16},{32,56},{40,32},{48,40},{56,48},{64,88... | collective-permute-start | bytes 442376 | tf_op jit(solution)/shard_map/ppermute | solution.py:22
  67.0 64.9 %collective-permute-start.13 = (bf16[8,1024,128]{2,1,0:T(8,128)(2,1)}, bf16[8,1024,128]{2,1,0:T(8,128)(2,1)S(1)}, u32[]{:S(2)}, u32[]{:S(2)}) collective-permute-start(bf16[8,1024,128]{2,1,0:T(8,128)(2,1)} %bitcast.32), channel_id=1, source_target_pairs={{0,24},{8,0},{16,8},{24,16},{32,56},{40,32},{48,40},{56,48},{64,88... | collective-permute-start | bytes 6291464 | tf_op jit(solution)/shard_map/ppermute | solution.py:22
  69.4 62.6 %collective-permute-start.12 = (bf16[8,1024,128]{2,1,0:T(8,128)(2,1)}, bf16[8,1024,128]{2,1,0:T(8,128)(2,1)}, u32[]{:S(2)}, u32[]{:S(2)}) collective-permute-start(bf16[8,1024,128]{2,1,0:T(8,128)(2,1)} %bitcast.33), channel_id=1, source_target_pairs={{0,8},{8,16},{16,24},{24,0},{32,40},{40,48},{48,56},{56,32},{64,72... | collective-permute-start | bytes 6291464 | tf_op jit(solution)/shard_map/ppermute | solution.py:22
  69.4 11.3 %collective-permute-start.15 = (bf16[768,512]{1,0:T(8,128)(2,1)S(1)}, bf16[768,512]{1,0:T(8,128)(2,1)}, u32[]{:S(2)}, u32[]{:S(2)}) collective-permute-start(bf16[768,512]{1,0:T(8,128)(2,1)S(1)} %copy-done.1), channel_id=1, source_target_pairs={{0,1},{1,0},{2,3},{3,2},{4,5},{5,4},{6,7},{7,6},{8,9},{9,8},{10,11... | collective-permute-start | bytes 2359304 | tf_op jit(solution)/shard_map/ppermute | solution.py:35
  69.4 12.6 %collective-permute-start.14 = (bf16[768,512]{1,0:T(8,128)(2,1)}, bf16[768,512]{1,0:T(8,128)(2,1)}, u32[]{:S(2)}, u32[]{:S(2)}) collective-permute-start(bf16[768,512]{1,0:T(8,128)(2,1)} %collective-permute-done.11.refs_2_), channel_id=1, source_target_pairs={{0,2},{1,7},{2,4},{3,1},{4,6},{5,3},{6,0},{7,5},{8,10},{9,15},{10,... | collective-permute-start | bytes 2359304 | tf_op jit(solution)/shard_map/ppermute | solution.py:27
  72.2 19.7 %all-to-all-start = ((bf16[8,72,128]{2,1,0:T(8,128)(2,1)}), bf16[8,72,128]{2,1,0:T(8,128)(2,1)S(1)}, u32[]{:S(2)}, u32[]{:S(2)}) async-start(bf16[8,72,128]{2,1,0:T(8,128)(2,1)} %add_convert_fusion), calls=%async_computation | async-start | bytes 294912 | tf_op jit(solution)/shard_map/all_to_all | solution.py:343
  80.6 15.3 %collective-permute-start.16 = (bf16[768,512]{1,0:T(8,128)(2,1)}, bf16[768,512]{1,0:T(8,128)(2,1)}, u32[]{:S(2)}, u32[]{:S(2)}) collective-permute-start(bf16[768,512]{1,0:T(8,128)(2,1)} %copy-done.5), channel_id=1, source_target_pairs={{0,1},{1,0},{2,3},{3,2},{4,5},{5,4},{6,7},{7,6},{8,9},{9,8},{10,11... | collective-permute-start | bytes 2359304 | tf_op jit(solution)/shard_map/ppermute | solution.py:35
  80.7 28.5 %collective-permute-start.17 = (bf16[768,512]{1,0:T(8,128)(2,1)}, bf16[768,512]{1,0:T(8,128)(2,1)S(1)}, u32[]{:S(2)}, u32[]{:S(2)}) collective-permute-start(bf16[768,512]{1,0:T(8,128)(2,1)} %collective-permute-done.11.refs_2_), channel_id=1, source_target_pairs={{0,1},{1,0},{2,3},{3,2},{4,5},{5,4},{6,7},{7,6},{8,9},{9,8},{10,11... | collective-permute-start | bytes 2359304 | tf_op jit(solution)/shard_map/ppermute | solution.py:35
  82.0 27.2 %collective-permute-start.18 = (bf16[768,512]{1,0:T(8,128)(2,1)}, bf16[768,512]{1,0:T(8,128)(2,1)}, u32[]{:S(2)}, u32[]{:S(2)}) collective-permute-start(bf16[768,512]{1,0:T(8,128)(2,1)} %collective-permute-done.14.refs_3_), channel_id=1, source_target_pairs={{0,1},{1,0},{2,3},{3,2},{4,5},{5,4},{6,7},{7,6},{8,9},{9,8},{10,11... | collective-permute-start | bytes 2359304 | tf_op jit(solution)/shard_map/ppermute | solution.py:35
  92.6 13.4 %all-to-all-start.1 = ((bf16[8,56,128]{2,1,0:T(8,128)(2,1)}), bf16[8,56,128]{2,1,0:T(8,128)(2,1)S(1)}, u32[]{:S(2)}, u32[]{:S(2)}) async-start(bf16[8,56,128]{2,1,0:T(8,128)(2,1)} %broadcast_in_dim.2), calls=%async_computation.1 | async-start | bytes 229376 | tf_op jit(solution)/shard_map/all_to_all | solution.py:347
  106.0 22.3 %collective-permute-start.21 = (bf16[8,56,128]{2,1,0:T(8,128)(2,1)S(1)}, bf16[8,56,128]{2,1,0:T(8,128)(2,1)S(1)}, u32[]{:S(2)}, u32[]{:S(2)}) collective-permute-start(bf16[8,56,128]{2,1,0:T(8,128)(2,1)S(1)} %all-to-all-done.1), channel_id=1, source_target_pairs={{0,24},{8,0},{16,8},{24,16},{32,56},{40,32},{48,40},{56,48},{64,88... | collective-permute-start | bytes 344072 | tf_op jit(solution)/shard_map/ppermute | solution.py:22
  109.2 22.7 %collective-permute-start.20 = (bf16[8,56,128]{2,1,0:T(8,128)(2,1)S(1)}, bf16[8,56,128]{2,1,0:T(8,128)(2,1)S(1)}, u32[]{:S(2)}, u32[]{:S(2)}) collective-permute-start(bf16[8,56,128]{2,1,0:T(8,128)(2,1)S(1)} %all-to-all-done.1), channel_id=1, source_target_pairs={{0,16},{8,24},{16,0},{24,8},{32,48},{40,56},{48,32},{56,40},{64,80... | collective-permute-start | bytes 344072 | tf_op jit(solution)/shard_map/ppermute | solution.py:22
  109.2 22.7 %collective-permute-start.19 = (bf16[8,56,128]{2,1,0:T(8,128)(2,1)S(1)}, bf16[8,56,128]{2,1,0:T(8,128)(2,1)S(1)}, u32[]{:S(2)}, u32[]{:S(2)}) collective-permute-start(bf16[8,56,128]{2,1,0:T(8,128)(2,1)S(1)} %all-to-all-done.1), channel_id=1, source_target_pairs={{0,8},{8,16},{16,24},{24,0},{32,40},{40,48},{48,56},{56,32},{64,72... | collective-permute-start | bytes 344072 | tf_op jit(solution)/shard_map/ppermute | solution.py:22
  128.3 31.8 %collective-permute-start.24 = (f32[16,128]{1,0:T(8,128)S(1)}, f32[16,128]{1,0:T(8,128)S(1)}, u32[]{:S(2)}, u32[]{:S(2)}) collective-permute-start(f32[16,128]{1,0:T(8,128)S(1)} %slice.26), channel_id=1, source_target_pairs={{0,0},{1,32},{2,64},{3,96},{4,128},{5,160},{6,192},{7,224},{8,1},{... | collective-permute-start | bytes 24584 | tf_op jit(solution)/shard_map/ppermute | solution.py:360
  136.1 25.5 %collective-permute-start.23 = (bf16[4,1024,128]{2,1,0:T(8,128)(2,1)}, bf16[4,1024,128]{2,1,0:T(8,128)(2,1)S(1)}, u32[]{:S(2)}, u32[]{:S(2)}) collective-permute-start(bf16[4,1024,128]{2,1,0:T(8,128)(2,1)} %slice.23), channel_id=1, source_target_pairs={{0,24},{8,0},{16,8},{24,16},{32,56},{40,32},{48,40},{56,48},{64,88... | collective-permute-start | bytes 3145736 | tf_op jit(solution)/shard_map/ppermute | solution.py:22
  136.8 26.1 %collective-permute-start.22 = (bf16[4,1024,128]{2,1,0:T(8,128)(2,1)}, bf16[4,1024,128]{2,1,0:T(8,128)(2,1)}, u32[]{:S(2)}, u32[]{:S(2)}) collective-permute-start(bf16[4,1024,128]{2,1,0:T(8,128)(2,1)} %slice.22), channel_id=1, source_target_pairs={{0,8},{8,16},{16,24},{24,0},{32,40},{40,48},{48,56},{56,32},{64,72... | collective-permute-start | bytes 3145736 | tf_op jit(solution)/shard_map/ppermute | solution.py:22
  (8 other events, 41.7 us)
Sparse Core Ops, SparseCore 0:
  9.8 44.2 all-gather.4
  55.9 78.3 all-gather.6

commit v3 on v2

--- a/solution.py
+++ b/solution.py
@@ -177,26 +177,23 @@
     return pl.ds(pl.multiple_of(owner * 128, 128), 128)
 
 
-def own_kernel(place, left, routed, factor, own, out, sides, later, picked):
+def early_kernel(place, left, routed, factor, own, p0, p1, m0, m1, out, later, right, picked):
+    half = NZ // 2
+
     @pl.when(pl.program_id(0) == 0)
     def _():
         for z in range(NZ):
-            lanes = pl.ds(z * 128, 128)
-            picked[:, lanes] = left[:, lanes_of(place, z, 0)]
-            sides[:, lanes] = left[:, lanes_of(place, z, 1)]
-            sides[:, pl.ds((NZ + z) * 128, 128)] = left[:, lanes_of(place, z, -1)]
-            later[:, lanes] = left[:, lanes_of(place, z, 2)]
-
-    right = jnp.concatenate([own[z] for z in range(NZ)], axis=1)
-    total = lax.dot_general(picked[...], right, LAST, preferred_element_type=jnp.float32)
+            for s, dy in enumerate((0, 1, -1)):
+                picked[:, pl.ds((s * NZ + z) * 128, 128)] = left[:, lanes_of(place, z, dy)]
+            later[:, pl.ds(z * 128, 128)] = left[:, lanes_of(place, z, 2)]
+
+    for s, pair in enumerate(((own, own), (p0, p1), (m0, m1))):
+        for z in range(NZ):
+            ref, i = pair[z // half], z if s == 0 else z % half
+            right[:, pl.ds((s * NZ + z) * 128, 128)] = ref[i]
+    total = lax.dot_general(picked[...], right[...], LAST, preferred_element_type=jnp.float32)
     total += lax.dot_general(routed[...], factor[...], LAST, preferred_element_type=jnp.float32)
     out[...] = total
-
-
-def sides_kernel(picked, partial, plus, minus, out):
-    right = jnp.concatenate([side[z] for side in (plus, minus) for z in range(NZ)], axis=1)
-    total = lax.dot_general(picked[...], right, LAST, preferred_element_type=jnp.float32)
-    out[...] = total + partial[...]
 
 
 def last_rows_kernel(place, left, routed, factor, blocks, out, right):
@@ -220,43 +217,28 @@
     return pl.BlockSpec(shape, lambda n: (0,) * len(shape), pipeline_mode=pl.Buffered(1))
 
 
-def project_own(place, left, routed, factor, own):
+def project_early(place, left, routed, factor, own, *sides):
     tokens, depth = left.shape
-    used = depth // NY
-    return pl.pallas_call(
-        own_kernel,
+    used = 3 * depth // NY
+    return pl.pallas_call(
+        early_kernel,
         grid=(A_TILES,),
         out_shape=(
             jax.ShapeDtypeStruct((tokens, ROWS_A), jnp.float32),
-            jax.ShapeDtypeStruct((tokens, 2 * used), jnp.bfloat16),
-            jax.ShapeDtypeStruct((tokens, used), jnp.bfloat16),
+            jax.ShapeDtypeStruct((tokens, depth - used), jnp.bfloat16),
         ),
         in_specs=[smem(), whole((tokens, depth)), whole((tokens, 128))]
         + [pl.BlockSpec((TILE, 128), lambda n: (n, 0))]
-        + [pl.BlockSpec((NZ, TILE, 128), lambda n: (0, n, 0))],
+        + [pl.BlockSpec((NZ, TILE, 128), lambda n: (0, n, 0))]
+        + [pl.BlockSpec((NZ // 2, TILE, 128), lambda n: (0, n, 0))] * 4,
         out_specs=(
             pl.BlockSpec((tokens, TILE), lambda n: (0, n)),
-            pl.BlockSpec((tokens, 2 * used), lambda n: (0, 0)),
-            pl.BlockSpec((tokens, used), lambda n: (0, 0)),
+            pl.BlockSpec((tokens, depth - used), lambda n: (0, 0)),
         ),
-        scratch_shapes=[pltpu.VMEM((tokens, used), jnp.bfloat16)],
-        compiler_params=PARAMS,
-        cost_estimate=LIGHT,
-    )(place, left, routed, factor, own)
-
-
-def project_sides(picked, partial, plus, minus):
-    tokens, depth = picked.shape
-    return pl.pallas_call(
-        sides_kernel,
-        grid=(A_TILES,),
-        out_shape=jax.ShapeDtypeStruct(partial.shape, jnp.float32),
-        in_specs=[whole((tokens, depth)), pl.BlockSpec((tokens, TILE), lambda n: (0, n))]
-        + [pl.BlockSpec((NZ, TILE, 128), lambda n: (0, n, 0))] * 2,
-        out_specs=pl.BlockSpec((tokens, TILE), lambda n: (0, n)),
-        compiler_params=PARAMS,
-        cost_estimate=LIGHT,
-    )(picked, partial, plus, minus)
+        scratch_shapes=[pltpu.VMEM((TILE, used), jnp.bfloat16), pltpu.VMEM((tokens, used), jnp.bfloat16)],
+        compiler_params=PARAMS,
+        cost_estimate=LIGHT,
+    )(place, left, routed, factor, own, *sides)
 
 
 def project_last_rows(place, left, routed, factor, blocks):
@@ -337,36 +319,35 @@
     near.append(turn_x(near[-1]))
 
     came = [move_y(chunks[j], j) for j in range(1, NY)]
-    parts = sum(chunk.astype(jnp.float32) for chunk in [chunks[0]] + came).astype(jnp.bfloat16)
+    parts = sum(chunk.astype(jnp.float32) for chunk in [chunks[0]] + came)
+    half = NZ // 2
     row, parts, near[2] = together(row, parts, near[2])
-    plus, minus = move_y(row, 1), move_y(row, -1)
+    halves = row[:half], row[half:]
+    plus, minus = [move_y(piece, 1) for piece in halves], [move_y(piece, -1) for piece in halves]
     parts = lax.all_to_all(parts, "dp", 0, 0, tiled=True, axis_index_groups=Z_GROUPS)
-    total = jnp.sum(parts.astype(jnp.float32), axis=0) * token_scale
+    total = jnp.sum(parts, axis=0) * token_scale
+    near.append(turn_x(near[-1]))
+    plus[0], minus[1], total, near[3] = together(plus[0], minus[1], total, near[3])
+
+    low, high = move_y(plus[0], 1), move_y(minus[1], -1)
     down_rows = hidden.shape[1] // n
     down = jnp.broadcast_to(total[:down_rows].astype(jnp.bfloat16)[None], (NZ, down_rows, 128))
     down = lax.all_to_all(down, "dp", 0, 0, tiled=True, axis_index_groups=Z_GROUPS)
-    near.append(turn_x(near[-1]))
     left = arrange(place, near + [swap_core(block) for block in near])
-    partial, side_left, late_left = project_own(place, left, routed, adapter_down_weight, row)
+    plus[1], minus[0], down, total, left = together(plus[1], minus[0], down, total, left)
+
+    partial, late_left = project_early(place, left, routed, adapter_down_weight, row, *plus, *minus)
     came = [down] + [move_y(down, j) for j in range(1, NY)]
-    plus, minus, partial, side_left, late_left, *came = together(
-        plus, minus, partial, side_left, late_left, *came
-    )
-
-    half = NZ // 2
-    low, high = move_y(plus[:half], 1), move_y(minus[half:], -1)
-    partial = project_sides(side_left, partial, plus, minus)
     pairs = [(d * 8 + t, (4 * t + d // 8) * 8 + d % 8) for d in range(n) for t in range(8)]
     up_factor_gradient = lax.ppermute(total[down_rows:], ("dp", "tensor"), pairs).T
+    hidden_input_gradient = project_last_rows(place, left, routed, adapter_down_weight, b_blocks)
+    hidden_input_gradient, low, high, partial, up_factor_gradient, *came = together(
+        hidden_input_gradient, low, high, partial, up_factor_gradient, *came
+    )
+    hidden_input_gradient = project_late(late_left, partial, low, high, hidden_input_gradient)
     came = jnp.stack([came[(3 - i) % NY] for i in range(2 * NY - 1)])
     came = lax.dynamic_slice_in_dim(came, 3 - place[1], NY, axis=0)
     down_factor_gradient = came.transpose(1, 0, 2, 3).reshape(-1, 128).astype(jnp.float32)
-
-    hidden_input_gradient = project_last_rows(place, left, routed, adapter_down_weight, b_blocks)
-    hidden_input_gradient, low, high, partial, down_factor_gradient, up_factor_gradient = together(
-        hidden_input_gradient, low, high, partial, down_factor_gradient, up_factor_gradient
-    )
-    hidden_input_gradient = project_late(late_left, partial, low, high, hidden_input_gradient)
     return (hidden_input_gradient, down_factor_gradient, up_factor_gradient, gate_gradient)
 
 

time: 178 us -> 191 us (1.073)
  the two profiles are of different devices: /device:TPU:4 before, /device:TPU:1 now
where the time goes in v3:
time: 191 us
  waiting for transfers between devices  58.3 us (31%)
  starting transfers between devices  52.3 us (27%)
  Pallas kernels  46.8 us (25%)
  between operations  14.3 us (7%)
  local copies, waits for them, and re-layouts  13.4 us (7%)
  other arithmetic  5.62 us (3%)
    ppermute x15, starting transfers between devices, move_y(): return lax.ppermute(value, 'dp', pairs)  19.6 us
    ppermute x15, waiting for transfers between devices, move_y(): return lax.ppermute(value, 'dp', pairs)  17.1 us
    ppermute x1, waiting for transfers between devices, per_device(): lax.ppermute(total[down_rows:], ('dp', 'tensor'), pairs)  15.2 us
    all_to_all x1, waiting for transfers between devices, per_device(): lax.all_to_all(parts, 'dp', 0, 0, tiled=True, axis_index_groups=Z_GROUPS)  14.8 us
    pallas_call x1, Pallas kernels, project_early(): pl.pallas_call(early_kernel, grid=(A_TILES,), out_shape=(jax.ShapeDtypeSt...  12.6 us
    pallas_call x1, Pallas kernels, project_last_rows(): pl.pallas_call(last_rows_kernel, grid=(units // TILE - A_TILES,), out_sha...  10.7 us
    ppermute x6, starting transfers between devices, swap_core(): return lax.ppermute(value, 'tensor', [(i, i ^ 1) for i in range(2 * NX)])  9.61 us
    ppermute x2, waiting for transfers between devices, swap_x(): lax.ppermute(value, 'tensor', [(x * 2 + c, partner(x) * 2 + c) for x in r...  9.54 us
  transfers between devices with their start and end apart: 31, of which 9 were waited for; matrix products, arithmetic and copies ran while one was open for 7% of the time, Pallas kernels for 21%

profile of v3, /device:TPU:1, one launch (start us, length us, event | category | flops | bytes accessed | tf_op | source)
XLA Modules:
  0.0 190.8 jit_solution(3604894091388897329)
XLA Ops:
  7.2 1.7 slice.19
  10.5 4.3 %shard_map.102 = (f32[384,256]{1,0:T(8,128)}, f32[384,256]{1,0:T(8,128)}) custom-call(s32[4]{0:T(128)} %pad_add_fusion.place, bf16[768,1792]{1,0:T(8,128)(2,1)} %hidden.3, bf16[1792,128]{1,0:T(8,128)(2,1)} %factor.5, bf16[768,512]{1,0:T(8,128)(2,1)} %refs_0_.2, bf16[128,4096]{1,0:T(8,128)(2,1)} %up.1), custom_call_target="tpu_custom_call" | custom-call | tf_op jit(solution)/shard_map/pallas_call | solution.py:66
  14.9 3.2 %collective-permute-start.3 = (f32[384,256]{1,0:T(8,128)}, f32[384,256]{1,0:T(8,128)S(1)}, u32[]{:S(2)}, u32[]{:S(2)}) collective-permute-start(f32[384,256]{1,0:T(8,128)} %get-tuple-element.52), channel_id=1, source_target_pairs={{0,1},{1,0},{2,3},{3,2},{4,5},{5,4},{6,7},{7,6},{8,9},{9,8},{10,11... | collective-permute-start | bytes 1179656 | tf_op jit(solution)/shard_map/ppermute | solution.py:35
  18.1 1.6 collective-permute-done.3
  24.0 2.0 %shard_map.103 = (s32[768,2]{1,0:T(8,128)}, f32[768,2]{1,0:T(8,128)}) custom-call(s32[768,2]{1,0:T(8,128)} %copy.20.refs_0_, f32[768,2]{1,0:T(8,128)} %copy.21.refs_1_), custom_call_target="tpu_custom_call" | custom-call | tf_op jit(solution)/shard_map/pallas_call | solution.py:134
  26.0 5.2 %collective-permute-done.4 = f32[384,256]{1,0:T(8,128)S(1)} collective-permute-done((f32[384,256]{1,0:T(8,128)S(1)}, f32[384,256]{1,0:T(8,128)S(1)}, u32[]{:S(2)}, u32[]{:S(2)}) %collective-permute-start.4) | collective-permute-done | bytes 393248 | tf_op jit(solution)/shard_map/ppermute | solution.py:31
  33.4 2.6 %collective-permute-start.1 = (bf16[768,128]{1,0:T(8,128)(2,1)S(1)}, bf16[768,128]{1,0:T(8,128)(2,1)S(1)}, u32[]{:S(2)}, u32[]{:S(2)}) collective-permute-start(bf16[768,128]{1,0:T(8,128)(2,1)S(1)} %slice.20), channel_id=1, source_target_pairs={{0,16},{8,24},{16,0},{24,8},{32,48},{40,56},{48,32},{56,40},{64,80... | collective-permute-start | bytes 589832 | tf_op jit(solution)/shard_map/ppermute | solution.py:22
  37.1 4.3 %collective-permute-done.5 = f32[384,256]{1,0:T(8,128)S(1)} collective-permute-done((f32[384,256]{1,0:T(8,128)S(1)}, f32[384,256]{1,0:T(8,128)S(1)}, u32[]{:S(2)}, u32[]{:S(2)}) %collective-permute-start.5) | collective-permute-done | bytes 393248 | tf_op jit(solution)/shard_map/ppermute | solution.py:31
  41.5 2.3 %collective-permute-done.1 = bf16[768,128]{1,0:T(8,128)(2,1)S(1)} collective-permute-done((bf16[768,128]{1,0:T(8,128)(2,1)S(1)}, bf16[768,128]{1,0:T(8,128)(2,1)S(1)}, u32[]{:S(2)}, u32[]{:S(2)}) %collective-permute-start.1) | collective-permute-done | bytes 196640 | tf_op jit(solution)/shard_map/ppermute | solution.py:22
  45.0 2.4 %collective-permute-start.7 = (f32[384,256]{1,0:T(8,128)S(1)}, f32[384,256]{1,0:T(8,128)S(1)}, u32[]{:S(2)}, u32[]{:S(2)}) collective-permute-start(f32[384,256]{1,0:T(8,128)S(1)} %add.24.kept), channel_id=1, source_target_pairs={{0,1},{1,0},{2,3},{3,2},{4,5},{5,4},{6,7},{7,6},{8,9},{9,8},{10,11... | collective-permute-start | bytes 1179656 | tf_op jit(solution)/shard_map/ppermute | solution.py:35
  49.5 5.1 %shard_map.104 = (bf16[8,72,128]{2,1,0:T(8,128)(2,1)}, bf16[8,72,128]{2,1,0:T(8,128)(2,1)}, bf16[8,72,128]{2,1,0:T(8,128)(2,1)}, bf16[8,72,128]{2,1,0:T(8,128)(2...) custom-call(s32[4]{0:T(128)} %pad_add_fusion.place, f32[384,256]{1,0:T(8,128)} %copy-done.2, f32[384,256]{1,0:T(8,128)} %copy-done.7, ...), custom_call_target="tpu_custom_call" | custom-call | tf_op jit(solution)/shard_map/pallas_call | solution.py:115
  54.6 2.3 %collective-permute-start.10 = (bf16[8,72,128]{2,1,0:T(8,128)(2,1)}, bf16[8,72,128]{2,1,0:T(8,128)(2,1)S(1)}, u32[]{:S(2)}, u32[]{:S(2)}) collective-permute-start(bf16[8,72,128]{2,1,0:T(8,128)(2,1)} %get-tuple-element.62), channel_id=1, source_target_pairs={{0,24},{8,0},{16,8},{24,16},{32,56},{40,32},{48,40},{56,48},{64,88... | collective-permute-start | bytes 442376 | tf_op jit(solution)/shard_map/ppermute | solution.py:22
  58.4 2.2 %collective-permute-done.10 = bf16[8,72,128]{2,1,0:T(8,128)(2,1)S(1)} collective-permute-done((bf16[8,72,128]{2,1,0:T(8,128)(2,1)}, bf16[8,72,128]{2,1,0:T(8,128)(2,1)S(1)}, u32[]{:S(2)}, u32[]{:S(2)}) %collective-permute-start.10) | collective-permute-done | bytes 147488 | tf_op jit(solution)/shard_map/ppermute | solution.py:22
  60.6 6.2 %collective-permute-done.8 = bf16[8,72,128]{2,1,0:T(8,128)(2,1)S(1)} collective-permute-done((bf16[8,72,128]{2,1,0:T(8,128)(2,1)}, bf16[8,72,128]{2,1,0:T(8,128)(2,1)S(1)}, u32[]{:S(2)}, u32[]{:S(2)}) %collective-permute-start.8) | collective-permute-done | bytes 147488 | tf_op jit(solution)/shard_map/ppermute | solution.py:22
  66.9 1.7 convert_add_fusion
  69.7 3.0 %fusion = (bf16[4,1024,128]{2,1,0:T(8,128)(2,1)}, bf16[4,1024,128]{2,1,0:T(8,128)(2,1)}) fusion(bf16[8,1024,128]{2,1,0:T(8,128)(2,1)} %bitcast.31), kind=kLoop, calls=%fused_computation.13 | loop fusion | bytes 4194304 | tf_op jit(solution)/shard_map/slice | solution.py:325
  72.7 2.7 %collective-permute-start.15 = (bf16[4,1024,128]{2,1,0:T(8,128)(2,1)}, bf16[4,1024,128]{2,1,0:T(8,128)(2,1)S(1)}, u32[]{:S(2)}, u32[]{:S(2)}) collective-permute-start(bf16[4,1024,128]{2,1,0:T(8,128)(2,1)} %get-tuple-element.101), channel_id=1, source_target_pairs={{0,24},{8,0},{16,8},{24,16},{32,56},{40,32},{48,40},{56,48},{64,88... | collective-permute-start | bytes 3145736 | tf_op jit(solution)/shard_map/ppermute | solution.py:22
  75.9 8.0 %all-to-all-start = ((f32[8,72,128]{2,1,0:T(8,128)}), f32[8,72,128]{2,1,0:T(8,128)S(1)}, u32[]{:S(2)}, u32[]{:S(2)}) async-start(f32[8,72,128]{2,1,0:T(8,128)} %convert_add_fusion), calls=%async_computation | async-start | bytes 589824 | tf_op jit(solution)/shard_map/all_to_all | solution.py:327
  84.8 14.8 %all-to-all-done = f32[8,72,128]{2,1,0:T(8,128)S(1)} async-done(((f32[8,72,128]{2,1,0:T(8,128)}), f32[8,72,128]{2,1,0:T(8,128)S(1)}, u32[]{:S(2)}, u32[]{:S(2)}) %all-to-all-start) | async-done | bytes 294944 | tf_op jit(solution)/shard_map/all_to_all | solution.py:327
  99.8 2.6 %collective-permute-start.13 = (bf16[4,1024,128]{2,1,0:T(8,128)(2,1)}, bf16[4,1024,128]{2,1,0:T(8,128)(2,1)}, u32[]{:S(2)}, u32[]{:S(2)}) collective-permute-start(bf16[4,1024,128]{2,1,0:T(8,128)(2,1)} %get-tuple-element.100), channel_id=1, source_target_pairs={{0,24},{8,0},{16,8},{24,16},{32,56},{40,32},{48,40},{56,48},{64,88... | collective-permute-start | bytes 3145736 | tf_op jit(solution)/shard_map/ppermute | solution.py:22
  102.5 2.7 %collective-permute-start.22 = (bf16[4,1024,128]{2,1,0:T(8,128)(2,1)S(1)}, bf16[4,1024,128]{2,1,0:T(8,128)(2,1)}, u32[]{:S(2)}, u32[]{:S(2)}) collective-permute-start(bf16[4,1024,128]{2,1,0:T(8,128)(2,1)S(1)} %collective-permute-done.15.m1), channel_id=1, source_target_pairs={{0,24},{8,0},{16,8},{24,16},{32,56},{40,32},{48,40},{56,48},{64,88... | collective-permute-start | bytes 3145736 | tf_op jit(solution)/shard_map/ppermute | solution.py:22
  105.2 2.6 %collective-permute-start.20 = (bf16[768,512]{1,0:T(8,128)(2,1)}, bf16[768,512]{1,0:T(8,128)(2,1)}, u32[]{:S(2)}, u32[]{:S(2)}) collective-permute-start(bf16[768,512]{1,0:T(8,128)(2,1)} %collective-permute-done.16.refs_3_), channel_id=1, source_target_pairs={{0,1},{1,0},{2,3},{3,2},{4,5},{5,4},{6,7},{7,6},{8,9},{9,8},{10,11... | collective-permute-start | bytes 2359304 | tf_op jit(solution)/shard_map/ppermute | solution.py:35
  108.5 3.7 %all-to-all-start.1 = ((bf16[8,56,128]{2,1,0:T(8,128)(2,1)}), bf16[8,56,128]{2,1,0:T(8,128)(2,1)S(1)}, u32[]{:S(2)}, u32[]{:S(2)}) async-start(bf16[8,56,128]{2,1,0:T(8,128)(2,1)} %broadcast_in_dim.2), calls=%async_computation.1 | async-start | bytes 229376 | tf_op jit(solution)/shard_map/all_to_all | solution.py:335
  112.2 6.0 %shard_map.105.left = bf16[768,4096]{1,0:T(8,128)(2,1)} custom-call(s32[4]{0:T(128)} %pad_add_fusion.place, bf16[768,512]{1,0:T(8,128)(2,1)} %refs_0_.2, bf16[768,512]{1,0:T(8,128)(2,1)} %copy-done.6, bf16[768,512]{1,0:T(8,128)(2,1)} %collective-permute-done.11.refs_2_, bf16[768,512]{1,0:T(8,128)(2,1)} %collective-permute-done.16.refs_3_, ...), custom_call_target="tpu_custom_call" | custom-call | tf_op jit(solution)/shard_map/pallas_call | solution.py:158
  118.1 6.3 %collective-permute-done.12.p1 = bf16[4,1024,128]{2,1,0:T(8,128)(2,1)} collective-permute-done((bf16[4,1024,128]{2,1,0:T(8,128)(2,1)}, bf16[4,1024,128]{2,1,0:T(8,128)(2,1)}, u32[]{:S(2)}, u32[]{:S(2)}) %collective-permute-start.12) | collective-permute-done | bytes 1048608 | tf_op jit(solution)/shard_map/ppermute | solution.py:22
  124.4 6.8 %collective-permute-start.23 = (f32[16,128]{1,0:T(8,128)S(1)}, f32[16,128]{1,0:T(8,128)S(1)}, u32[]{:S(2)}, u32[]{:S(2)}) collective-permute-start(f32[16,128]{1,0:T(8,128)S(1)} %slice.24), channel_id=1, source_target_pairs={{0,0},{1,32},{2,64},{3,96},{4,128},{5,160},{6,192},{7,224},{8,1},{... | collective-permute-start | bytes 24584 | tf_op jit(solution)/shard_map/ppermute | solution.py:342
  131.3 2.6 %collective-permute-start.25 = (bf16[8,56,128]{2,1,0:T(8,128)(2,1)S(1)}, bf16[8,56,128]{2,1,0:T(8,128)(2,1)S(1)}, u32[]{:S(2)}, u32[]{:S(2)}) collective-permute-start(bf16[8,56,128]{2,1,0:T(8,128)(2,1)S(1)} %all-to-all-done.1), channel_id=1, source_target_pairs={{0,16},{8,24},{16,0},{24,8},{32,48},{40,56},{48,32},{56,40},{64,80... | collective-permute-start | bytes 344072 | tf_op jit(solution)/shard_map/ppermute | solution.py:22
  133.9 15.2 %collective-permute-done.23 = f32[16,128]{1,0:T(8,128)S(1)} collective-permute-done((f32[16,128]{1,0:T(8,128)S(1)}, f32[16,128]{1,0:T(8,128)S(1)}, u32[]{:S(2)}, u32[]{:S(2)}) %collective-permute-start.23) | collective-permute-done | bytes 8224 | tf_op jit(solution)/shard_map/ppermute | solution.py:342
  149.1 1.7 copy.27
  150.9 12.6 %shard_map.106 = (f32[768,1024]{1,0:T(8,128)}, bf16[768,1024]{1,0:T(8,128)(2,1)}) custom-call(s32[4]{0:T(128)} %pad_add_fusion.place, bf16[768,4096]{1,0:T(8,128)(2,1)} %shard_map.105.left, bf16[768,128]{1,0:T(8,128)(2,1)} %get-tuple-element.70.routed, bf16[1792,128]{1,0:T(8,128)(2,1)} %factor.5, bf16[8,1024,128]{2,1,0:T(8,128)(2,1)} %bitcast.32, ...), custom_call_target="tpu_custom_call" | custom-call | tf_op jit(solution)/shard_map/pallas_call | solution.py:223
  163.5 10.7 %shard_map.107.base = bf16[768,1792]{1,0:T(8,128)(2,1)} custom-call(s32[4]{0:T(128)} %pad_add_fusion.place, bf16[768,4096]{1,0:T(8,128)(2,1)} %shard_map.105.left, bf16[768,128]{1,0:T(8,128)(2,1)} %get-tuple-element.70.routed, bf16[1792,128]{1,0:T(8,128)(2,1)} %factor.5, bf16[8,4,768,128]{3,2,1,0:T(8,128)(2,1)} %bitcast.33), custom_call_target="tpu_custom_call" | custom-call | tf_op jit(solution)/shard_map/pallas_call | solution.py:247
  177.4 6.0 %shard_map.108 = bf16[768,1792]{1,0:T(8,128)(2,1)} custom-call(bf16[768,1024]{1,0:T(8,128)(2,1)} %get-tuple-element.75.picked, f32[768,1024]{1,0:T(8,128)} %get-tuple-element.82.partial, bf16[4,1024,128]{2,1,0:T(8,128)(2,1)} %copy-done.5, bf16[4,1024,128]{2,1,0:T(8,128)(2,1)} %collective-permute-done.22.high, ...), custom_call_target="tpu_custom_call", output_to_operand_aliasing={{}: (4, {})} | custom-call | tf_op jit(solution)/shard_map/pallas_call | solution.py:265
  (85 shorter events, 21.2 us)
Async XLA Ops:
  7.2 61.4 %all-gather.5.cloned.1.call-start = ((), (), s32[]{:S(2)}) async-start(), calls=%async_computation.2 | async-start | bytes 2359296 | tf_op jit(solution)/shard_map/all_gather | solution.py:299
  8.9 154.6 %all-gather.7.cloned.1.call-start = ((), (), s32[]{:S(2)}) async-start(), calls=%async_computation.3 | async-start | bytes 7077888 | tf_op jit(solution)/shard_map/all_gather | solution.py:313
  14.9 4.8 %collective-permute-start.3 = (f32[384,256]{1,0:T(8,128)}, f32[384,256]{1,0:T(8,128)S(1)}, u32[]{:S(2)}, u32[]{:S(2)}) collective-permute-start(f32[384,256]{1,0:T(8,128)} %get-tuple-element.52), channel_id=1, source_target_pairs={{0,1},{1,0},{2,3},{3,2},{4,5},{5,4},{6,7},{7,6},{8,9},{9,8},{10,11... | collective-permute-start | bytes 1179656 | tf_op jit(solution)/shard_map/ppermute | solution.py:35
  20.7 10.5 %collective-permute-start.4 = (f32[384,256]{1,0:T(8,128)S(1)}, f32[384,256]{1,0:T(8,128)S(1)}, u32[]{:S(2)}, u32[]{:S(2)}) collective-permute-start(f32[384,256]{1,0:T(8,128)S(1)} %add.22), channel_id=1, source_target_pairs={{0,2},{1,3},{2,0},{3,1},{4,6},{5,7},{6,4},{7,5},{8,10},{9,11},{10,... | collective-permute-start | bytes 1179656 | tf_op jit(solution)/shard_map/ppermute | solution.py:31
  20.8 23.0 %collective-permute-start.6 = (bf16[768,512]{1,0:T(8,128)(2,1)S(1)}, bf16[768,512]{1,0:T(8,128)(2,1)S(1)}, u32[]{:S(2)}, u32[]{:S(2)}) collective-permute-start(bf16[768,512]{1,0:T(8,128)(2,1)S(1)} %copy-done), channel_id=1, source_target_pairs={{0,2},{1,7},{2,4},{3,1},{4,6},{5,3},{6,0},{7,5},{8,10},{9,15},{10,... | collective-permute-start | bytes 2359304 | tf_op jit(solution)/shard_map/ppermute | solution.py:27
  31.3 10.1 %collective-permute-start.5 = (f32[384,256]{1,0:T(8,128)S(1)}, f32[384,256]{1,0:T(8,128)S(1)}, u32[]{:S(2)}, u32[]{:S(2)}) collective-permute-start(f32[384,256]{1,0:T(8,128)S(1)} %add.23), channel_id=1, source_target_pairs={{0,6},{1,7},{2,4},{3,5},{4,2},{5,3},{6,0},{7,1},{8,14},{9,15},{10,... | collective-permute-start | bytes 1179656 | tf_op jit(solution)/shard_map/ppermute | solution.py:31
  32.1 9.4 %collective-permute-start = (bf16[768,128]{1,0:T(8,128)(2,1)S(1)}, bf16[768,128]{1,0:T(8,128)(2,1)S(1)}, u32[]{:S(2)}, u32[]{:S(2)}) collective-permute-start(bf16[768,128]{1,0:T(8,128)(2,1)S(1)} %slice.20), channel_id=1, source_target_pairs={{0,8},{8,16},{16,24},{24,0},{32,40},{40,48},{48,56},{56,32},{64,72... | collective-permute-start | bytes 589832 | tf_op jit(solution)/shard_map/ppermute | solution.py:22
  33.4 10.4 %collective-permute-start.1 = (bf16[768,128]{1,0:T(8,128)(2,1)S(1)}, bf16[768,128]{1,0:T(8,128)(2,1)S(1)}, u32[]{:S(2)}, u32[]{:S(2)}) collective-permute-start(bf16[768,128]{1,0:T(8,128)(2,1)S(1)} %slice.20), channel_id=1, source_target_pairs={{0,16},{8,24},{16,0},{24,8},{32,48},{40,56},{48,32},{56,40},{64,80... | collective-permute-start | bytes 589832 | tf_op jit(solution)/shard_map/ppermute | solution.py:22
  36.1 7.8 %collective-permute-start.2 = (bf16[768,128]{1,0:T(8,128)(2,1)S(1)}, bf16[768,128]{1,0:T(8,128)(2,1)S(1)}, u32[]{:S(2)}, u32[]{:S(2)}) collective-permute-start(bf16[768,128]{1,0:T(8,128)(2,1)S(1)} %slice.20), channel_id=1, source_target_pairs={{0,24},{8,0},{16,8},{24,16},{32,56},{40,32},{48,40},{56,48},{64,88... | collective-permute-start | bytes 589832 | tf_op jit(solution)/shard_map/ppermute | solution.py:22
  43.8 28.9 %copy-start.6 = (bf16[768,512]{1,0:T(8,128)(2,1)}, bf16[768,512]{1,0:T(8,128)(2,1)S(1)}, u32[]{:S(2)}) copy-start(bf16[768,512]{1,0:T(8,128)(2,1)S(1)} %collective-permute-done.6.refs_1_) | copy-start | bytes 2359300
  45.0 3.7 %collective-permute-start.7 = (f32[384,256]{1,0:T(8,128)S(1)}, f32[384,256]{1,0:T(8,128)S(1)}, u32[]{:S(2)}, u32[]{:S(2)}) collective-permute-start(f32[384,256]{1,0:T(8,128)S(1)} %add.24.kept), channel_id=1, source_target_pairs={{0,1},{1,0},{2,3},{3,2},{4,5},{5,4},{6,7},{7,6},{8,9},{9,8},{10,11... | collective-permute-start | bytes 1179656 | tf_op jit(solution)/shard_map/ppermute | solution.py:35
  47.4 21.2 %collective-permute-start.11 = (bf16[768,512]{1,0:T(8,128)(2,1)S(1)}, bf16[768,512]{1,0:T(8,128)(2,1)}, u32[]{:S(2)}, u32[]{:S(2)}) collective-permute-start(bf16[768,512]{1,0:T(8,128)(2,1)S(1)} %collective-permute-done.6.refs_1_), channel_id=1, source_target_pairs={{0,2},{1,7},{2,4},{3,1},{4,6},{5,3},{6,0},{7,5},{8,10},{9,15},{10,... | collective-permute-start | bytes 2359304 | tf_op jit(solution)/shard_map/ppermute | solution.py:27
  54.6 6.0 %collective-permute-start.10 = (bf16[8,72,128]{2,1,0:T(8,128)(2,1)}, bf16[8,72,128]{2,1,0:T(8,128)(2,1)S(1)}, u32[]{:S(2)}, u32[]{:S(2)}) collective-permute-start(bf16[8,72,128]{2,1,0:T(8,128)(2,1)} %get-tuple-element.62), channel_id=1, source_target_pairs={{0,24},{8,0},{16,8},{24,16},{32,56},{40,32},{48,40},{56,48},{64,88... | collective-permute-start | bytes 442376 | tf_op jit(solution)/shard_map/ppermute | solution.py:22
  57.0 9.9 %collective-permute-start.8 = (bf16[8,72,128]{2,1,0:T(8,128)(2,1)}, bf16[8,72,128]{2,1,0:T(8,128)(2,1)S(1)}, u32[]{:S(2)}, u32[]{:S(2)}) collective-permute-start(bf16[8,72,128]{2,1,0:T(8,128)(2,1)} %get-tuple-element.60), channel_id=1, source_target_pairs={{0,8},{8,16},{16,24},{24,0},{32,40},{40,48},{48,56},{56,32},{64,72... | collective-permute-start | bytes 442376 | tf_op jit(solution)/shard_map/ppermute | solution.py:22
  57.0 9.9 %collective-permute-start.9 = (bf16[8,72,128]{2,1,0:T(8,128)(2,1)}, bf16[8,72,128]{2,1,0:T(8,128)(2,1)S(1)}, u32[]{:S(2)}, u32[]{:S(2)}) collective-permute-start(bf16[8,72,128]{2,1,0:T(8,128)(2,1)} %get-tuple-element.61), channel_id=1, source_target_pairs={{0,16},{8,24},{16,0},{24,8},{32,48},{40,56},{48,32},{56,40},{64,80... | collective-permute-start | bytes 442376 | tf_op jit(solution)/shard_map/ppermute | solution.py:22
  68.6 15.3 %collective-permute-start.16 = (bf16[768,512]{1,0:T(8,128)(2,1)}, bf16[768,512]{1,0:T(8,128)(2,1)}, u32[]{:S(2)}, u32[]{:S(2)}) collective-permute-start(bf16[768,512]{1,0:T(8,128)(2,1)} %collective-permute-done.11.refs_2_), channel_id=1, source_target_pairs={{0,2},{1,7},{2,4},{3,1},{4,6},{5,3},{6,0},{7,5},{8,10},{9,15},{10,... | collective-permute-start | bytes 2359304 | tf_op jit(solution)/shard_map/ppermute | solution.py:27
  72.7 26.9 %collective-permute-start.14 = (bf16[4,1024,128]{2,1,0:T(8,128)(2,1)}, bf16[4,1024,128]{2,1,0:T(8,128)(2,1)S(1)}, u32[]{:S(2)}, u32[]{:S(2)}) collective-permute-start(bf16[4,1024,128]{2,1,0:T(8,128)(2,1)} %get-tuple-element.100), channel_id=1, source_target_pairs={{0,8},{8,16},{16,24},{24,0},{32,40},{40,48},{48,56},{56,32},{64,72... | collective-permute-start | bytes 3145736 | tf_op jit(solution)/shard_map/ppermute | solution.py:22
  72.7 27.0 %collective-permute-start.15 = (bf16[4,1024,128]{2,1,0:T(8,128)(2,1)}, bf16[4,1024,128]{2,1,0:T(8,128)(2,1)S(1)}, u32[]{:S(2)}, u32[]{:S(2)}) collective-permute-start(bf16[4,1024,128]{2,1,0:T(8,128)(2,1)} %get-tuple-element.101), channel_id=1, source_target_pairs={{0,24},{8,0},{16,8},{24,16},{32,56},{40,32},{48,40},{56,48},{64,88... | collective-permute-start | bytes 3145736 | tf_op jit(solution)/shard_map/ppermute | solution.py:22
  75.4 27.0 %collective-permute-start.17 = (bf16[768,512]{1,0:T(8,128)(2,1)S(1)}, bf16[768,512]{1,0:T(8,128)(2,1)}, u32[]{:S(2)}, u32[]{:S(2)}) collective-permute-start(bf16[768,512]{1,0:T(8,128)(2,1)S(1)} %copy-done.1), channel_id=1, source_target_pairs={{0,1},{1,0},{2,3},{3,2},{4,5},{5,4},{6,7},{7,6},{8,9},{9,8},{10,11... | collective-permute-start | bytes 2359304 | tf_op jit(solution)/shard_map/ppermute | solution.py:35
  75.8 26.7 %collective-permute-start.18 = (bf16[768,512]{1,0:T(8,128)(2,1)}, bf16[768,512]{1,0:T(8,128)(2,1)}, u32[]{:S(2)}, u32[]{:S(2)}) collective-permute-start(bf16[768,512]{1,0:T(8,128)(2,1)} %copy-done.6), channel_id=1, source_target_pairs={{0,1},{1,0},{2,3},{3,2},{4,5},{5,4},{6,7},{7,6},{8,9},{9,8},{10,11... | collective-permute-start | bytes 2359304 | tf_op jit(solution)/shard_map/ppermute | solution.py:35
  75.9 23.7 %all-to-all-start = ((f32[8,72,128]{2,1,0:T(8,128)}), f32[8,72,128]{2,1,0:T(8,128)S(1)}, u32[]{:S(2)}, u32[]{:S(2)}) async-start(f32[8,72,128]{2,1,0:T(8,128)} %convert_add_fusion), calls=%async_computation | async-start | bytes 589824 | tf_op jit(solution)/shard_map/all_to_all | solution.py:327
  83.9 21.3 %collective-permute-start.19 = (bf16[768,512]{1,0:T(8,128)(2,1)}, bf16[768,512]{1,0:T(8,128)(2,1)}, u32[]{:S(2)}, u32[]{:S(2)}) collective-permute-start(bf16[768,512]{1,0:T(8,128)(2,1)} %collective-permute-done.11.refs_2_), channel_id=1, source_target_pairs={{0,1},{1,0},{2,3},{3,2},{4,5},{5,4},{6,7},{7,6},{8,9},{9,8},{10,11... | collective-permute-start | bytes 2359304 | tf_op jit(solution)/shard_map/ppermute | solution.py:35
  99.6 24.8 %collective-permute-start.12 = (bf16[4,1024,128]{2,1,0:T(8,128)(2,1)}, bf16[4,1024,128]{2,1,0:T(8,128)(2,1)}, u32[]{:S(2)}, u32[]{:S(2)}) collective-permute-start(bf16[4,1024,128]{2,1,0:T(8,128)(2,1)} %get-tuple-element.101), channel_id=1, source_target_pairs={{0,8},{8,16},{16,24},{24,0},{32,40},{40,48},{48,56},{56,32},{64,72... | collective-permute-start | bytes 3145736 | tf_op jit(solution)/shard_map/ppermute | solution.py:22
  99.8 24.6 %collective-permute-start.13 = (bf16[4,1024,128]{2,1,0:T(8,128)(2,1)}, bf16[4,1024,128]{2,1,0:T(8,128)(2,1)}, u32[]{:S(2)}, u32[]{:S(2)}) collective-permute-start(bf16[4,1024,128]{2,1,0:T(8,128)(2,1)} %get-tuple-element.100), channel_id=1, source_target_pairs={{0,24},{8,0},{16,8},{24,16},{32,56},{40,32},{48,40},{56,48},{64,88... | collective-permute-start | bytes 3145736 | tf_op jit(solution)/shard_map/ppermute | solution.py:22
  102.4 71.8 %collective-permute-start.21 = (bf16[4,1024,128]{2,1,0:T(8,128)(2,1)S(1)}, bf16[4,1024,128]{2,1,0:T(8,128)(2,1)S(1)}, u32[]{:S(2)}, u32[]{:S(2)}) collective-permute-start(bf16[4,1024,128]{2,1,0:T(8,128)(2,1)S(1)} %collective-permute-done.14.p0), channel_id=1, source_target_pairs={{0,8},{8,16},{16,24},{24,0},{32,40},{40,48},{48,56},{56,32},{64,72... | collective-permute-start | bytes 3145736 | tf_op jit(solution)/shard_map/ppermute | solution.py:22
  102.5 71.7 %collective-permute-start.22 = (bf16[4,1024,128]{2,1,0:T(8,128)(2,1)S(1)}, bf16[4,1024,128]{2,1,0:T(8,128)(2,1)}, u32[]{:S(2)}, u32[]{:S(2)}) collective-permute-start(bf16[4,1024,128]{2,1,0:T(8,128)(2,1)S(1)} %collective-permute-done.15.m1), channel_id=1, source_target_pairs={{0,24},{8,0},{16,8},{24,16},{32,56},{40,32},{48,40},{56,48},{64,88... | collective-permute-start | bytes 3145736 | tf_op jit(solution)/shard_map/ppermute | solution.py:22
  105.2 7.0 %collective-permute-start.20 = (bf16[768,512]{1,0:T(8,128)(2,1)}, bf16[768,512]{1,0:T(8,128)(2,1)}, u32[]{:S(2)}, u32[]{:S(2)}) collective-permute-start(bf16[768,512]{1,0:T(8,128)(2,1)} %collective-permute-done.16.refs_3_), channel_id=1, source_target_pairs={{0,1},{1,0},{2,3},{3,2},{4,5},{5,4},{6,7},{7,6},{8,9},{9,8},{10,11... | collective-permute-start | bytes 2359304 | tf_op jit(solution)/shard_map/ppermute | solution.py:35
  108.5 15.9 %all-to-all-start.1 = ((bf16[8,56,128]{2,1,0:T(8,128)(2,1)}), bf16[8,56,128]{2,1,0:T(8,128)(2,1)S(1)}, u32[]{:S(2)}, u32[]{:S(2)}) async-start(bf16[8,56,128]{2,1,0:T(8,128)(2,1)} %broadcast_in_dim.2), calls=%async_computation.1 | async-start | bytes 229376 | tf_op jit(solution)/shard_map/all_to_all | solution.py:335
  124.4 24.7 %collective-permute-start.23 = (f32[16,128]{1,0:T(8,128)S(1)}, f32[16,128]{1,0:T(8,128)S(1)}, u32[]{:S(2)}, u32[]{:S(2)}) collective-permute-start(f32[16,128]{1,0:T(8,128)S(1)} %slice.24), channel_id=1, source_target_pairs={{0,0},{1,32},{2,64},{3,96},{4,128},{5,160},{6,192},{7,224},{8,1},{... | collective-permute-start | bytes 24584 | tf_op jit(solution)/shard_map/ppermute | solution.py:342
  131.2 43.0 %collective-permute-start.24 = (bf16[8,56,128]{2,1,0:T(8,128)(2,1)S(1)}, bf16[8,56,128]{2,1,0:T(8,128)(2,1)S(1)}, u32[]{:S(2)}, u32[]{:S(2)}) collective-permute-start(bf16[8,56,128]{2,1,0:T(8,128)(2,1)S(1)} %all-to-all-done.1), channel_id=1, source_target_pairs={{0,8},{8,16},{16,24},{24,0},{32,40},{40,48},{48,56},{56,32},{64,72... | collective-permute-start | bytes 344072 | tf_op jit(solution)/shard_map/ppermute | solution.py:22
  131.3 42.9 %collective-permute-start.25 = (bf16[8,56,128]{2,1,0:T(8,128)(2,1)S(1)}, bf16[8,56,128]{2,1,0:T(8,128)(2,1)S(1)}, u32[]{:S(2)}, u32[]{:S(2)}) collective-permute-start(bf16[8,56,128]{2,1,0:T(8,128)(2,1)S(1)} %all-to-all-done.1), channel_id=1, source_target_pairs={{0,16},{8,24},{16,0},{24,8},{32,48},{40,56},{48,32},{56,40},{64,80... | collective-permute-start | bytes 344072 | tf_op jit(solution)/shard_map/ppermute | solution.py:22
  149.1 25.1 %collective-permute-start.26 = (bf16[8,56,128]{2,1,0:T(8,128)(2,1)S(1)}, bf16[8,56,128]{2,1,0:T(8,128)(2,1)}, u32[]{:S(2)}, u32[]{:S(2)}) collective-permute-start(bf16[8,56,128]{2,1,0:T(8,128)(2,1)S(1)} %all-to-all-done.1), channel_id=1, source_target_pairs={{0,24},{8,0},{16,8},{24,16},{32,56},{40,32},{48,40},{56,48},{64,88... | collective-permute-start | bytes 344072 | tf_op jit(solution)/shard_map/ppermute | solution.py:22
  (9 other events, 103.2 us)
Sparse Core Ops, SparseCore 0:
  9.8 41.1 all-gather.4
  52.8 85.4 all-gather.6

commit v4 on v2

--- a/solution.py
+++ b/solution.py
@@ -337,17 +337,18 @@
     near.append(turn_x(near[-1]))
 
     came = [move_y(chunks[j], j) for j in range(1, NY)]
-    parts = sum(chunk.astype(jnp.float32) for chunk in [chunks[0]] + came).astype(jnp.bfloat16)
+    parts = sum(chunk.astype(jnp.float32) for chunk in [chunks[0]] + came)
     row, parts, near[2] = together(row, parts, near[2])
     plus, minus = move_y(row, 1), move_y(row, -1)
     parts = lax.all_to_all(parts, "dp", 0, 0, tiled=True, axis_index_groups=Z_GROUPS)
-    total = jnp.sum(parts.astype(jnp.float32), axis=0) * token_scale
+    total = jnp.sum(parts, axis=0) * token_scale
     down_rows = hidden.shape[1] // n
     down = jnp.broadcast_to(total[:down_rows].astype(jnp.bfloat16)[None], (NZ, down_rows, 128))
     down = lax.all_to_all(down, "dp", 0, 0, tiled=True, axis_index_groups=Z_GROUPS)
     near.append(turn_x(near[-1]))
     left = arrange(place, near + [swap_core(block) for block in near])
     partial, side_left, late_left = project_own(place, left, routed, adapter_down_weight, row)
+    down, partial, side_left, late_left = together(down, partial, side_left, late_left)
     came = [down] + [move_y(down, j) for j in range(1, NY)]
     plus, minus, partial, side_left, late_left, *came = together(
         plus, minus, partial, side_left, late_left, *came

time: 178 us -> 178 us (level)
  starting transfers between devices: 38.9 us -> 42.1 us
  waiting for transfers between devices: 50 us -> 47.9 us
    all_to_all x1, waiting for transfers between devices: 10 us -> 0.01 us  [per_device(): lax.all_to_all(down, 'dp', 0, 0, tiled=True, axis_index_groups=Z_GROUPS)]
    ppermute x1, starting transfers between devices: 3.57 us -> 8.29 us  [per_device(): lax.ppermute(total[down_rows:], ('dp', 'tensor'), pairs)]
    all_to_all x1, waiting for transfers between devices: 9.54 us -> 14.1 us  [per_device(): lax.all_to_all(parts, 'dp', 0, 0, tiled=True, axis_index_groups=Z_GROUPS)]
    ppermute x13, waiting for transfers between devices: 15 us -> 18.3 us  [move_y(): return lax.ppermute(value, 'dp', pairs)]
    unnamed x32 -> x34, local copies, waits for them, and re-layouts: 6.04 us -> 5.92 us
  transfers between devices with their start and end apart: 29 -> 29, of which waited for: 14 -> 14; matrix products, arithmetic and copies ran while one was open for 10% -> 9% of each run, Pallas kernels for 27% -> 27%
where the time goes in v4:
time: 178 us; the launch traced here: 177 us
  Pallas kernels  53 us (30%)
  waiting for transfers between devices  47.9 us (27%)
  starting transfers between devices  42.1 us (24%)
  local copies, waits for them, and re-layouts  14.3 us (8%)
  between operations  14.3 us (8%)
  other arithmetic  5.62 us (3%)
    ppermute x13, waiting for transfers between devices, move_y(): return lax.ppermute(value, 'dp', pairs)  18.3 us
    ppermute x13, starting transfers between devices, move_y(): return lax.ppermute(value, 'dp', pairs)  16.3 us
    all_to_all x1, waiting for transfers between devices, per_device(): lax.all_to_all(parts, 'dp', 0, 0, tiled=True, axis_index_groups=Z_GROUPS)  14.1 us
    ppermute x2, waiting for transfers between devices, swap_x(): lax.ppermute(value, 'tensor', [(x * 2 + c, partner(x) * 2 + c) for x in r...  10.9 us
    pallas_call x1, Pallas kernels, project_last_rows(): pl.pallas_call(last_rows_kernel, grid=(units // TILE - A_TILES,), out_sha...  10.7 us
    pallas_call x1, Pallas kernels, project_own(): pl.pallas_call(own_kernel, grid=(A_TILES,), out_shape=(jax.ShapeDtypeStru...  10.4 us
    all_to_all x1, starting transfers between devices, per_device(): lax.all_to_all(parts, 'dp', 0, 0, tiled=True, axis_index_groups=Z_GROUPS)  8.45 us
    pallas_call x1, Pallas kernels, project_sides(): pl.pallas_call(sides_kernel, grid=(A_TILES,), out_shape=jax.ShapeDtypeStr...  8.38 us
  transfers between devices with their start and end apart: 29, of which 14 were waited for; matrix products, arithmetic and copies ran while one was open for 9% of the time, Pallas kernels for 27%

profile of v4, /device:TPU:4, one launch (start us, length us, event | category | flops | bytes accessed | tf_op | source)
XLA Modules:
  0.0 177.2 jit_solution(12744623652540558681)
XLA Ops:
  7.2 1.7 slice.19
  10.5 4.3 %shard_map.102 = (f32[384,256]{1,0:T(8,128)}, f32[384,256]{1,0:T(8,128)}) custom-call(s32[4]{0:T(128)} %pad_add_fusion.place, bf16[768,1792]{1,0:T(8,128)(2,1)} %hidden.3, bf16[1792,128]{1,0:T(8,128)(2,1)} %factor.5, bf16[768,512]{1,0:T(8,128)(2,1)} %refs_0_.2, bf16[128,4096]{1,0:T(8,128)(2,1)} %up.1), custom_call_target="tpu_custom_call" | custom-call | tf_op jit(solution)/shard_map/pallas_call | solution.py:66
  14.9 1.9 %collective-permute-done.3 = f32[384,256]{1,0:T(8,128)S(1)} collective-permute-done((f32[384,256]{1,0:T(8,128)}, f32[384,256]{1,0:T(8,128)S(1)}, u32[]{:S(2)}, u32[]{:S(2)}) %collective-permute-start.3) | collective-permute-done | bytes 393248 | tf_op jit(solution)/shard_map/ppermute | solution.py:35
  17.8 1.3 collective-permute-start.4
  21.9 2.1 %shard_map.103 = (s32[768,2]{1,0:T(8,128)}, f32[768,2]{1,0:T(8,128)}) custom-call(s32[768,2]{1,0:T(8,128)} %copy.20.refs_0_, f32[768,2]{1,0:T(8,128)} %copy.21.refs_1_), custom_call_target="tpu_custom_call" | custom-call | tf_op jit(solution)/shard_map/pallas_call | solution.py:134
  23.9 6.0 %collective-permute-done.4 = f32[384,256]{1,0:T(8,128)S(1)} collective-permute-done((f32[384,256]{1,0:T(8,128)S(1)}, f32[384,256]{1,0:T(8,128)S(1)}, u32[]{:S(2)}, u32[]{:S(2)}) %collective-permute-start.4) | collective-permute-done | bytes 393248 | tf_op jit(solution)/shard_map/ppermute | solution.py:31
  30.4 2.8 %collective-permute-start.2 = (bf16[768,128]{1,0:T(8,128)(2,1)S(1)}, bf16[768,128]{1,0:T(8,128)(2,1)S(1)}, u32[]{:S(2)}, u32[]{:S(2)}) collective-permute-start(bf16[768,128]{1,0:T(8,128)(2,1)S(1)} %slice.20), channel_id=1, source_target_pairs={{0,24},{8,0},{16,8},{24,16},{32,56},{40,32},{48,40},{56,48},{64,88... | collective-permute-start | bytes 589832 | tf_op jit(solution)/shard_map/ppermute | solution.py:22
  34.7 4.9 %collective-permute-done.5 = f32[384,256]{1,0:T(8,128)S(1)} collective-permute-done((f32[384,256]{1,0:T(8,128)S(1)}, f32[384,256]{1,0:T(8,128)S(1)}, u32[]{:S(2)}, u32[]{:S(2)}) %collective-permute-start.5) | collective-permute-done | bytes 393248 | tf_op jit(solution)/shard_map/ppermute | solution.py:31
  40.5 1.6 collective-permute-done.1
  42.1 2.0 %collective-permute-done = bf16[768,128]{1,0:T(8,128)(2,1)S(1)} collective-permute-done((bf16[768,128]{1,0:T(8,128)(2,1)S(1)}, bf16[768,128]{1,0:T(8,128)(2,1)S(1)}, u32[]{:S(2)}, u32[]{:S(2)}) %collective-permute-start) | collective-permute-done | bytes 196640 | tf_op jit(solution)/shard_map/ppermute | solution.py:22
  45.5 1.2 collective-permute-start.11
  47.9 5.2 %shard_map.104 = (bf16[8,72,128]{2,1,0:T(8,128)(2,1)}, bf16[8,72,128]{2,1,0:T(8,128)(2,1)}, bf16[8,72,128]{2,1,0:T(8,128)(2,1)}, bf16[8,72,128]{2,1,0:T(8,128)(2...) custom-call(s32[4]{0:T(128)} %pad_add_fusion.place, f32[384,256]{1,0:T(8,128)} %copy-done.3, f32[384,256]{1,0:T(8,128)} %copy-done.9, ...), custom_call_target="tpu_custom_call" | custom-call | tf_op jit(solution)/shard_map/pallas_call | solution.py:115
  53.1 2.1 %collective-permute-start.9 = (bf16[8,72,128]{2,1,0:T(8,128)(2,1)}, bf16[8,72,128]{2,1,0:T(8,128)(2,1)S(1)}, u32[]{:S(2)}, u32[]{:S(2)}) collective-permute-start(bf16[8,72,128]{2,1,0:T(8,128)(2,1)} %get-tuple-element.63), channel_id=1, source_target_pairs={{0,16},{8,24},{16,0},{24,8},{32,48},{40,56},{48,32},{56,40},{64,80... | collective-permute-start | bytes 442376 | tf_op jit(solution)/shard_map/ppermute | solution.py:22
  56.4 7.1 %collective-permute-done.8 = bf16[8,72,128]{2,1,0:T(8,128)(2,1)S(1)} collective-permute-done((bf16[8,72,128]{2,1,0:T(8,128)(2,1)}, bf16[8,72,128]{2,1,0:T(8,128)(2,1)S(1)}, u32[]{:S(2)}, u32[]{:S(2)}) %collective-permute-start.8) | collective-permute-done | bytes 147488 | tf_op jit(solution)/shard_map/ppermute | solution.py:22
  64.2 1.7 convert_add_fusion
  65.9 2.3 %collective-permute-start.13 = (bf16[8,1024,128]{2,1,0:T(8,128)(2,1)}, bf16[8,1024,128]{2,1,0:T(8,128)(2,1)S(1)}, u32[]{:S(2)}, u32[]{:S(2)}) collective-permute-start(bf16[8,1024,128]{2,1,0:T(8,128)(2,1)} %bitcast.32), channel_id=1, source_target_pairs={{0,24},{8,0},{16,8},{24,16},{32,56},{40,32},{48,40},{56,48},{64,88... | collective-permute-start | bytes 6291464 | tf_op jit(solution)/shard_map/ppermute | solution.py:22
  68.2 1.2 collective-permute-start.14
  69.4 8.5 %all-to-all-start = ((f32[8,72,128]{2,1,0:T(8,128)}), f32[8,72,128]{2,1,0:T(8,128)S(1)}, u32[]{:S(2)}, u32[]{:S(2)}) async-start(f32[8,72,128]{2,1,0:T(8,128)} %convert_add_fusion), calls=%async_computation | async-start | bytes 589824 | tf_op jit(solution)/shard_map/all_to_all | solution.py:343
  78.4 2.2 %collective-permute-done.14.refs_3_ = bf16[768,512]{1,0:T(8,128)(2,1)} collective-permute-done((bf16[768,512]{1,0:T(8,128)(2,1)}, bf16[768,512]{1,0:T(8,128)(2,1)}, u32[]{:S(2)}, u32[]{:S(2)}) %collective-permute-start.14) | collective-permute-done | bytes 786464 | tf_op jit(solution)/shard_map/ppermute | solution.py:27
  80.6 14.1 %all-to-all-done = f32[8,72,128]{2,1,0:T(8,128)S(1)} async-done(((f32[8,72,128]{2,1,0:T(8,128)}), f32[8,72,128]{2,1,0:T(8,128)S(1)}, u32[]{:S(2)}, u32[]{:S(2)}) %all-to-all-start) | async-done | bytes 294944 | tf_op jit(solution)/shard_map/all_to_all | solution.py:343
  95.4 3.4 %all-to-all-start.1 = ((bf16[8,56,128]{2,1,0:T(8,128)(2,1)}), bf16[8,56,128]{2,1,0:T(8,128)(2,1)S(1)}, u32[]{:S(2)}, u32[]{:S(2)}) async-start(bf16[8,56,128]{2,1,0:T(8,128)(2,1)} %broadcast_in_dim.2), calls=%async_computation.1 | async-start | bytes 229376 | tf_op jit(solution)/shard_map/all_to_all | solution.py:347
  99.7 6.0 %shard_map.105.left = bf16[768,4096]{1,0:T(8,128)(2,1)} custom-call(s32[4]{0:T(128)} %pad_add_fusion.place, bf16[768,512]{1,0:T(8,128)(2,1)} %refs_0_.2, bf16[768,512]{1,0:T(8,128)(2,1)} %copy-done.5, bf16[768,512]{1,0:T(8,128)(2,1)} %collective-permute-done.11.refs_2_, bf16[768,512]{1,0:T(8,128)(2,1)} %collective-permute-done.14.refs_3_, ...), custom_call_target="tpu_custom_call" | custom-call | tf_op jit(solution)/shard_map/pallas_call | solution.py:158
  105.7 10.4 %shard_map.106 = (f32[768,1024]{1,0:T(8,128)}, bf16[768,2048]{1,0:T(8,128)(2,1)}, bf16[768,1024]{1,0:T(8,128)(2,1)}) custom-call(s32[4]{0:T(128)} %pad_add_fusion.place, bf16[768,4096]{1,0:T(8,128)(2,1)} %shard_map.105.left, bf16[768,128]{1,0:T(8,128)(2,1)} %get-tuple-element.69.routed, bf16[1792,128]{1,0:T(8,128)(2,1)} %factor.5, bf16[8,1024,128]{2,1,0:T(8,128)(2,1)} %bitcast.34), custom_call_target="tpu_custom_call" | custom-call | tf_op jit(solution)/shard_map/pallas_call | solution.py:226
  116.1 3.3 %collective-permute-start.21 = (bf16[8,56,128]{2,1,0:T(8,128)(2,1)S(1)}, bf16[8,56,128]{2,1,0:T(8,128)(2,1)S(1)}, u32[]{:S(2)}, u32[]{:S(2)}) collective-permute-start(bf16[8,56,128]{2,1,0:T(8,128)(2,1)S(1)} %all-to-all-done.1), channel_id=1, source_target_pairs={{0,24},{8,0},{16,8},{24,16},{32,56},{40,32},{48,40},{56,48},{64,88... | collective-permute-start | bytes 344072 | tf_op jit(solution)/shard_map/ppermute | solution.py:22
  121.1 3.0 %collective-permute-done.21 = bf16[8,56,128]{2,1,0:T(8,128)(2,1)S(1)} collective-permute-done((bf16[8,56,128]{2,1,0:T(8,128)(2,1)S(1)}, bf16[8,56,128]{2,1,0:T(8,128)(2,1)S(1)}, u32[]{:S(2)}, u32[]{:S(2)}) %collective-permute-start.21) | collective-permute-done | bytes 114720 | tf_op jit(solution)/shard_map/ppermute | solution.py:22
  124.1 8.3 %collective-permute-start.24 = (f32[16,128]{1,0:T(8,128)S(1)}, f32[16,128]{1,0:T(8,128)S(1)}, u32[]{:S(2)}, u32[]{:S(2)}) collective-permute-start(f32[16,128]{1,0:T(8,128)S(1)} %slice.26), channel_id=1, source_target_pairs={{0,0},{1,32},{2,64},{3,96},{4,128},{5,160},{6,192},{7,224},{8,1},{... | collective-permute-start | bytes 24584 | tf_op jit(solution)/shard_map/ppermute | solution.py:361
  132.5 3.0 %slice.22 = bf16[4,1024,128]{2,1,0:T(8,128)(2,1)} slice(bf16[8,1024,128]{2,1,0:T(8,128)(2,1)} %collective-permute-done.12.plus), slice={[0:4], [0:1024], [0:128]} | slice | bytes 2097152 | tf_op jit(solution)/shard_map/slice | solution.py:358
  136.6 1.6 collective-permute-start.23
  141.6 8.4 %shard_map.108.partial = f32[768,1024]{1,0:T(8,128)} custom-call(bf16[768,2048]{1,0:T(8,128)(2,1)} %get-tuple-element.83.picked, f32[768,1024]{1,0:T(8,128)} %get-tuple-element.84.partial, bf16[8,1024,128]{2,1,0:T(8,128)(2,1)} %collective-permute-done.12.plus, bf16[8,1024,128]{2,1,0:T(8,128)(2,1)} %copy-done.2), custom_call_target="tpu_custom_call" | custom-call | tf_op jit(solution)/shard_map/pallas_call | solution.py:250
  150.0 10.7 %shard_map.107.base = bf16[768,1792]{1,0:T(8,128)(2,1)} custom-call(s32[4]{0:T(128)} %pad_add_fusion.place, bf16[768,4096]{1,0:T(8,128)(2,1)} %shard_map.105.left, bf16[768,128]{1,0:T(8,128)(2,1)} %get-tuple-element.69.routed, bf16[1792,128]{1,0:T(8,128)(2,1)} %factor.5, bf16[8,4,768,128]{3,2,1,0:T(8,128)(2,1)} %bitcast.31), custom_call_target="tpu_custom_call" | custom-call | tf_op jit(solution)/shard_map/pallas_call | solution.py:265
  161.1 2.7 %collective-permute-done.22.low = bf16[4,1024,128]{2,1,0:T(8,128)(2,1)} collective-permute-done((bf16[4,1024,128]{2,1,0:T(8,128)(2,1)}, bf16[4,1024,128]{2,1,0:T(8,128)(2,1)}, u32[]{:S(2)}, u32[]{:S(2)}) %collective-permute-start.22) | collective-permute-done | bytes 1048608 | tf_op jit(solution)/shard_map/ppermute | solution.py:22
  163.8 6.0 %shard_map.109 = bf16[768,1792]{1,0:T(8,128)(2,1)} custom-call(bf16[768,1024]{1,0:T(8,128)(2,1)} %get-tuple-element.77.picked, f32[768,1024]{1,0:T(8,128)} %shard_map.108.partial, bf16[4,1024,128]{2,1,0:T(8,128)(2,1)} %collective-permute-done.22.low, bf16[4,1024,128]{2,1,0:T(8,128)(2,1)} %copy-done.4, ...), custom_call_target="tpu_custom_call", output_to_operand_aliasing={{}: (4, {})} | custom-call | tf_op jit(solution)/shard_map/pallas_call | solution.py:283
  (87 shorter events, 21.9 us)
Async XLA Ops:
  7.2 58.7 %all-gather.5.cloned.1.call-start = ((), (), s32[]{:S(2)}) async-start(), calls=%async_computation.2 | async-start | bytes 2359296 | tf_op jit(solution)/shard_map/all_gather | solution.py:317
  8.9 141.1 %all-gather.7.cloned.1.call-start = ((), (), s32[]{:S(2)}) async-start(), calls=%async_computation.3 | async-start | bytes 7077888 | tf_op jit(solution)/shard_map/all_gather | solution.py:331
  10.5 10.4 %copy-start.11 = (f32[768,2]{0,1:T(2,128)S(1)}, f32[768,2]{0,1:T(2,128)}, u32[]{:S(2)}) copy-start(f32[768,2]{0,1:T(2,128)} %param.13) | copy-start | bytes 18436
  14.9 1.9 %collective-permute-start.3 = (f32[384,256]{1,0:T(8,128)}, f32[384,256]{1,0:T(8,128)S(1)}, u32[]{:S(2)}, u32[]{:S(2)}) collective-permute-start(f32[384,256]{1,0:T(8,128)} %get-tuple-element.54), channel_id=1, source_target_pairs={{0,1},{1,0},{2,3},{3,2},{4,5},{5,4},{6,7},{7,6},{8,9},{9,8},{10,11... | collective-permute-start | bytes 1179656 | tf_op jit(solution)/shard_map/ppermute | solution.py:35
  17.8 12.0 %collective-permute-start.4 = (f32[384,256]{1,0:T(8,128)S(1)}, f32[384,256]{1,0:T(8,128)S(1)}, u32[]{:S(2)}, u32[]{:S(2)}) collective-permute-start(f32[384,256]{1,0:T(8,128)S(1)} %add.22), channel_id=1, source_target_pairs={{0,2},{1,3},{2,0},{3,1},{4,6},{5,7},{6,4},{7,5},{8,10},{9,11},{10,... | collective-permute-start | bytes 1179656 | tf_op jit(solution)/shard_map/ppermute | solution.py:31
  19.1 25.0 %collective-permute-start.6 = (bf16[768,512]{1,0:T(8,128)(2,1)S(1)}, bf16[768,512]{1,0:T(8,128)(2,1)S(1)}, u32[]{:S(2)}, u32[]{:S(2)}) collective-permute-start(bf16[768,512]{1,0:T(8,128)(2,1)S(1)} %copy-done), channel_id=1, source_target_pairs={{0,2},{1,7},{2,4},{3,1},{4,6},{5,3},{6,0},{7,5},{8,10},{9,15},{10,... | collective-permute-start | bytes 2359304 | tf_op jit(solution)/shard_map/ppermute | solution.py:27
  29.9 9.7 %collective-permute-start.5 = (f32[384,256]{1,0:T(8,128)S(1)}, f32[384,256]{1,0:T(8,128)S(1)}, u32[]{:S(2)}, u32[]{:S(2)}) collective-permute-start(f32[384,256]{1,0:T(8,128)S(1)} %add.23), channel_id=1, source_target_pairs={{0,6},{1,7},{2,4},{3,5},{4,2},{5,3},{6,0},{7,1},{8,14},{9,15},{10,... | collective-permute-start | bytes 1179656 | tf_op jit(solution)/shard_map/ppermute | solution.py:31
  30.4 10.1 %collective-permute-start.2 = (bf16[768,128]{1,0:T(8,128)(2,1)S(1)}, bf16[768,128]{1,0:T(8,128)(2,1)S(1)}, u32[]{:S(2)}, u32[]{:S(2)}) collective-permute-start(bf16[768,128]{1,0:T(8,128)(2,1)S(1)} %slice.20), channel_id=1, source_target_pairs={{0,24},{8,0},{16,8},{24,16},{32,56},{40,32},{48,40},{56,48},{64,88... | collective-permute-start | bytes 589832 | tf_op jit(solution)/shard_map/ppermute | solution.py:22
  33.1 9.0 %collective-permute-start.1 = (bf16[768,128]{1,0:T(8,128)(2,1)S(1)}, bf16[768,128]{1,0:T(8,128)(2,1)S(1)}, u32[]{:S(2)}, u32[]{:S(2)}) collective-permute-start(bf16[768,128]{1,0:T(8,128)(2,1)S(1)} %slice.20), channel_id=1, source_target_pairs={{0,16},{8,24},{16,0},{24,8},{32,48},{40,56},{48,32},{56,40},{64,80... | collective-permute-start | bytes 589832 | tf_op jit(solution)/shard_map/ppermute | solution.py:22
  33.8 10.4 %collective-permute-start = (bf16[768,128]{1,0:T(8,128)(2,1)S(1)}, bf16[768,128]{1,0:T(8,128)(2,1)S(1)}, u32[]{:S(2)}, u32[]{:S(2)}) collective-permute-start(bf16[768,128]{1,0:T(8,128)(2,1)S(1)} %slice.20), channel_id=1, source_target_pairs={{0,8},{8,16},{16,24},{24,0},{32,40},{40,48},{48,56},{56,32},{64,72... | collective-permute-start | bytes 589832 | tf_op jit(solution)/shard_map/ppermute | solution.py:22
  45.3 22.9 %copy-start.1 = (bf16[768,512]{1,0:T(8,128)(2,1)S(1)}, bf16[768,512]{1,0:T(8,128)(2,1)}, u32[]{:S(2)}) copy-start(bf16[768,512]{1,0:T(8,128)(2,1)} %refs_0_.2) | copy-start | bytes 2359300
  45.4 1.8 %collective-permute-start.7 = (f32[384,256]{1,0:T(8,128)S(1)}, f32[384,256]{1,0:T(8,128)S(1)}, u32[]{:S(2)}, u32[]{:S(2)}) collective-permute-start(f32[384,256]{1,0:T(8,128)S(1)} %add.24.kept), channel_id=1, source_target_pairs={{0,1},{1,0},{2,3},{3,2},{4,5},{5,4},{6,7},{7,6},{8,9},{9,8},{10,11... | collective-permute-start | bytes 1179656 | tf_op jit(solution)/shard_map/ppermute | solution.py:35
  45.5 20.4 %collective-permute-start.11 = (bf16[768,512]{1,0:T(8,128)(2,1)S(1)}, bf16[768,512]{1,0:T(8,128)(2,1)}, u32[]{:S(2)}, u32[]{:S(2)}) collective-permute-start(bf16[768,512]{1,0:T(8,128)(2,1)S(1)} %collective-permute-done.6.refs_1_), channel_id=1, source_target_pairs={{0,2},{1,7},{2,4},{3,1},{4,6},{5,3},{6,0},{7,5},{8,10},{9,15},{10,... | collective-permute-start | bytes 2359304 | tf_op jit(solution)/shard_map/ppermute | solution.py:27
  53.1 10.5 %collective-permute-start.8 = (bf16[8,72,128]{2,1,0:T(8,128)(2,1)}, bf16[8,72,128]{2,1,0:T(8,128)(2,1)S(1)}, u32[]{:S(2)}, u32[]{:S(2)}) collective-permute-start(bf16[8,72,128]{2,1,0:T(8,128)(2,1)} %get-tuple-element.62), channel_id=1, source_target_pairs={{0,8},{8,16},{16,24},{24,0},{32,40},{40,48},{48,56},{56,32},{64,72... | collective-permute-start | bytes 442376 | tf_op jit(solution)/shard_map/ppermute | solution.py:22
  53.1 10.4 %collective-permute-start.9 = (bf16[8,72,128]{2,1,0:T(8,128)(2,1)}, bf16[8,72,128]{2,1,0:T(8,128)(2,1)S(1)}, u32[]{:S(2)}, u32[]{:S(2)}) collective-permute-start(bf16[8,72,128]{2,1,0:T(8,128)(2,1)} %get-tuple-element.63), channel_id=1, source_target_pairs={{0,16},{8,24},{16,0},{24,8},{32,48},{40,56},{48,32},{56,40},{64,80... | collective-permute-start | bytes 442376 | tf_op jit(solution)/shard_map/ppermute | solution.py:22
  55.2 8.9 %collective-permute-start.10 = (bf16[8,72,128]{2,1,0:T(8,128)(2,1)}, bf16[8,72,128]{2,1,0:T(8,128)(2,1)S(1)}, u32[]{:S(2)}, u32[]{:S(2)}) collective-permute-start(bf16[8,72,128]{2,1,0:T(8,128)(2,1)} %get-tuple-element.64), channel_id=1, source_target_pairs={{0,24},{8,0},{16,8},{24,16},{32,56},{40,32},{48,40},{56,48},{64,88... | collective-permute-start | bytes 442376 | tf_op jit(solution)/shard_map/ppermute | solution.py:22
  65.9 66.6 %collective-permute-start.13 = (bf16[8,1024,128]{2,1,0:T(8,128)(2,1)}, bf16[8,1024,128]{2,1,0:T(8,128)(2,1)S(1)}, u32[]{:S(2)}, u32[]{:S(2)}) collective-permute-start(bf16[8,1024,128]{2,1,0:T(8,128)(2,1)} %bitcast.32), channel_id=1, source_target_pairs={{0,24},{8,0},{16,8},{24,16},{32,56},{40,32},{48,40},{56,48},{64,88... | collective-permute-start | bytes 6291464 | tf_op jit(solution)/shard_map/ppermute | solution.py:22
  68.2 64.2 %collective-permute-start.12 = (bf16[8,1024,128]{2,1,0:T(8,128)(2,1)}, bf16[8,1024,128]{2,1,0:T(8,128)(2,1)}, u32[]{:S(2)}, u32[]{:S(2)}) collective-permute-start(bf16[8,1024,128]{2,1,0:T(8,128)(2,1)} %bitcast.33), channel_id=1, source_target_pairs={{0,8},{8,16},{16,24},{24,0},{32,40},{40,48},{48,56},{56,32},{64,72... | collective-permute-start | bytes 6291464 | tf_op jit(solution)/shard_map/ppermute | solution.py:22
  68.2 10.0 %collective-permute-start.15 = (bf16[768,512]{1,0:T(8,128)(2,1)S(1)}, bf16[768,512]{1,0:T(8,128)(2,1)}, u32[]{:S(2)}, u32[]{:S(2)}) collective-permute-start(bf16[768,512]{1,0:T(8,128)(2,1)S(1)} %copy-done.1), channel_id=1, source_target_pairs={{0,1},{1,0},{2,3},{3,2},{4,5},{5,4},{6,7},{7,6},{8,9},{9,8},{10,11... | collective-permute-start | bytes 2359304 | tf_op jit(solution)/shard_map/ppermute | solution.py:35
  68.2 12.4 %collective-permute-start.14 = (bf16[768,512]{1,0:T(8,128)(2,1)}, bf16[768,512]{1,0:T(8,128)(2,1)}, u32[]{:S(2)}, u32[]{:S(2)}) collective-permute-start(bf16[768,512]{1,0:T(8,128)(2,1)} %collective-permute-done.11.refs_2_), channel_id=1, source_target_pairs={{0,2},{1,7},{2,4},{3,1},{4,6},{5,3},{6,0},{7,5},{8,10},{9,15},{10,... | collective-permute-start | bytes 2359304 | tf_op jit(solution)/shard_map/ppermute | solution.py:27
  69.4 25.2 %all-to-all-start = ((f32[8,72,128]{2,1,0:T(8,128)}), f32[8,72,128]{2,1,0:T(8,128)S(1)}, u32[]{:S(2)}, u32[]{:S(2)}) async-start(f32[8,72,128]{2,1,0:T(8,128)} %convert_add_fusion), calls=%async_computation | async-start | bytes 589824 | tf_op jit(solution)/shard_map/all_to_all | solution.py:343
  77.9 20.9 %collective-permute-start.16 = (bf16[768,512]{1,0:T(8,128)(2,1)}, bf16[768,512]{1,0:T(8,128)(2,1)}, u32[]{:S(2)}, u32[]{:S(2)}) collective-permute-start(bf16[768,512]{1,0:T(8,128)(2,1)} %copy-done.5), channel_id=1, source_target_pairs={{0,1},{1,0},{2,3},{3,2},{4,5},{5,4},{6,7},{7,6},{8,9},{9,8},{10,11... | collective-permute-start | bytes 2359304 | tf_op jit(solution)/shard_map/ppermute | solution.py:35
  78.3 20.5 %collective-permute-start.17 = (bf16[768,512]{1,0:T(8,128)(2,1)}, bf16[768,512]{1,0:T(8,128)(2,1)S(1)}, u32[]{:S(2)}, u32[]{:S(2)}) collective-permute-start(bf16[768,512]{1,0:T(8,128)(2,1)} %collective-permute-done.11.refs_2_), channel_id=1, source_target_pairs={{0,1},{1,0},{2,3},{3,2},{4,5},{5,4},{6,7},{7,6},{8,9},{9,8},{10,11... | collective-permute-start | bytes 2359304 | tf_op jit(solution)/shard_map/ppermute | solution.py:35
  80.6 18.2 %collective-permute-start.18 = (bf16[768,512]{1,0:T(8,128)(2,1)}, bf16[768,512]{1,0:T(8,128)(2,1)}, u32[]{:S(2)}, u32[]{:S(2)}) collective-permute-start(bf16[768,512]{1,0:T(8,128)(2,1)} %collective-permute-done.14.refs_3_), channel_id=1, source_target_pairs={{0,1},{1,0},{2,3},{3,2},{4,5},{5,4},{6,7},{7,6},{8,9},{9,8},{10,11... | collective-permute-start | bytes 2359304 | tf_op jit(solution)/shard_map/ppermute | solution.py:35
  95.4 20.7 %all-to-all-start.1 = ((bf16[8,56,128]{2,1,0:T(8,128)(2,1)}), bf16[8,56,128]{2,1,0:T(8,128)(2,1)S(1)}, u32[]{:S(2)}, u32[]{:S(2)}) async-start(bf16[8,56,128]{2,1,0:T(8,128)(2,1)} %broadcast_in_dim.2), calls=%async_computation.1 | async-start | bytes 229376 | tf_op jit(solution)/shard_map/all_to_all | solution.py:347
  105.7 14.6 %copy-start.8 = (f32[768,2]{1,0:T(8,128)S(1)}, f32[768,2]{1,0:T(8,128)}, u32[]{:S(2)}) copy-start(f32[768,2]{1,0:T(8,128)} %get-tuple-element.103) | copy-start | bytes 18436
  116.1 8.0 %collective-permute-start.21 = (bf16[8,56,128]{2,1,0:T(8,128)(2,1)S(1)}, bf16[8,56,128]{2,1,0:T(8,128)(2,1)S(1)}, u32[]{:S(2)}, u32[]{:S(2)}) collective-permute-start(bf16[8,56,128]{2,1,0:T(8,128)(2,1)S(1)} %all-to-all-done.1), channel_id=1, source_target_pairs={{0,24},{8,0},{16,8},{24,16},{32,56},{40,32},{48,40},{56,48},{64,88... | collective-permute-start | bytes 344072 | tf_op jit(solution)/shard_map/ppermute | solution.py:22
  119.4 13.0 %collective-permute-start.20 = (bf16[8,56,128]{2,1,0:T(8,128)(2,1)S(1)}, bf16[8,56,128]{2,1,0:T(8,128)(2,1)S(1)}, u32[]{:S(2)}, u32[]{:S(2)}) collective-permute-start(bf16[8,56,128]{2,1,0:T(8,128)(2,1)S(1)} %all-to-all-done.1), channel_id=1, source_target_pairs={{0,16},{8,24},{16,0},{24,8},{32,48},{40,56},{48,32},{56,40},{64,80... | collective-permute-start | bytes 344072 | tf_op jit(solution)/shard_map/ppermute | solution.py:22
  119.4 13.0 %collective-permute-start.19 = (bf16[8,56,128]{2,1,0:T(8,128)(2,1)S(1)}, bf16[8,56,128]{2,1,0:T(8,128)(2,1)S(1)}, u32[]{:S(2)}, u32[]{:S(2)}) collective-permute-start(bf16[8,56,128]{2,1,0:T(8,128)(2,1)S(1)} %all-to-all-done.1), channel_id=1, source_target_pairs={{0,8},{8,16},{16,24},{24,0},{32,40},{40,48},{48,56},{56,32},{64,72... | collective-permute-start | bytes 344072 | tf_op jit(solution)/shard_map/ppermute | solution.py:22
  124.1 36.6 %collective-permute-start.24 = (f32[16,128]{1,0:T(8,128)S(1)}, f32[16,128]{1,0:T(8,128)S(1)}, u32[]{:S(2)}, u32[]{:S(2)}) collective-permute-start(f32[16,128]{1,0:T(8,128)S(1)} %slice.26), channel_id=1, source_target_pairs={{0,0},{1,32},{2,64},{3,96},{4,128},{5,160},{6,192},{7,224},{8,1},{... | collective-permute-start | bytes 24584 | tf_op jit(solution)/shard_map/ppermute | solution.py:361
  136.6 24.5 %collective-permute-start.23 = (bf16[4,1024,128]{2,1,0:T(8,128)(2,1)}, bf16[4,1024,128]{2,1,0:T(8,128)(2,1)S(1)}, u32[]{:S(2)}, u32[]{:S(2)}) collective-permute-start(bf16[4,1024,128]{2,1,0:T(8,128)(2,1)} %slice.23), channel_id=1, source_target_pairs={{0,24},{8,0},{16,8},{24,16},{32,56},{40,32},{48,40},{56,48},{64,88... | collective-permute-start | bytes 3145736 | tf_op jit(solution)/shard_map/ppermute | solution.py:22
  138.2 25.6 %collective-permute-start.22 = (bf16[4,1024,128]{2,1,0:T(8,128)(2,1)}, bf16[4,1024,128]{2,1,0:T(8,128)(2,1)}, u32[]{:S(2)}, u32[]{:S(2)}) collective-permute-start(bf16[4,1024,128]{2,1,0:T(8,128)(2,1)} %slice.22), channel_id=1, source_target_pairs={{0,8},{8,16},{16,24},{24,0},{32,40},{40,48},{48,56},{56,32},{64,72... | collective-permute-start | bytes 3145736 | tf_op jit(solution)/shard_map/ppermute | solution.py:22
  (9 other events, 49.1 us)
Sparse Core Ops, SparseCore 0:
  9.8 44.2 all-gather.4
  55.9 81.5 all-gather.6

commit v5 on v4

--- a/solution.py
+++ b/solution.py
@@ -348,26 +348,25 @@
     near.append(turn_x(near[-1]))
     left = arrange(place, near + [swap_core(block) for block in near])
     partial, side_left, late_left = project_own(place, left, routed, adapter_down_weight, row)
-    down, partial, side_left, late_left = together(down, partial, side_left, late_left)
-    came = [down] + [move_y(down, j) for j in range(1, NY)]
-    plus, minus, partial, side_left, late_left, *came = together(
-        plus, minus, partial, side_left, late_left, *came
+    plus, minus, partial, side_left, late_left, down, total = together(
+        plus, minus, partial, side_left, late_left, down, total
     )
 
     half = NZ // 2
     low, high = move_y(plus[:half], 1), move_y(minus[half:], -1)
     partial = project_sides(side_left, partial, plus, minus)
+    partial, down, total = together(partial, down, total)
+    came = [down] + [move_y(down, j) for j in range(1, NY)]
+    hidden_input_gradient = project_last_rows(place, left, routed, adapter_down_weight, b_blocks)
+    hidden_input_gradient, low, high, partial, total, *came = together(
+        hidden_input_gradient, low, high, partial, total, *came
+    )
     pairs = [(d * 8 + t, (4 * t + d // 8) * 8 + d % 8) for d in range(n) for t in range(8)]
     up_factor_gradient = lax.ppermute(total[down_rows:], ("dp", "tensor"), pairs).T
+    hidden_input_gradient = project_late(late_left, partial, low, high, hidden_input_gradient)
     came = jnp.stack([came[(3 - i) % NY] for i in range(2 * NY - 1)])
     came = lax.dynamic_slice_in_dim(came, 3 - place[1], NY, axis=0)
     down_factor_gradient = came.transpose(1, 0, 2, 3).reshape(-1, 128).astype(jnp.float32)
-
-    hidden_input_gradient = project_last_rows(place, left, routed, adapter_down_weight, b_blocks)
-    hidden_input_gradient, low, high, partial, down_factor_gradient, up_factor_gradient = together(
-        hidden_input_gradient, low, high, partial, down_factor_gradient, up_factor_gradient
-    )
-    hidden_input_gradient = project_late(late_left, partial, low, high, hidden_input_gradient)
     return (hidden_input_gradient, down_factor_gradient, up_factor_gradient, gate_gradient)
 
 

time: 178 us -> 178 us (level)
    unnamed x34 -> x30, local copies, waits for them, and re-layouts: 5.92 us -> 5.98 us
  transfers between devices with their start and end apart: 29 -> 29, of which waited for: 14 -> 15; matrix products, arithmetic and copies ran while one was open for 9% -> 8% of each run, Pallas kernels for 27% -> 30%
where the time goes in v5:
time: 178 us; the launch traced here: 177 us
  Pallas kernels  53 us (30%)
  waiting for transfers between devices  48.5 us (27%)
  starting transfers between devices  43.1 us (24%)
  between operations  14.3 us (8%)
  local copies, waits for them, and re-layouts  12.6 us (7%)
  other arithmetic  5.61 us (3%)
    ppermute x13, waiting for transfers between devices, move_y(): return lax.ppermute(value, 'dp', pairs)  18.8 us
    ppermute x13, starting transfers between devices, move_y(): return lax.ppermute(value, 'dp', pairs)  17.4 us
    all_to_all x1, waiting for transfers between devices, per_device(): lax.all_to_all(parts, 'dp', 0, 0, tiled=True, axis_index_groups=Z_GROUPS)  14 us
    ppermute x2, waiting for transfers between devices, swap_x(): lax.ppermute(value, 'tensor', [(x * 2 + c, partner(x) * 2 + c) for x in r...  10.9 us
    pallas_call x1, Pallas kernels, project_last_rows(): pl.pallas_call(last_rows_kernel, grid=(units // TILE - A_TILES,), out_sha...  10.7 us
    pallas_call x1, Pallas kernels, project_own(): pl.pallas_call(own_kernel, grid=(A_TILES,), out_shape=(jax.ShapeDtypeStru...  10.3 us
    pallas_call x1, Pallas kernels, project_sides(): pl.pallas_call(sides_kernel, grid=(A_TILES,), out_shape=jax.ShapeDtypeStr...  8.44 us
    all_to_all x1, starting transfers between devices, per_device(): lax.all_to_all(parts, 'dp', 0, 0, tiled=True, axis_index_groups=Z_GROUPS)  8.39 us
  transfers between devices with their start and end apart: 29, of which 15 were waited for; matrix products, arithmetic and copies ran while one was open for 8% of the time, Pallas kernels for 30%

profile of v5, /device:TPU:4, one launch (start us, length us, event | category | flops | bytes accessed | tf_op | source)
XLA Modules:
  0.0 177.1 jit_solution(13295738946849598284)
XLA Ops:
  7.2 1.7 slice.19
  10.5 4.3 %shard_map.102 = (f32[384,256]{1,0:T(8,128)}, f32[384,256]{1,0:T(8,128)}) custom-call(s32[4]{0:T(128)} %pad_add_fusion.place, bf16[768,1792]{1,0:T(8,128)(2,1)} %hidden.3, bf16[1792,128]{1,0:T(8,128)(2,1)} %factor.5, bf16[768,512]{1,0:T(8,128)(2,1)} %refs_0_.2, bf16[128,4096]{1,0:T(8,128)(2,1)} %up.1), custom_call_target="tpu_custom_call" | custom-call | tf_op jit(solution)/shard_map/pallas_call | solution.py:66
  14.8 1.9 %collective-permute-done.3 = f32[384,256]{1,0:T(8,128)S(1)} collective-permute-done((f32[384,256]{1,0:T(8,128)}, f32[384,256]{1,0:T(8,128)S(1)}, u32[]{:S(2)}, u32[]{:S(2)}) %collective-permute-start.3) | collective-permute-done | bytes 393248 | tf_op jit(solution)/shard_map/ppermute | solution.py:35
  17.8 1.3 collective-permute-start.4
  21.8 2.1 %shard_map.103 = (s32[768,2]{1,0:T(8,128)}, f32[768,2]{1,0:T(8,128)}) custom-call(s32[768,2]{1,0:T(8,128)} %copy.20.refs_0_, f32[768,2]{1,0:T(8,128)} %copy.21.refs_1_), custom_call_target="tpu_custom_call" | custom-call | tf_op jit(solution)/shard_map/pallas_call | solution.py:134
  23.9 5.9 %collective-permute-done.4 = f32[384,256]{1,0:T(8,128)S(1)} collective-permute-done((f32[384,256]{1,0:T(8,128)S(1)}, f32[384,256]{1,0:T(8,128)S(1)}, u32[]{:S(2)}, u32[]{:S(2)}) %collective-permute-start.4) | collective-permute-done | bytes 393248 | tf_op jit(solution)/shard_map/ppermute | solution.py:31
  30.3 2.8 %collective-permute-start.2 = (bf16[768,128]{1,0:T(8,128)(2,1)S(1)}, bf16[768,128]{1,0:T(8,128)(2,1)S(1)}, u32[]{:S(2)}, u32[]{:S(2)}) collective-permute-start(bf16[768,128]{1,0:T(8,128)(2,1)S(1)} %slice.20), channel_id=1, source_target_pairs={{0,24},{8,0},{16,8},{24,16},{32,56},{40,32},{48,40},{56,48},{64,88... | collective-permute-start | bytes 589832 | tf_op jit(solution)/shard_map/ppermute | solution.py:22
  34.7 4.9 %collective-permute-done.5 = f32[384,256]{1,0:T(8,128)S(1)} collective-permute-done((f32[384,256]{1,0:T(8,128)S(1)}, f32[384,256]{1,0:T(8,128)S(1)}, u32[]{:S(2)}, u32[]{:S(2)}) %collective-permute-start.5) | collective-permute-done | bytes 393248 | tf_op jit(solution)/shard_map/ppermute | solution.py:31
  40.5 1.6 collective-permute-done.1
  42.1 2.0 %collective-permute-done = bf16[768,128]{1,0:T(8,128)(2,1)S(1)} collective-permute-done((bf16[768,128]{1,0:T(8,128)(2,1)S(1)}, bf16[768,128]{1,0:T(8,128)(2,1)S(1)}, u32[]{:S(2)}, u32[]{:S(2)}) %collective-permute-start) | collective-permute-done | bytes 196640 | tf_op jit(solution)/shard_map/ppermute | solution.py:22
  45.4 1.2 collective-permute-start.11
  47.9 5.2 %shard_map.104 = (bf16[8,72,128]{2,1,0:T(8,128)(2,1)}, bf16[8,72,128]{2,1,0:T(8,128)(2,1)}, bf16[8,72,128]{2,1,0:T(8,128)(2,1)}, bf16[8,72,128]{2,1,0:T(8,128)(2...) custom-call(s32[4]{0:T(128)} %pad_add_fusion.place, f32[384,256]{1,0:T(8,128)} %copy-done.3, f32[384,256]{1,0:T(8,128)} %copy-done.7, ...), custom_call_target="tpu_custom_call" | custom-call | tf_op jit(solution)/shard_map/pallas_call | solution.py:115
  53.1 2.1 %collective-permute-start.9 = (bf16[8,72,128]{2,1,0:T(8,128)(2,1)}, bf16[8,72,128]{2,1,0:T(8,128)(2,1)S(1)}, u32[]{:S(2)}, u32[]{:S(2)}) collective-permute-start(bf16[8,72,128]{2,1,0:T(8,128)(2,1)} %get-tuple-element.63), channel_id=1, source_target_pairs={{0,16},{8,24},{16,0},{24,8},{32,48},{40,56},{48,32},{56,40},{64,80... | collective-permute-start | bytes 442376 | tf_op jit(solution)/shard_map/ppermute | solution.py:22
  56.4 7.1 %collective-permute-done.8 = bf16[8,72,128]{2,1,0:T(8,128)(2,1)S(1)} collective-permute-done((bf16[8,72,128]{2,1,0:T(8,128)(2,1)}, bf16[8,72,128]{2,1,0:T(8,128)(2,1)S(1)}, u32[]{:S(2)}, u32[]{:S(2)}) %collective-permute-start.8) | collective-permute-done | bytes 147488 | tf_op jit(solution)/shard_map/ppermute | solution.py:22
  64.1 1.7 convert_add_fusion
  65.8 2.3 %collective-permute-start.13 = (bf16[8,1024,128]{2,1,0:T(8,128)(2,1)}, bf16[8,1024,128]{2,1,0:T(8,128)(2,1)S(1)}, u32[]{:S(2)}, u32[]{:S(2)}) collective-permute-start(bf16[8,1024,128]{2,1,0:T(8,128)(2,1)} %bitcast.32), channel_id=1, source_target_pairs={{0,24},{8,0},{16,8},{24,16},{32,56},{40,32},{48,40},{56,48},{64,88... | collective-permute-start | bytes 6291464 | tf_op jit(solution)/shard_map/ppermute | solution.py:22
  69.4 8.4 %all-to-all-start = ((f32[8,72,128]{2,1,0:T(8,128)}), f32[8,72,128]{2,1,0:T(8,128)S(1)}, u32[]{:S(2)}, u32[]{:S(2)}) async-start(f32[8,72,128]{2,1,0:T(8,128)} %convert_add_fusion), calls=%async_computation | async-start | bytes 589824 | tf_op jit(solution)/shard_map/all_to_all | solution.py:343
  78.3 2.2 %collective-permute-done.14.refs_3_ = bf16[768,512]{1,0:T(8,128)(2,1)} collective-permute-done((bf16[768,512]{1,0:T(8,128)(2,1)}, bf16[768,512]{1,0:T(8,128)(2,1)}, u32[]{:S(2)}, u32[]{:S(2)}) %collective-permute-start.14) | collective-permute-done | bytes 786464 | tf_op jit(solution)/shard_map/ppermute | solution.py:27
  80.6 14.0 %all-to-all-done = f32[8,72,128]{2,1,0:T(8,128)S(1)} async-done(((f32[8,72,128]{2,1,0:T(8,128)}), f32[8,72,128]{2,1,0:T(8,128)S(1)}, u32[]{:S(2)}, u32[]{:S(2)}) %all-to-all-start) | async-done | bytes 294944 | tf_op jit(solution)/shard_map/all_to_all | solution.py:343
  95.3 3.4 %all-to-all-start.1 = ((bf16[8,56,128]{2,1,0:T(8,128)(2,1)}), bf16[8,56,128]{2,1,0:T(8,128)(2,1)S(1)}, u32[]{:S(2)}, u32[]{:S(2)}) async-start(bf16[8,56,128]{2,1,0:T(8,128)(2,1)} %broadcast_in_dim.2), calls=%async_computation.1 | async-start | bytes 229376 | tf_op jit(solution)/shard_map/all_to_all | solution.py:347
  99.6 6.0 %shard_map.105.left = bf16[768,4096]{1,0:T(8,128)(2,1)} custom-call(s32[4]{0:T(128)} %pad_add_fusion.place, bf16[768,512]{1,0:T(8,128)(2,1)} %refs_0_.2, bf16[768,512]{1,0:T(8,128)(2,1)} %copy-done.5, bf16[768,512]{1,0:T(8,128)(2,1)} %collective-permute-done.11.refs_2_, bf16[768,512]{1,0:T(8,128)(2,1)} %collective-permute-done.14.refs_3_, ...), custom_call_target="tpu_custom_call" | custom-call | tf_op jit(solution)/shard_map/pallas_call | solution.py:158
  105.6 10.3 %shard_map.106 = (f32[768,1024]{1,0:T(8,128)}, bf16[768,2048]{1,0:T(8,128)(2,1)}, bf16[768,1024]{1,0:T(8,128)(2,1)}) custom-call(s32[4]{0:T(128)} %pad_add_fusion.place, bf16[768,4096]{1,0:T(8,128)(2,1)} %shard_map.105.left, bf16[768,128]{1,0:T(8,128)(2,1)} %get-tuple-element.68.routed, bf16[1792,128]{1,0:T(8,128)(2,1)} %factor.5, bf16[8,1024,128]{2,1,0:T(8,128)(2,1)} %bitcast.34), custom_call_target="tpu_custom_call" | custom-call | tf_op jit(solution)/shard_map/pallas_call | solution.py:226
  116.7 2.3 %slice.22 = bf16[4,1024,128]{2,1,0:T(8,128)(2,1)} slice(bf16[8,1024,128]{2,1,0:T(8,128)(2,1)} %collective-permute-done.12.plus), slice={[0:4], [0:1024], [0:128]} | slice | bytes 2097152 | tf_op jit(solution)/shard_map/slice | solution.py:356
  120.0 3.3 %collective-permute-start.20 = (bf16[4,1024,128]{2,1,0:T(8,128)(2,1)}, bf16[4,1024,128]{2,1,0:T(8,128)(2,1)S(1)}, u32[]{:S(2)}, u32[]{:S(2)}) collective-permute-start(bf16[4,1024,128]{2,1,0:T(8,128)(2,1)} %slice.23), channel_id=1, source_target_pairs={{0,24},{8,0},{16,8},{24,16},{32,56},{40,32},{48,40},{56,48},{64,88... | collective-permute-start | bytes 3145736 | tf_op jit(solution)/shard_map/ppermute | solution.py:22
  123.3 8.4 %shard_map.108.partial = f32[768,1024]{1,0:T(8,128)} custom-call(bf16[768,2048]{1,0:T(8,128)(2,1)} %get-tuple-element.79.picked, f32[768,1024]{1,0:T(8,128)} %get-tuple-element.80.partial, bf16[8,1024,128]{2,1,0:T(8,128)(2,1)} %collective-permute-done.12.plus, bf16[8,1024,128]{2,1,0:T(8,128)(2,1)} %copy-done.2), custom_call_target="tpu_custom_call" | custom-call | tf_op jit(solution)/shard_map/pallas_call | solution.py:250
  131.7 3.2 %collective-permute-start.23 = (bf16[8,56,128]{2,1,0:T(8,128)(2,1)S(1)}, bf16[8,56,128]{2,1,0:T(8,128)(2,1)S(1)}, u32[]{:S(2)}, u32[]{:S(2)}) collective-permute-start(bf16[8,56,128]{2,1,0:T(8,128)(2,1)S(1)} %all-to-all-done.1), channel_id=1, source_target_pairs={{0,24},{8,0},{16,8},{24,16},{32,56},{40,32},{48,40},{56,48},{64,88... | collective-permute-start | bytes 344072 | tf_op jit(solution)/shard_map/ppermute | solution.py:22
  135.8 1.7 copy.27
  137.5 10.7 %shard_map.107.base = bf16[768,1792]{1,0:T(8,128)(2,1)} custom-call(s32[4]{0:T(128)} %pad_add_fusion.place, bf16[768,4096]{1,0:T(8,128)(2,1)} %shard_map.105.left, bf16[768,128]{1,0:T(8,128)(2,1)} %get-tuple-element.68.routed, bf16[1792,128]{1,0:T(8,128)(2,1)} %factor.5, bf16[8,4,768,128]{3,2,1,0:T(8,128)(2,1)} %bitcast.31), custom_call_target="tpu_custom_call" | custom-call | tf_op jit(solution)/shard_map/pallas_call | solution.py:265
  148.3 2.5 %collective-permute-done.23 = bf16[8,56,128]{2,1,0:T(8,128)(2,1)S(1)} collective-permute-done((bf16[8,56,128]{2,1,0:T(8,128)(2,1)S(1)}, bf16[8,56,128]{2,1,0:T(8,128)(2,1)S(1)}, u32[]{:S(2)}, u32[]{:S(2)}) %collective-permute-start.23) | collective-permute-done | bytes 114720 | tf_op jit(solution)/shard_map/ppermute | solution.py:22
  151.5 2.7 %collective-permute-done.21 = bf16[8,56,128]{2,1,0:T(8,128)(2,1)S(1)} collective-permute-done((bf16[8,56,128]{2,1,0:T(8,128)(2,1)S(1)}, bf16[8,56,128]{2,1,0:T(8,128)(2,1)S(1)}, u32[]{:S(2)}, u32[]{:S(2)}) %collective-permute-start.21) | collective-permute-done | bytes 114720 | tf_op jit(solution)/shard_map/ppermute | solution.py:22
  154.2 8.3 %collective-permute-start.24 = (f32[16,128]{1,0:T(8,128)S(1)}, f32[16,128]{1,0:T(8,128)S(1)}, u32[]{:S(2)}, u32[]{:S(2)}) collective-permute-start(f32[16,128]{1,0:T(8,128)S(1)} %slice.24), channel_id=1, source_target_pairs={{0,0},{1,32},{2,64},{3,96},{4,128},{5,160},{6,192},{7,224},{8,1},{... | collective-permute-start | bytes 24584 | tf_op jit(solution)/shard_map/ppermute | solution.py:365
  163.7 6.0 %shard_map.109 = bf16[768,1792]{1,0:T(8,128)(2,1)} custom-call(bf16[768,1024]{1,0:T(8,128)(2,1)} %get-tuple-element.73.picked, f32[768,1024]{1,0:T(8,128)} %shard_map.108.partial, bf16[4,1024,128]{2,1,0:T(8,128)(2,1)} %collective-permute-done.19.low, bf16[4,1024,128]{2,1,0:T(8,128)(2,1)} %copy-done.4, ...), custom_call_target="tpu_custom_call", output_to_operand_aliasing={{}: (4, {})} | custom-call | tf_op jit(solution)/shard_map/pallas_call | solution.py:283
  (83 shorter events, 21.0 us)
Async XLA Ops:
  7.2 58.7 %all-gather.5.cloned.1.call-start = ((), (), s32[]{:S(2)}) async-start(), calls=%async_computation.2 | async-start | bytes 2359296 | tf_op jit(solution)/shard_map/all_gather | solution.py:317
  8.9 128.6 %all-gather.7.cloned.1.call-start = ((), (), s32[]{:S(2)}) async-start(), calls=%async_computation.3 | async-start | bytes 7077888 | tf_op jit(solution)/shard_map/all_gather | solution.py:331
  10.5 10.4 %copy-start.9 = (f32[768,2]{0,1:T(2,128)S(1)}, f32[768,2]{0,1:T(2,128)}, u32[]{:S(2)}) copy-start(f32[768,2]{0,1:T(2,128)} %param.13) | copy-start | bytes 18436
  14.8 1.9 %collective-permute-start.3 = (f32[384,256]{1,0:T(8,128)}, f32[384,256]{1,0:T(8,128)S(1)}, u32[]{:S(2)}, u32[]{:S(2)}) collective-permute-start(f32[384,256]{1,0:T(8,128)} %get-tuple-element.54), channel_id=1, source_target_pairs={{0,1},{1,0},{2,3},{3,2},{4,5},{5,4},{6,7},{7,6},{8,9},{9,8},{10,11... | collective-permute-start | bytes 1179656 | tf_op jit(solution)/shard_map/ppermute | solution.py:35
  17.8 12.0 %collective-permute-start.4 = (f32[384,256]{1,0:T(8,128)S(1)}, f32[384,256]{1,0:T(8,128)S(1)}, u32[]{:S(2)}, u32[]{:S(2)}) collective-permute-start(f32[384,256]{1,0:T(8,128)S(1)} %add.22), channel_id=1, source_target_pairs={{0,2},{1,3},{2,0},{3,1},{4,6},{5,7},{6,4},{7,5},{8,10},{9,11},{10,... | collective-permute-start | bytes 1179656 | tf_op jit(solution)/shard_map/ppermute | solution.py:31
  19.1 25.0 %collective-permute-start.6 = (bf16[768,512]{1,0:T(8,128)(2,1)S(1)}, bf16[768,512]{1,0:T(8,128)(2,1)S(1)}, u32[]{:S(2)}, u32[]{:S(2)}) collective-permute-start(bf16[768,512]{1,0:T(8,128)(2,1)S(1)} %copy-done), channel_id=1, source_target_pairs={{0,2},{1,7},{2,4},{3,1},{4,6},{5,3},{6,0},{7,5},{8,10},{9,15},{10,... | collective-permute-start | bytes 2359304 | tf_op jit(solution)/shard_map/ppermute | solution.py:27
  29.9 9.7 %collective-permute-start.5 = (f32[384,256]{1,0:T(8,128)S(1)}, f32[384,256]{1,0:T(8,128)S(1)}, u32[]{:S(2)}, u32[]{:S(2)}) collective-permute-start(f32[384,256]{1,0:T(8,128)S(1)} %add.23), channel_id=1, source_target_pairs={{0,6},{1,7},{2,4},{3,5},{4,2},{5,3},{6,0},{7,1},{8,14},{9,15},{10,... | collective-permute-start | bytes 1179656 | tf_op jit(solution)/shard_map/ppermute | solution.py:31
  30.3 10.1 %collective-permute-start.2 = (bf16[768,128]{1,0:T(8,128)(2,1)S(1)}, bf16[768,128]{1,0:T(8,128)(2,1)S(1)}, u32[]{:S(2)}, u32[]{:S(2)}) collective-permute-start(bf16[768,128]{1,0:T(8,128)(2,1)S(1)} %slice.20), channel_id=1, source_target_pairs={{0,24},{8,0},{16,8},{24,16},{32,56},{40,32},{48,40},{56,48},{64,88... | collective-permute-start | bytes 589832 | tf_op jit(solution)/shard_map/ppermute | solution.py:22
  33.1 9.0 %collective-permute-start.1 = (bf16[768,128]{1,0:T(8,128)(2,1)S(1)}, bf16[768,128]{1,0:T(8,128)(2,1)S(1)}, u32[]{:S(2)}, u32[]{:S(2)}) collective-permute-start(bf16[768,128]{1,0:T(8,128)(2,1)S(1)} %slice.20), channel_id=1, source_target_pairs={{0,16},{8,24},{16,0},{24,8},{32,48},{40,56},{48,32},{56,40},{64,80... | collective-permute-start | bytes 589832 | tf_op jit(solution)/shard_map/ppermute | solution.py:22
  33.7 10.4 %collective-permute-start = (bf16[768,128]{1,0:T(8,128)(2,1)S(1)}, bf16[768,128]{1,0:T(8,128)(2,1)S(1)}, u32[]{:S(2)}, u32[]{:S(2)}) collective-permute-start(bf16[768,128]{1,0:T(8,128)(2,1)S(1)} %slice.20), channel_id=1, source_target_pairs={{0,8},{8,16},{16,24},{24,0},{32,40},{40,48},{48,56},{56,32},{64,72... | collective-permute-start | bytes 589832 | tf_op jit(solution)/shard_map/ppermute | solution.py:22
  45.3 22.9 %copy-start.1 = (bf16[768,512]{1,0:T(8,128)(2,1)S(1)}, bf16[768,512]{1,0:T(8,128)(2,1)}, u32[]{:S(2)}) copy-start(bf16[768,512]{1,0:T(8,128)(2,1)} %refs_0_.2) | copy-start | bytes 2359300
  45.3 1.8 %collective-permute-start.7 = (f32[384,256]{1,0:T(8,128)S(1)}, f32[384,256]{1,0:T(8,128)S(1)}, u32[]{:S(2)}, u32[]{:S(2)}) collective-permute-start(f32[384,256]{1,0:T(8,128)S(1)} %add.24.kept), channel_id=1, source_target_pairs={{0,1},{1,0},{2,3},{3,2},{4,5},{5,4},{6,7},{7,6},{8,9},{9,8},{10,11... | collective-permute-start | bytes 1179656 | tf_op jit(solution)/shard_map/ppermute | solution.py:35
  45.4 20.4 %collective-permute-start.11 = (bf16[768,512]{1,0:T(8,128)(2,1)S(1)}, bf16[768,512]{1,0:T(8,128)(2,1)}, u32[]{:S(2)}, u32[]{:S(2)}) collective-permute-start(bf16[768,512]{1,0:T(8,128)(2,1)S(1)} %collective-permute-done.6.refs_1_), channel_id=1, source_target_pairs={{0,2},{1,7},{2,4},{3,1},{4,6},{5,3},{6,0},{7,5},{8,10},{9,15},{10,... | collective-permute-start | bytes 2359304 | tf_op jit(solution)/shard_map/ppermute | solution.py:27
  53.1 10.5 %collective-permute-start.8 = (bf16[8,72,128]{2,1,0:T(8,128)(2,1)}, bf16[8,72,128]{2,1,0:T(8,128)(2,1)S(1)}, u32[]{:S(2)}, u32[]{:S(2)}) collective-permute-start(bf16[8,72,128]{2,1,0:T(8,128)(2,1)} %get-tuple-element.62), channel_id=1, source_target_pairs={{0,8},{8,16},{16,24},{24,0},{32,40},{40,48},{48,56},{56,32},{64,72... | collective-permute-start | bytes 442376 | tf_op jit(solution)/shard_map/ppermute | solution.py:22
  53.1 10.4 %collective-permute-start.9 = (bf16[8,72,128]{2,1,0:T(8,128)(2,1)}, bf16[8,72,128]{2,1,0:T(8,128)(2,1)S(1)}, u32[]{:S(2)}, u32[]{:S(2)}) collective-permute-start(bf16[8,72,128]{2,1,0:T(8,128)(2,1)} %get-tuple-element.63), channel_id=1, source_target_pairs={{0,16},{8,24},{16,0},{24,8},{32,48},{40,56},{48,32},{56,40},{64,80... | collective-permute-start | bytes 442376 | tf_op jit(solution)/shard_map/ppermute | solution.py:22
  55.2 8.9 %collective-permute-start.10 = (bf16[8,72,128]{2,1,0:T(8,128)(2,1)}, bf16[8,72,128]{2,1,0:T(8,128)(2,1)S(1)}, u32[]{:S(2)}, u32[]{:S(2)}) collective-permute-start(bf16[8,72,128]{2,1,0:T(8,128)(2,1)} %get-tuple-element.64), channel_id=1, source_target_pairs={{0,24},{8,0},{16,8},{24,16},{32,56},{40,32},{48,40},{56,48},{64,88... | collective-permute-start | bytes 442376 | tf_op jit(solution)/shard_map/ppermute | solution.py:22
  65.8 50.1 %collective-permute-start.13 = (bf16[8,1024,128]{2,1,0:T(8,128)(2,1)}, bf16[8,1024,128]{2,1,0:T(8,128)(2,1)S(1)}, u32[]{:S(2)}, u32[]{:S(2)}) collective-permute-start(bf16[8,1024,128]{2,1,0:T(8,128)(2,1)} %bitcast.32), channel_id=1, source_target_pairs={{0,24},{8,0},{16,8},{24,16},{32,56},{40,32},{48,40},{56,48},{64,88... | collective-permute-start | bytes 6291464 | tf_op jit(solution)/shard_map/ppermute | solution.py:22
  68.2 48.5 %collective-permute-start.12 = (bf16[8,1024,128]{2,1,0:T(8,128)(2,1)}, bf16[8,1024,128]{2,1,0:T(8,128)(2,1)}, u32[]{:S(2)}, u32[]{:S(2)}) collective-permute-start(bf16[8,1024,128]{2,1,0:T(8,128)(2,1)} %bitcast.33), channel_id=1, source_target_pairs={{0,8},{8,16},{16,24},{24,0},{32,40},{40,48},{48,56},{56,32},{64,72... | collective-permute-start | bytes 6291464 | tf_op jit(solution)/shard_map/ppermute | solution.py:22
  68.2 10.0 %collective-permute-start.15 = (bf16[768,512]{1,0:T(8,128)(2,1)S(1)}, bf16[768,512]{1,0:T(8,128)(2,1)}, u32[]{:S(2)}, u32[]{:S(2)}) collective-permute-start(bf16[768,512]{1,0:T(8,128)(2,1)S(1)} %copy-done.1), channel_id=1, source_target_pairs={{0,1},{1,0},{2,3},{3,2},{4,5},{5,4},{6,7},{7,6},{8,9},{9,8},{10,11... | collective-permute-start | bytes 2359304 | tf_op jit(solution)/shard_map/ppermute | solution.py:35
  68.2 12.4 %collective-permute-start.14 = (bf16[768,512]{1,0:T(8,128)(2,1)}, bf16[768,512]{1,0:T(8,128)(2,1)}, u32[]{:S(2)}, u32[]{:S(2)}) collective-permute-start(bf16[768,512]{1,0:T(8,128)(2,1)} %collective-permute-done.11.refs_2_), channel_id=1, source_target_pairs={{0,2},{1,7},{2,4},{3,1},{4,6},{5,3},{6,0},{7,5},{8,10},{9,15},{10,... | collective-permute-start | bytes 2359304 | tf_op jit(solution)/shard_map/ppermute | solution.py:27
  69.4 25.2 %all-to-all-start = ((f32[8,72,128]{2,1,0:T(8,128)}), f32[8,72,128]{2,1,0:T(8,128)S(1)}, u32[]{:S(2)}, u32[]{:S(2)}) async-start(f32[8,72,128]{2,1,0:T(8,128)} %convert_add_fusion), calls=%async_computation | async-start | bytes 589824 | tf_op jit(solution)/shard_map/all_to_all | solution.py:343
  77.8 20.9 %collective-permute-start.16 = (bf16[768,512]{1,0:T(8,128)(2,1)}, bf16[768,512]{1,0:T(8,128)(2,1)}, u32[]{:S(2)}, u32[]{:S(2)}) collective-permute-start(bf16[768,512]{1,0:T(8,128)(2,1)} %copy-done.5), channel_id=1, source_target_pairs={{0,1},{1,0},{2,3},{3,2},{4,5},{5,4},{6,7},{7,6},{8,9},{9,8},{10,11... | collective-permute-start | bytes 2359304 | tf_op jit(solution)/shard_map/ppermute | solution.py:35
  78.2 20.5 %collective-permute-start.17 = (bf16[768,512]{1,0:T(8,128)(2,1)}, bf16[768,512]{1,0:T(8,128)(2,1)S(1)}, u32[]{:S(2)}, u32[]{:S(2)}) collective-permute-start(bf16[768,512]{1,0:T(8,128)(2,1)} %collective-permute-done.11.refs_2_), channel_id=1, source_target_pairs={{0,1},{1,0},{2,3},{3,2},{4,5},{5,4},{6,7},{7,6},{8,9},{9,8},{10,11... | collective-permute-start | bytes 2359304 | tf_op jit(solution)/shard_map/ppermute | solution.py:35
  80.6 18.1 %collective-permute-start.18 = (bf16[768,512]{1,0:T(8,128)(2,1)}, bf16[768,512]{1,0:T(8,128)(2,1)}, u32[]{:S(2)}, u32[]{:S(2)}) collective-permute-start(bf16[768,512]{1,0:T(8,128)(2,1)} %collective-permute-done.14.refs_3_), channel_id=1, source_target_pairs={{0,1},{1,0},{2,3},{3,2},{4,5},{5,4},{6,7},{7,6},{8,9},{9,8},{10,11... | collective-permute-start | bytes 2359304 | tf_op jit(solution)/shard_map/ppermute | solution.py:35
  95.3 20.6 %all-to-all-start.1 = ((bf16[8,56,128]{2,1,0:T(8,128)(2,1)}), bf16[8,56,128]{2,1,0:T(8,128)(2,1)S(1)}, u32[]{:S(2)}, u32[]{:S(2)}) async-start(bf16[8,56,128]{2,1,0:T(8,128)(2,1)} %broadcast_in_dim.2), calls=%async_computation.1 | async-start | bytes 229376 | tf_op jit(solution)/shard_map/all_to_all | solution.py:347
  120.0 34.2 %collective-permute-start.20 = (bf16[4,1024,128]{2,1,0:T(8,128)(2,1)}, bf16[4,1024,128]{2,1,0:T(8,128)(2,1)S(1)}, u32[]{:S(2)}, u32[]{:S(2)}) collective-permute-start(bf16[4,1024,128]{2,1,0:T(8,128)(2,1)} %slice.23), channel_id=1, source_target_pairs={{0,24},{8,0},{16,8},{24,16},{32,56},{40,32},{48,40},{56,48},{64,88... | collective-permute-start | bytes 3145736 | tf_op jit(solution)/shard_map/ppermute | solution.py:22
  123.3 30.9 %collective-permute-start.19 = (bf16[4,1024,128]{2,1,0:T(8,128)(2,1)}, bf16[4,1024,128]{2,1,0:T(8,128)(2,1)}, u32[]{:S(2)}, u32[]{:S(2)}) collective-permute-start(bf16[4,1024,128]{2,1,0:T(8,128)(2,1)} %slice.22), channel_id=1, source_target_pairs={{0,8},{8,16},{16,24},{24,0},{32,40},{40,48},{48,56},{56,32},{64,72... | collective-permute-start | bytes 3145736 | tf_op jit(solution)/shard_map/ppermute | solution.py:22
  131.7 19.0 %collective-permute-start.23 = (bf16[8,56,128]{2,1,0:T(8,128)(2,1)S(1)}, bf16[8,56,128]{2,1,0:T(8,128)(2,1)S(1)}, u32[]{:S(2)}, u32[]{:S(2)}) collective-permute-start(bf16[8,56,128]{2,1,0:T(8,128)(2,1)S(1)} %all-to-all-done.1), channel_id=1, source_target_pairs={{0,24},{8,0},{16,8},{24,16},{32,56},{40,32},{48,40},{56,48},{64,88... | collective-permute-start | bytes 344072 | tf_op jit(solution)/shard_map/ppermute | solution.py:22
  134.9 16.5 %collective-permute-start.22 = (bf16[8,56,128]{2,1,0:T(8,128)(2,1)S(1)}, bf16[8,56,128]{2,1,0:T(8,128)(2,1)S(1)}, u32[]{:S(2)}, u32[]{:S(2)}) collective-permute-start(bf16[8,56,128]{2,1,0:T(8,128)(2,1)S(1)} %all-to-all-done.1), channel_id=1, source_target_pairs={{0,16},{8,24},{16,0},{24,8},{32,48},{40,56},{48,32},{56,40},{64,80... | collective-permute-start | bytes 344072 | tf_op jit(solution)/shard_map/ppermute | solution.py:22
  134.9 19.2 %collective-permute-start.21 = (bf16[8,56,128]{2,1,0:T(8,128)(2,1)S(1)}, bf16[8,56,128]{2,1,0:T(8,128)(2,1)S(1)}, u32[]{:S(2)}, u32[]{:S(2)}) collective-permute-start(bf16[8,56,128]{2,1,0:T(8,128)(2,1)S(1)} %all-to-all-done.1), channel_id=1, source_target_pairs={{0,8},{8,16},{16,24},{24,0},{32,40},{40,48},{48,56},{56,32},{64,72... | collective-permute-start | bytes 344072 | tf_op jit(solution)/shard_map/ppermute | solution.py:22
  154.2 9.5 %copy-start.4 = (bf16[4,1024,128]{2,1,0:T(8,128)(2,1)}, bf16[4,1024,128]{2,1,0:T(8,128)(2,1)S(1)}, u32[]{:S(2)}) copy-start(bf16[4,1024,128]{2,1,0:T(8,128)(2,1)S(1)} %collective-permute-done.20.high) | copy-start | bytes 3145732
  154.2 15.4 %collective-permute-start.24 = (f32[16,128]{1,0:T(8,128)S(1)}, f32[16,128]{1,0:T(8,128)S(1)}, u32[]{:S(2)}, u32[]{:S(2)}) collective-permute-start(f32[16,128]{1,0:T(8,128)S(1)} %slice.24), channel_id=1, source_target_pairs={{0,0},{1,32},{2,64},{3,96},{4,128},{5,160},{6,192},{7,224},{8,1},{... | collective-permute-start | bytes 24584 | tf_op jit(solution)/shard_map/ppermute | solution.py:365
  (7 other events, 43.4 us)
Sparse Core Ops, SparseCore 0:
  9.8 44.2 all-gather.4
  55.9 81.5 all-gather.6

commit v6 on v5

--- a/solution.py
+++ b/solution.py
@@ -355,12 +355,11 @@
     half = NZ // 2
     low, high = move_y(plus[:half], 1), move_y(minus[half:], -1)
     partial = project_sides(side_left, partial, plus, minus)
-    partial, down, total = together(partial, down, total)
+    hidden_input_gradient = project_last_rows(place, left, routed, adapter_down_weight, b_blocks)
+    hidden_input_gradient, low, high, partial, down, total = together(
+        hidden_input_gradient, low, high, partial, down, total
+    )
     came = [down] + [move_y(down, j) for j in range(1, NY)]
-    hidden_input_gradient = project_last_rows(place, left, routed, adapter_down_weight, b_blocks)
-    hidden_input_gradient, low, high, partial, total, *came = together(
-        hidden_input_gradient, low, high, partial, total, *came
-    )
     pairs = [(d * 8 + t, (4 * t + d // 8) * 8 + d % 8) for d in range(n) for t in range(8)]
     up_factor_gradient = lax.ppermute(total[down_rows:], ("dp", "tensor"), pairs).T
     hidden_input_gradient = project_late(late_left, partial, low, high, hidden_input_gradient)

time: 178 us -> 177 us (level)
    all_gather x1, waiting for transfers between devices: 0.01 us -> 5.7 us  [per_device(): b_blocks = lax.all_gather(column, 'dp', axis=0, axis_index_groups=Z_GROUPS)]
    ppermute x13, waiting for transfers between devices: 18.8 us -> 14 us  [move_y(): return lax.ppermute(value, 'dp', pairs)]
    unnamed x30 -> x32, local copies, waits for them, and re-layouts: 5.98 us -> 4.99 us
  transfers between devices with their start and end apart: 29 -> 29, of which waited for: 15 -> 14; matrix products, arithmetic and copies ran while one was open for 8% -> 7% of each run, Pallas kernels for 30% -> 30%
where the time goes in v6:
time: 177 us; the launch traced here: 176 us
  Pallas kernels  53.1 us (30%)
  waiting for transfers between devices  49.3 us (28%)
  starting transfers between devices  42.3 us (24%)
  between operations  14.3 us (8%)
  local copies, waits for them, and re-layouts  11.7 us (7%)
  other arithmetic  5.66 us (3%)
    ppermute x13, starting transfers between devices, move_y(): return lax.ppermute(value, 'dp', pairs)  18.1 us
    all_to_all x1, waiting for transfers between devices, per_device(): lax.all_to_all(parts, 'dp', 0, 0, tiled=True, axis_index_groups=Z_GROUPS)  14.1 us
    ppermute x13, waiting for transfers between devices, move_y(): return lax.ppermute(value, 'dp', pairs)  14 us
    ppermute x2, waiting for transfers between devices, swap_x(): lax.ppermute(value, 'tensor', [(x * 2 + c, partner(x) * 2 + c) for x in r...  10.9 us
    pallas_call x1, Pallas kernels, project_last_rows(): pl.pallas_call(last_rows_kernel, grid=(units // TILE - A_TILES,), out_sha...  10.7 us
    pallas_call x1, Pallas kernels, project_own(): pl.pallas_call(own_kernel, grid=(A_TILES,), out_shape=(jax.ShapeDtypeStru...  10.4 us
    all_to_all x1, starting transfers between devices, per_device(): lax.all_to_all(parts, 'dp', 0, 0, tiled=True, axis_index_groups=Z_GROUPS)  8.45 us
    pallas_call x1, Pallas kernels, project_sides(): pl.pallas_call(sides_kernel, grid=(A_TILES,), out_shape=jax.ShapeDtypeStr...  8.38 us
  transfers between devices with their start and end apart: 29, of which 14 were waited for; matrix products, arithmetic and copies ran while one was open for 7% of the time, Pallas kernels for 30%

profile of v6, /device:TPU:4, one launch (start us, length us, event | category | flops | bytes accessed | tf_op | source)
XLA Modules:
  0.0 176.4 jit_solution(7262093948516915633)
XLA Ops:
  7.2 1.7 slice.19
  10.5 4.3 %shard_map.102 = (f32[384,256]{1,0:T(8,128)}, f32[384,256]{1,0:T(8,128)}) custom-call(s32[4]{0:T(128)} %pad_add_fusion.place, bf16[768,1792]{1,0:T(8,128)(2,1)} %hidden.3, bf16[1792,128]{1,0:T(8,128)(2,1)} %factor.5, bf16[768,512]{1,0:T(8,128)(2,1)} %refs_0_.2, bf16[128,4096]{1,0:T(8,128)(2,1)} %up.1), custom_call_target="tpu_custom_call" | custom-call | tf_op jit(solution)/shard_map/pallas_call | solution.py:66
  14.9 1.9 %collective-permute-done.3 = f32[384,256]{1,0:T(8,128)S(1)} collective-permute-done((f32[384,256]{1,0:T(8,128)}, f32[384,256]{1,0:T(8,128)S(1)}, u32[]{:S(2)}, u32[]{:S(2)}) %collective-permute-start.3) | collective-permute-done | bytes 393248 | tf_op jit(solution)/shard_map/ppermute | solution.py:35
  17.9 1.3 collective-permute-start.4
  21.9 2.1 %shard_map.103 = (s32[768,2]{1,0:T(8,128)}, f32[768,2]{1,0:T(8,128)}) custom-call(s32[768,2]{1,0:T(8,128)} %copy.20.refs_0_, f32[768,2]{1,0:T(8,128)} %copy.21.refs_1_), custom_call_target="tpu_custom_call" | custom-call | tf_op jit(solution)/shard_map/pallas_call | solution.py:134
  23.9 5.9 %collective-permute-done.4 = f32[384,256]{1,0:T(8,128)S(1)} collective-permute-done((f32[384,256]{1,0:T(8,128)S(1)}, f32[384,256]{1,0:T(8,128)S(1)}, u32[]{:S(2)}, u32[]{:S(2)}) %collective-permute-start.4) | collective-permute-done | bytes 393248 | tf_op jit(solution)/shard_map/ppermute | solution.py:31
  30.4 2.8 %collective-permute-start.2 = (bf16[768,128]{1,0:T(8,128)(2,1)S(1)}, bf16[768,128]{1,0:T(8,128)(2,1)S(1)}, u32[]{:S(2)}, u32[]{:S(2)}) collective-permute-start(bf16[768,128]{1,0:T(8,128)(2,1)S(1)} %slice.20), channel_id=1, source_target_pairs={{0,24},{8,0},{16,8},{24,16},{32,56},{40,32},{48,40},{56,48},{64,88... | collective-permute-start | bytes 589832 | tf_op jit(solution)/shard_map/ppermute | solution.py:22
  34.7 4.9 %collective-permute-done.5 = f32[384,256]{1,0:T(8,128)S(1)} collective-permute-done((f32[384,256]{1,0:T(8,128)S(1)}, f32[384,256]{1,0:T(8,128)S(1)}, u32[]{:S(2)}, u32[]{:S(2)}) %collective-permute-start.5) | collective-permute-done | bytes 393248 | tf_op jit(solution)/shard_map/ppermute | solution.py:31
  40.5 1.6 collective-permute-done.1
  42.1 2.0 %collective-permute-done = bf16[768,128]{1,0:T(8,128)(2,1)S(1)} collective-permute-done((bf16[768,128]{1,0:T(8,128)(2,1)S(1)}, bf16[768,128]{1,0:T(8,128)(2,1)S(1)}, u32[]{:S(2)}, u32[]{:S(2)}) %collective-permute-start) | collective-permute-done | bytes 196640 | tf_op jit(solution)/shard_map/ppermute | solution.py:22
  45.5 1.2 collective-permute-start.11
  47.9 5.2 %shard_map.104 = (bf16[8,72,128]{2,1,0:T(8,128)(2,1)}, bf16[8,72,128]{2,1,0:T(8,128)(2,1)}, bf16[8,72,128]{2,1,0:T(8,128)(2,1)}, bf16[8,72,128]{2,1,0:T(8,128)(2...) custom-call(s32[4]{0:T(128)} %pad_add_fusion.place, f32[384,256]{1,0:T(8,128)} %copy-done.3, f32[384,256]{1,0:T(8,128)} %copy-done.8, ...), custom_call_target="tpu_custom_call" | custom-call | tf_op jit(solution)/shard_map/pallas_call | solution.py:115
  53.1 2.1 %collective-permute-start.9 = (bf16[8,72,128]{2,1,0:T(8,128)(2,1)}, bf16[8,72,128]{2,1,0:T(8,128)(2,1)S(1)}, u32[]{:S(2)}, u32[]{:S(2)}) collective-permute-start(bf16[8,72,128]{2,1,0:T(8,128)(2,1)} %get-tuple-element.57), channel_id=1, source_target_pairs={{0,16},{8,24},{16,0},{24,8},{32,48},{40,56},{48,32},{56,40},{64,80... | collective-permute-start | bytes 442376 | tf_op jit(solution)/shard_map/ppermute | solution.py:22
  56.4 7.1 %collective-permute-done.8 = bf16[8,72,128]{2,1,0:T(8,128)(2,1)S(1)} collective-permute-done((bf16[8,72,128]{2,1,0:T(8,128)(2,1)}, bf16[8,72,128]{2,1,0:T(8,128)(2,1)S(1)}, u32[]{:S(2)}, u32[]{:S(2)}) %collective-permute-start.8) | collective-permute-done | bytes 147488 | tf_op jit(solution)/shard_map/ppermute | solution.py:22
  64.2 1.7 convert_add_fusion
  65.9 2.3 %collective-permute-start.13 = (bf16[8,1024,128]{2,1,0:T(8,128)(2,1)}, bf16[8,1024,128]{2,1,0:T(8,128)(2,1)S(1)}, u32[]{:S(2)}, u32[]{:S(2)}) collective-permute-start(bf16[8,1024,128]{2,1,0:T(8,128)(2,1)} %bitcast.32), channel_id=1, source_target_pairs={{0,24},{8,0},{16,8},{24,16},{32,56},{40,32},{48,40},{56,48},{64,88... | collective-permute-start | bytes 6291464 | tf_op jit(solution)/shard_map/ppermute | solution.py:22
  68.2 1.2 collective-permute-start.14
  69.4 8.4 %all-to-all-start = ((f32[8,72,128]{2,1,0:T(8,128)}), f32[8,72,128]{2,1,0:T(8,128)S(1)}, u32[]{:S(2)}, u32[]{:S(2)}) async-start(f32[8,72,128]{2,1,0:T(8,128)} %convert_add_fusion), calls=%async_computation | async-start | bytes 589824 | tf_op jit(solution)/shard_map/all_to_all | solution.py:343
  78.4 2.2 %collective-permute-done.14.refs_3_ = bf16[768,512]{1,0:T(8,128)(2,1)} collective-permute-done((bf16[768,512]{1,0:T(8,128)(2,1)}, bf16[768,512]{1,0:T(8,128)(2,1)}, u32[]{:S(2)}, u32[]{:S(2)}) %collective-permute-start.14) | collective-permute-done | bytes 786464 | tf_op jit(solution)/shard_map/ppermute | solution.py:27
  80.6 14.1 %all-to-all-done = f32[8,72,128]{2,1,0:T(8,128)S(1)} async-done(((f32[8,72,128]{2,1,0:T(8,128)}), f32[8,72,128]{2,1,0:T(8,128)S(1)}, u32[]{:S(2)}, u32[]{:S(2)}) %all-to-all-start) | async-done | bytes 294944 | tf_op jit(solution)/shard_map/all_to_all | solution.py:343
  95.4 3.4 %all-to-all-start.1 = ((bf16[8,56,128]{2,1,0:T(8,128)(2,1)}), bf16[8,56,128]{2,1,0:T(8,128)(2,1)S(1)}, u32[]{:S(2)}, u32[]{:S(2)}) async-start(bf16[8,56,128]{2,1,0:T(8,128)(2,1)} %broadcast_in_dim.2), calls=%async_computation.1 | async-start | bytes 229376 | tf_op jit(solution)/shard_map/all_to_all | solution.py:347
  99.7 6.0 %shard_map.105.left = bf16[768,4096]{1,0:T(8,128)(2,1)} custom-call(s32[4]{0:T(128)} %pad_add_fusion.place, bf16[768,512]{1,0:T(8,128)(2,1)} %refs_0_.2, bf16[768,512]{1,0:T(8,128)(2,1)} %copy-done.5, bf16[768,512]{1,0:T(8,128)(2,1)} %collective-permute-done.11.refs_2_, bf16[768,512]{1,0:T(8,128)(2,1)} %collective-permute-done.14.refs_3_, ...), custom_call_target="tpu_custom_call" | custom-call | tf_op jit(solution)/shard_map/pallas_call | solution.py:158
  105.7 10.4 %shard_map.106 = (f32[768,1024]{1,0:T(8,128)}, bf16[768,2048]{1,0:T(8,128)(2,1)}, bf16[768,1024]{1,0:T(8,128)(2,1)}) custom-call(s32[4]{0:T(128)} %pad_add_fusion.place, bf16[768,4096]{1,0:T(8,128)(2,1)} %shard_map.105.left, bf16[768,128]{1,0:T(8,128)(2,1)} %get-tuple-element.62.routed, bf16[1792,128]{1,0:T(8,128)(2,1)} %factor.5, bf16[8,1024,128]{2,1,0:T(8,128)(2,1)} %bitcast.34), custom_call_target="tpu_custom_call" | custom-call | tf_op jit(solution)/shard_map/pallas_call | solution.py:226
  116.7 2.4 %slice.22 = bf16[4,1024,128]{2,1,0:T(8,128)(2,1)} slice(bf16[8,1024,128]{2,1,0:T(8,128)(2,1)} %collective-permute-done.12.plus), slice={[0:4], [0:1024], [0:128]} | slice | bytes 2097152 | tf_op jit(solution)/shard_map/slice | solution.py:356
  120.1 3.3 %collective-permute-start.20 = (bf16[4,1024,128]{2,1,0:T(8,128)(2,1)}, bf16[4,1024,128]{2,1,0:T(8,128)(2,1)S(1)}, u32[]{:S(2)}, u32[]{:S(2)}) collective-permute-start(bf16[4,1024,128]{2,1,0:T(8,128)(2,1)} %slice.23), channel_id=1, source_target_pairs={{0,24},{8,0},{16,8},{24,16},{32,56},{40,32},{48,40},{56,48},{64,88... | collective-permute-start | bytes 3145736 | tf_op jit(solution)/shard_map/ppermute | solution.py:22
  123.4 8.4 %shard_map.108.partial = f32[768,1024]{1,0:T(8,128)} custom-call(bf16[768,2048]{1,0:T(8,128)(2,1)} %get-tuple-element.73.picked, f32[768,1024]{1,0:T(8,128)} %get-tuple-element.74.partial, bf16[8,1024,128]{2,1,0:T(8,128)(2,1)} %collective-permute-done.12.plus, bf16[8,1024,128]{2,1,0:T(8,128)(2,1)} %copy-done.2), custom_call_target="tpu_custom_call" | custom-call | tf_op jit(solution)/shard_map/pallas_call | solution.py:250
  131.8 5.7 %all-gather.7.cloned.1.call-done = bf16[32,768,128]{2,1,0:T(8,128)(2,1)} async-done(((bf16[4,768,128]{2,1,0:T(8,128)(2,1)}), bf16[32,768,128]{2,1,0:T(8,128)(2,1)}) %all-gather.7.cloned.1.call-update) | async-done | bytes 6291472 | tf_op jit(solution)/shard_map/all_gather | solution.py:331
  137.5 10.7 %shard_map.107.base = bf16[768,1792]{1,0:T(8,128)(2,1)} custom-call(s32[4]{0:T(128)} %pad_add_fusion.place, bf16[768,4096]{1,0:T(8,128)(2,1)} %shard_map.105.left, bf16[768,128]{1,0:T(8,128)(2,1)} %get-tuple-element.62.routed, bf16[1792,128]{1,0:T(8,128)(2,1)} %factor.5, bf16[8,4,768,128]{3,2,1,0:T(8,128)(2,1)} %bitcast.31), custom_call_target="tpu_custom_call" | custom-call | tf_op jit(solution)/shard_map/pallas_call | solution.py:265
  149.4 1.6 collective-permute-start.21
  151.1 6.8 %collective-permute-start.24 = (f32[16,128]{1,0:T(8,128)S(1)}, f32[16,128]{1,0:T(8,128)S(1)}, u32[]{:S(2)}, u32[]{:S(2)}) collective-permute-start(f32[16,128]{1,0:T(8,128)S(1)} %slice.24), channel_id=1, source_target_pairs={{0,0},{1,32},{2,64},{3,96},{4,128},{5,160},{6,192},{7,224},{8,1},{... | collective-permute-start | bytes 24584 | tf_op jit(solution)/shard_map/ppermute | solution.py:364
  158.6 3.2 %collective-permute-start.22 = (bf16[8,56,128]{2,1,0:T(8,128)(2,1)S(1)}, bf16[8,56,128]{2,1,0:T(8,128)(2,1)S(1)}, u32[]{:S(2)}, u32[]{:S(2)}) collective-permute-start(bf16[8,56,128]{2,1,0:T(8,128)(2,1)S(1)} %all-to-all-done.1), channel_id=1, source_target_pairs={{0,16},{8,24},{16,0},{24,8},{32,48},{40,56},{48,32},{56,40},{64,80... | collective-permute-start | bytes 344072 | tf_op jit(solution)/shard_map/ppermute | solution.py:22
  161.8 6.0 %shard_map.109 = bf16[768,1792]{1,0:T(8,128)(2,1)} custom-call(bf16[768,1024]{1,0:T(8,128)(2,1)} %get-tuple-element.67.picked, f32[768,1024]{1,0:T(8,128)} %shard_map.108.partial, bf16[4,1024,128]{2,1,0:T(8,128)(2,1)} %collective-permute-done.19.low, bf16[4,1024,128]{2,1,0:T(8,128)(2,1)} %copy-done.4, ...), custom_call_target="tpu_custom_call", output_to_operand_aliasing={{}: (4, {})} | custom-call | tf_op jit(solution)/shard_map/pallas_call | solution.py:283
  (85 shorter events, 20.1 us)
Async XLA Ops:
  7.2 58.7 %all-gather.5.cloned.1.call-start = ((), (), s32[]{:S(2)}) async-start(), calls=%async_computation.2 | async-start | bytes 2359296 | tf_op jit(solution)/shard_map/all_gather | solution.py:317
  8.9 128.6 %all-gather.7.cloned.1.call-start = ((), (), s32[]{:S(2)}) async-start(), calls=%async_computation.3 | async-start | bytes 7077888 | tf_op jit(solution)/shard_map/all_gather | solution.py:331
  14.9 1.9 %collective-permute-start.3 = (f32[384,256]{1,0:T(8,128)}, f32[384,256]{1,0:T(8,128)S(1)}, u32[]{:S(2)}, u32[]{:S(2)}) collective-permute-start(f32[384,256]{1,0:T(8,128)} %get-tuple-element.48), channel_id=1, source_target_pairs={{0,1},{1,0},{2,3},{3,2},{4,5},{5,4},{6,7},{7,6},{8,9},{9,8},{10,11... | collective-permute-start | bytes 1179656 | tf_op jit(solution)/shard_map/ppermute | solution.py:35
  17.9 12.0 %collective-permute-start.4 = (f32[384,256]{1,0:T(8,128)S(1)}, f32[384,256]{1,0:T(8,128)S(1)}, u32[]{:S(2)}, u32[]{:S(2)}) collective-permute-start(f32[384,256]{1,0:T(8,128)S(1)} %add.22), channel_id=1, source_target_pairs={{0,2},{1,3},{2,0},{3,1},{4,6},{5,7},{6,4},{7,5},{8,10},{9,11},{10,... | collective-permute-start | bytes 1179656 | tf_op jit(solution)/shard_map/ppermute | solution.py:31
  19.1 25.0 %collective-permute-start.6 = (bf16[768,512]{1,0:T(8,128)(2,1)S(1)}, bf16[768,512]{1,0:T(8,128)(2,1)S(1)}, u32[]{:S(2)}, u32[]{:S(2)}) collective-permute-start(bf16[768,512]{1,0:T(8,128)(2,1)S(1)} %copy-done), channel_id=1, source_target_pairs={{0,2},{1,7},{2,4},{3,1},{4,6},{5,3},{6,0},{7,5},{8,10},{9,15},{10,... | collective-permute-start | bytes 2359304 | tf_op jit(solution)/shard_map/ppermute | solution.py:27
  29.9 9.7 %collective-permute-start.5 = (f32[384,256]{1,0:T(8,128)S(1)}, f32[384,256]{1,0:T(8,128)S(1)}, u32[]{:S(2)}, u32[]{:S(2)}) collective-permute-start(f32[384,256]{1,0:T(8,128)S(1)} %add.23), channel_id=1, source_target_pairs={{0,6},{1,7},{2,4},{3,5},{4,2},{5,3},{6,0},{7,1},{8,14},{9,15},{10,... | collective-permute-start | bytes 1179656 | tf_op jit(solution)/shard_map/ppermute | solution.py:31
  30.4 10.1 %collective-permute-start.2 = (bf16[768,128]{1,0:T(8,128)(2,1)S(1)}, bf16[768,128]{1,0:T(8,128)(2,1)S(1)}, u32[]{:S(2)}, u32[]{:S(2)}) collective-permute-start(bf16[768,128]{1,0:T(8,128)(2,1)S(1)} %slice.20), channel_id=1, source_target_pairs={{0,24},{8,0},{16,8},{24,16},{32,56},{40,32},{48,40},{56,48},{64,88... | collective-permute-start | bytes 589832 | tf_op jit(solution)/shard_map/ppermute | solution.py:22
  33.1 9.0 %collective-permute-start.1 = (bf16[768,128]{1,0:T(8,128)(2,1)S(1)}, bf16[768,128]{1,0:T(8,128)(2,1)S(1)}, u32[]{:S(2)}, u32[]{:S(2)}) collective-permute-start(bf16[768,128]{1,0:T(8,128)(2,1)S(1)} %slice.20), channel_id=1, source_target_pairs={{0,16},{8,24},{16,0},{24,8},{32,48},{40,56},{48,32},{56,40},{64,80... | collective-permute-start | bytes 589832 | tf_op jit(solution)/shard_map/ppermute | solution.py:22
  33.8 10.4 %collective-permute-start = (bf16[768,128]{1,0:T(8,128)(2,1)S(1)}, bf16[768,128]{1,0:T(8,128)(2,1)S(1)}, u32[]{:S(2)}, u32[]{:S(2)}) collective-permute-start(bf16[768,128]{1,0:T(8,128)(2,1)S(1)} %slice.20), channel_id=1, source_target_pairs={{0,8},{8,16},{16,24},{24,0},{32,40},{40,48},{48,56},{56,32},{64,72... | collective-permute-start | bytes 589832 | tf_op jit(solution)/shard_map/ppermute | solution.py:22
  45.3 22.9 %copy-start.1 = (bf16[768,512]{1,0:T(8,128)(2,1)S(1)}, bf16[768,512]{1,0:T(8,128)(2,1)}, u32[]{:S(2)}) copy-start(bf16[768,512]{1,0:T(8,128)(2,1)} %refs_0_.2) | copy-start | bytes 2359300
  45.4 1.8 %collective-permute-start.7 = (f32[384,256]{1,0:T(8,128)S(1)}, f32[384,256]{1,0:T(8,128)S(1)}, u32[]{:S(2)}, u32[]{:S(2)}) collective-permute-start(f32[384,256]{1,0:T(8,128)S(1)} %add.24.kept), channel_id=1, source_target_pairs={{0,1},{1,0},{2,3},{3,2},{4,5},{5,4},{6,7},{7,6},{8,9},{9,8},{10,11... | collective-permute-start | bytes 1179656 | tf_op jit(solution)/shard_map/ppermute | solution.py:35
  45.5 20.4 %collective-permute-start.11 = (bf16[768,512]{1,0:T(8,128)(2,1)S(1)}, bf16[768,512]{1,0:T(8,128)(2,1)}, u32[]{:S(2)}, u32[]{:S(2)}) collective-permute-start(bf16[768,512]{1,0:T(8,128)(2,1)S(1)} %collective-permute-done.6.refs_1_), channel_id=1, source_target_pairs={{0,2},{1,7},{2,4},{3,1},{4,6},{5,3},{6,0},{7,5},{8,10},{9,15},{10,... | collective-permute-start | bytes 2359304 | tf_op jit(solution)/shard_map/ppermute | solution.py:27
  53.1 10.4 %collective-permute-start.8 = (bf16[8,72,128]{2,1,0:T(8,128)(2,1)}, bf16[8,72,128]{2,1,0:T(8,128)(2,1)S(1)}, u32[]{:S(2)}, u32[]{:S(2)}) collective-permute-start(bf16[8,72,128]{2,1,0:T(8,128)(2,1)} %get-tuple-element.56), channel_id=1, source_target_pairs={{0,8},{8,16},{16,24},{24,0},{32,40},{40,48},{48,56},{56,32},{64,72... | collective-permute-start | bytes 442376 | tf_op jit(solution)/shard_map/ppermute | solution.py:22
  53.1 10.4 %collective-permute-start.9 = (bf16[8,72,128]{2,1,0:T(8,128)(2,1)}, bf16[8,72,128]{2,1,0:T(8,128)(2,1)S(1)}, u32[]{:S(2)}, u32[]{:S(2)}) collective-permute-start(bf16[8,72,128]{2,1,0:T(8,128)(2,1)} %get-tuple-element.57), channel_id=1, source_target_pairs={{0,16},{8,24},{16,0},{24,8},{32,48},{40,56},{48,32},{56,40},{64,80... | collective-permute-start | bytes 442376 | tf_op jit(solution)/shard_map/ppermute | solution.py:22
  55.2 8.9 %collective-permute-start.10 = (bf16[8,72,128]{2,1,0:T(8,128)(2,1)}, bf16[8,72,128]{2,1,0:T(8,128)(2,1)S(1)}, u32[]{:S(2)}, u32[]{:S(2)}) collective-permute-start(bf16[8,72,128]{2,1,0:T(8,128)(2,1)} %get-tuple-element.58), channel_id=1, source_target_pairs={{0,24},{8,0},{16,8},{24,16},{32,56},{40,32},{48,40},{56,48},{64,88... | collective-permute-start | bytes 442376 | tf_op jit(solution)/shard_map/ppermute | solution.py:22
  65.9 50.2 %collective-permute-start.13 = (bf16[8,1024,128]{2,1,0:T(8,128)(2,1)}, bf16[8,1024,128]{2,1,0:T(8,128)(2,1)S(1)}, u32[]{:S(2)}, u32[]{:S(2)}) collective-permute-start(bf16[8,1024,128]{2,1,0:T(8,128)(2,1)} %bitcast.32), channel_id=1, source_target_pairs={{0,24},{8,0},{16,8},{24,16},{32,56},{40,32},{48,40},{56,48},{64,88... | collective-permute-start | bytes 6291464 | tf_op jit(solution)/shard_map/ppermute | solution.py:22
  68.2 48.5 %collective-permute-start.12 = (bf16[8,1024,128]{2,1,0:T(8,128)(2,1)}, bf16[8,1024,128]{2,1,0:T(8,128)(2,1)}, u32[]{:S(2)}, u32[]{:S(2)}) collective-permute-start(bf16[8,1024,128]{2,1,0:T(8,128)(2,1)} %bitcast.33), channel_id=1, source_target_pairs={{0,8},{8,16},{16,24},{24,0},{32,40},{40,48},{48,56},{56,32},{64,72... | collective-permute-start | bytes 6291464 | tf_op jit(solution)/shard_map/ppermute | solution.py:22
  68.2 10.0 %collective-permute-start.15 = (bf16[768,512]{1,0:T(8,128)(2,1)S(1)}, bf16[768,512]{1,0:T(8,128)(2,1)}, u32[]{:S(2)}, u32[]{:S(2)}) collective-permute-start(bf16[768,512]{1,0:T(8,128)(2,1)S(1)} %copy-done.1), channel_id=1, source_target_pairs={{0,1},{1,0},{2,3},{3,2},{4,5},{5,4},{6,7},{7,6},{8,9},{9,8},{10,11... | collective-permute-start | bytes 2359304 | tf_op jit(solution)/shard_map/ppermute | solution.py:35
  68.2 12.4 %collective-permute-start.14 = (bf16[768,512]{1,0:T(8,128)(2,1)}, bf16[768,512]{1,0:T(8,128)(2,1)}, u32[]{:S(2)}, u32[]{:S(2)}) collective-permute-start(bf16[768,512]{1,0:T(8,128)(2,1)} %collective-permute-done.11.refs_2_), channel_id=1, source_target_pairs={{0,2},{1,7},{2,4},{3,1},{4,6},{5,3},{6,0},{7,5},{8,10},{9,15},{10,... | collective-permute-start | bytes 2359304 | tf_op jit(solution)/shard_map/ppermute | solution.py:27
  69.4 25.2 %all-to-all-start = ((f32[8,72,128]{2,1,0:T(8,128)}), f32[8,72,128]{2,1,0:T(8,128)S(1)}, u32[]{:S(2)}, u32[]{:S(2)}) async-start(f32[8,72,128]{2,1,0:T(8,128)} %convert_add_fusion), calls=%async_computation | async-start | bytes 589824 | tf_op jit(solution)/shard_map/all_to_all | solution.py:343
  77.9 20.9 %collective-permute-start.16 = (bf16[768,512]{1,0:T(8,128)(2,1)}, bf16[768,512]{1,0:T(8,128)(2,1)}, u32[]{:S(2)}, u32[]{:S(2)}) collective-permute-start(bf16[768,512]{1,0:T(8,128)(2,1)} %copy-done.5), channel_id=1, source_target_pairs={{0,1},{1,0},{2,3},{3,2},{4,5},{5,4},{6,7},{7,6},{8,9},{9,8},{10,11... | collective-permute-start | bytes 2359304 | tf_op jit(solution)/shard_map/ppermute | solution.py:35
  78.3 20.5 %collective-permute-start.17 = (bf16[768,512]{1,0:T(8,128)(2,1)}, bf16[768,512]{1,0:T(8,128)(2,1)S(1)}, u32[]{:S(2)}, u32[]{:S(2)}) collective-permute-start(bf16[768,512]{1,0:T(8,128)(2,1)} %collective-permute-done.11.refs_2_), channel_id=1, source_target_pairs={{0,1},{1,0},{2,3},{3,2},{4,5},{5,4},{6,7},{7,6},{8,9},{9,8},{10,11... | collective-permute-start | bytes 2359304 | tf_op jit(solution)/shard_map/ppermute | solution.py:35
  80.6 18.2 %collective-permute-start.18 = (bf16[768,512]{1,0:T(8,128)(2,1)}, bf16[768,512]{1,0:T(8,128)(2,1)}, u32[]{:S(2)}, u32[]{:S(2)}) collective-permute-start(bf16[768,512]{1,0:T(8,128)(2,1)} %collective-permute-done.14.refs_3_), channel_id=1, source_target_pairs={{0,1},{1,0},{2,3},{3,2},{4,5},{5,4},{6,7},{7,6},{8,9},{9,8},{10,11... | collective-permute-start | bytes 2359304 | tf_op jit(solution)/shard_map/ppermute | solution.py:35
  95.4 20.6 %all-to-all-start.1 = ((bf16[8,56,128]{2,1,0:T(8,128)(2,1)}), bf16[8,56,128]{2,1,0:T(8,128)(2,1)S(1)}, u32[]{:S(2)}, u32[]{:S(2)}) async-start(bf16[8,56,128]{2,1,0:T(8,128)(2,1)} %broadcast_in_dim.2), calls=%async_computation.1 | async-start | bytes 229376 | tf_op jit(solution)/shard_map/all_to_all | solution.py:347
  120.1 28.1 %collective-permute-start.20 = (bf16[4,1024,128]{2,1,0:T(8,128)(2,1)}, bf16[4,1024,128]{2,1,0:T(8,128)(2,1)S(1)}, u32[]{:S(2)}, u32[]{:S(2)}) collective-permute-start(bf16[4,1024,128]{2,1,0:T(8,128)(2,1)} %slice.23), channel_id=1, source_target_pairs={{0,24},{8,0},{16,8},{24,16},{32,56},{40,32},{48,40},{56,48},{64,88... | collective-permute-start | bytes 3145736 | tf_op jit(solution)/shard_map/ppermute | solution.py:22
  123.4 26.0 %collective-permute-start.19 = (bf16[4,1024,128]{2,1,0:T(8,128)(2,1)}, bf16[4,1024,128]{2,1,0:T(8,128)(2,1)}, u32[]{:S(2)}, u32[]{:S(2)}) collective-permute-start(bf16[4,1024,128]{2,1,0:T(8,128)(2,1)} %slice.22), channel_id=1, source_target_pairs={{0,8},{8,16},{16,24},{24,0},{32,40},{40,48},{48,56},{56,32},{64,72... | collective-permute-start | bytes 3145736 | tf_op jit(solution)/shard_map/ppermute | solution.py:22
  137.5 20.4 %copy-start.7 = (f32[768,2]{1,0:T(8,128)S(1)}, f32[768,2]{1,0:T(8,128)}, u32[]{:S(2)}) copy-start(f32[768,2]{1,0:T(8,128)} %get-tuple-element.91) | copy-start | bytes 18436
  148.2 13.5 %copy-start.4 = (bf16[4,1024,128]{2,1,0:T(8,128)(2,1)}, bf16[4,1024,128]{2,1,0:T(8,128)(2,1)S(1)}, u32[]{:S(2)}) copy-start(bf16[4,1024,128]{2,1,0:T(8,128)(2,1)S(1)} %collective-permute-done.20.high) | copy-start | bytes 3145732
  149.4 18.3 %collective-permute-start.21 = (bf16[8,56,128]{2,1,0:T(8,128)(2,1)S(1)}, bf16[8,56,128]{2,1,0:T(8,128)(2,1)S(1)}, u32[]{:S(2)}, u32[]{:S(2)}) collective-permute-start(bf16[8,56,128]{2,1,0:T(8,128)(2,1)S(1)} %all-to-all-done.1), channel_id=1, source_target_pairs={{0,24},{8,0},{16,8},{24,16},{32,56},{40,32},{48,40},{56,48},{64,88... | collective-permute-start | bytes 344072 | tf_op jit(solution)/shard_map/ppermute | solution.py:22
  151.1 16.7 %collective-permute-start.24 = (f32[16,128]{1,0:T(8,128)S(1)}, f32[16,128]{1,0:T(8,128)S(1)}, u32[]{:S(2)}, u32[]{:S(2)}) collective-permute-start(f32[16,128]{1,0:T(8,128)S(1)} %slice.24), channel_id=1, source_target_pairs={{0,0},{1,32},{2,64},{3,96},{4,128},{5,160},{6,192},{7,224},{8,1},{... | collective-permute-start | bytes 24584 | tf_op jit(solution)/shard_map/ppermute | solution.py:364
  158.6 9.2 %collective-permute-start.23 = (bf16[8,56,128]{2,1,0:T(8,128)(2,1)S(1)}, bf16[8,56,128]{2,1,0:T(8,128)(2,1)S(1)}, u32[]{:S(2)}, u32[]{:S(2)}) collective-permute-start(bf16[8,56,128]{2,1,0:T(8,128)(2,1)S(1)} %all-to-all-done.1), channel_id=1, source_target_pairs={{0,8},{8,16},{16,24},{24,0},{32,40},{40,48},{48,56},{56,32},{64,72... | collective-permute-start | bytes 344072 | tf_op jit(solution)/shard_map/ppermute | solution.py:22
  158.6 9.2 %collective-permute-start.22 = (bf16[8,56,128]{2,1,0:T(8,128)(2,1)S(1)}, bf16[8,56,128]{2,1,0:T(8,128)(2,1)S(1)}, u32[]{:S(2)}, u32[]{:S(2)}) collective-permute-start(bf16[8,56,128]{2,1,0:T(8,128)(2,1)S(1)} %all-to-all-done.1), channel_id=1, source_target_pairs={{0,16},{8,24},{16,0},{24,8},{32,48},{40,56},{48,32},{56,40},{64,80... | collective-permute-start | bytes 344072 | tf_op jit(solution)/shard_map/ppermute | solution.py:22
  (8 other events, 53.8 us)
Sparse Core Ops, SparseCore 0:
  9.8 44.2 all-gather.4
  55.9 81.5 all-gather.6
